TPU v7x, 128 devices: a whole 4x4x4 slice. The times are simulated.
128 devices in a mesh: dp: 4 (over z_lo, core), context: 16 (over y, x), tensor: 2 (over z_hi).
Axes of the slice: x: 4, y: 4, z: 4 (z_hi: 2, z_lo: 2; z = z_hi * 2 + z_lo), core: 2. Of those that a mesh axis runs over, the one named last changes fastest.
Arguments:
- queries: bfloat16 [24576, 2048], P(('dp', 'context'), 'tensor'), parts along dimension 0, may hold values from -256 to 256
- keys: bfloat16 [24576, 2048], P(('dp', 'context'), 'tensor'), parts along dimension 0, may hold values from -256 to 256
- values: bfloat16 [24576, 2048], P(('dp', 'context'), 'tensor'), parts along dimension 0, may hold values from -6 to 6
- out_weight: bfloat16 [2048, 4096], P('tensor'), may hold values from -0.125 to 0.125
- doc_lengths: int32 [24], P('dp'), parts along dimension 0, may hold values from 1 to 1536, 6144 in all
- spans: int32 [124, 2], P('dp'), parts along dimension 0, may hold values from 0 to 6144, as said below
- assignment: int32 [192], P('dp'), parts along dimension 0, may hold values from 0 to 47, each once
Outputs:
- mixed: bfloat16 [24576, 4096], P(('dp', 'context', 'tensor')), parts along dimension 0
There are 4 independent parts, one for each index of `dp`. A program takes and returns all parts, laid end to end along the dimension named above; an argument that names none is the same for every part. Nothing has to cross between parts.
Inputs may be any that keep to these rules, and one draw needn't show every extreme that they name: `doc_lengths`: they sum to 6144. Each row is a span [start, end) with start < end; spans are disjoint and in increasing order; each holds at most 198 positions, and one holds exactly that many. `assignment`: a permutation of the query blocks.
All inputs are finite; a program needn't handle non-finite values.
Results may differ from a plain program's by a relative error of at most 0.013.
Values may be sent and summed in bfloat16 or wider, within the bound.
No kernel may reach another device: no remote copies, remote signals or barrier semaphores. Data moves between devices by JAX's collectives and lax.ppermute only.
A program may use at most 128 MiB of HBM per device.

v0:
```python
import math

import jax
import jax.numpy as jnp
from jax import lax
from jax.sharding import PartitionSpec as P

HD = 128
QB = 128


def document_index(positions, doc_lengths):
    bounds = jnp.cumsum(doc_lengths)[:-1]
    return jnp.sum((positions[:, None] >= bounds[None, :]).astype(jnp.int32), axis=1)


def span_index(positions, spans):
    inside = (positions[:, None] >= spans[None, :, 0]) & (positions[:, None] < spans[None, :, 1])
    labels = jnp.arange(1, spans.shape[0] + 1, dtype=jnp.int32)
    return jnp.sum(jnp.where(inside, labels[None, :], 0), axis=1) - 1


def visible(query_pos, key_pos, doc_lengths, spans, seq_total):
    query_doc = document_index(query_pos, doc_lengths)
    key_doc = document_index(key_pos, doc_lengths)
    query_span = span_index(query_pos, spans)
    key_span = span_index(key_pos, spans)
    same_doc = query_doc[:, None] == key_doc[None, :]
    earlier = key_pos[None, :] <= query_pos[:, None]
    same_span = (query_span[:, None] == key_span[None, :]) & (query_span[:, None] >= 0)
    in_range = (key_pos >= 0) & (key_pos < seq_total)
    return same_doc & (earlier | same_span) & in_range[None, :]


def attend(carried, query_rows, query_pos, key_rows, value_rows, doc_lengths, spans, seq_total):
    key_count = key_rows.shape[0]
    block_len = math.gcd(key_count, 768)
    head_count = query_rows.shape[1] // HD
    query_heads = query_rows.reshape(query_rows.shape[0], head_count, HD)
    scale = 1.0 / math.sqrt(HD)

    def advance(block_index, running):
        offset_rows = block_index * block_len
        block_keys = lax.dynamic_slice_in_dim(key_rows, offset_rows, block_len, 0).reshape(
            block_len, head_count, HD
        )
        block_values = lax.dynamic_slice_in_dim(value_rows, offset_rows, block_len, 0).reshape(
            block_len, head_count, HD
        )
        key_pos = offset_rows + jnp.arange(block_len, dtype=jnp.int32)
        allowed = visible(query_pos, key_pos, doc_lengths, spans, seq_total)
        highest, denominator, summed = running
        scores = (
            jnp.einsum("rhd,khd->hrk", query_heads, block_keys, preferred_element_type=jnp.float32)
            * scale
        )
        scores = jnp.where(allowed[None], scores, -1e30)
        new_highest = jnp.maximum(highest, jnp.max(scores, axis=2))
        factor = jnp.exp(highest - new_highest)
        weights = jnp.where(allowed[None], jnp.exp(scores - new_highest[:, :, None]), 0.0)
        denominator = denominator * factor + jnp.sum(weights, axis=2)
        summed = summed * factor[:, :, None] + jnp.einsum(
            "hrk,khd->hrd",
            weights.astype(jnp.bfloat16),
            block_values,
            preferred_element_type=jnp.float32,
        )
        return (new_highest, denominator, summed)

    return lax.fori_loop(0, key_count // block_len, advance, carried)


def shards(queries, keys, values, out_weight, doc_lengths, spans, assignment):
    row_count, features = queries.shape
    head_count = features // HD
    context_size = lax.axis_size("context")
    my_index = lax.axis_index("context")
    seq_total = row_count * context_size
    blocks_here = row_count // QB
    owned_blocks = lax.dynamic_slice_in_dim(assignment, my_index * blocks_here, blocks_here, 0)
    initial = (
        jnp.full((head_count, row_count), -1e30, jnp.float32),
        jnp.zeros((head_count, row_count), jnp.float32),
        jnp.zeros((head_count, row_count, HD), jnp.float32),
    )
    everyone = lax.all_gather(queries, "context", axis=0, tiled=True)
    assigned = everyone.reshape(-1, QB, features)[owned_blocks].reshape(row_count, features)
    query_pos = (owned_blocks[:, None] * QB + jnp.arange(QB, dtype=jnp.int32)[None, :]).reshape(
        row_count
    )
    running = attend(
        initial,
        assigned,
        query_pos,
        lax.all_gather(keys, "context", axis=0, tiled=True),
        lax.all_gather(values, "context", axis=0, tiled=True),
        doc_lengths,
        spans,
        seq_total,
    )
    highest, denominator, summed = running
    result = summed / denominator[:, :, None]
    attended = jnp.transpose(result, (1, 0, 2)).reshape(row_count, features).astype(jnp.bfloat16)
    return lax.psum_scatter(
        jnp.dot(attended, out_weight, preferred_element_type=jnp.float32).astype(jnp.bfloat16),
        "tensor",
        scatter_dimension=0,
        tiled=True,
    )


def solution(mesh):
    placed = (
        P(("dp", "context"), "tensor"),
        P(("dp", "context"), "tensor"),
        P(("dp", "context"), "tensor"),
        P("tensor", None),
        P("dp"),
        P("dp", None),
        P("dp"),
    )
    return jax.shard_map(
        shards,
        mesh=mesh,
        in_specs=placed,
        out_specs=P(("dp", "context", "tensor"), None),
        check_vma=False,
    )
```

profile of v0, /device:TPU:1, one launch (start us, length us, event | category | flops | bytes accessed | tf_op | source)
XLA Modules:
  0.0 463.1 jit_solution(11742648295321434710)
XLA Ops:
  7.3 2.3 copy.19
  9.7 2.3 copy.20
  12.4 90.2 %all-gather.6.cloned.1.call-done = bf16[6144,1024]{1,0:T(8,128)(2,1)} async-done(((bf16[384,1024]{1,0:T(8,128)(2,1)}), bf16[6144,1024]{1,0:T(8,128)(2,1)}) %all-gather.6.cloned.1.call-update) | async-done | bytes 12582928 | tf_op jit(solution)/shard_map/all_gather | solution.py:86
  102.6 5.2 %gather_fusion = bf16[3,128,1024]{2,1,0:T(8,128)(2,1)S(1)} fusion(bf16[48,128,1024]{2,1,0:T(8,128)(2,1)} %bitcast.63, s32[1024]{0:T(1024)S(1)} %pad_clamp_fusion), kind=kCustom, calls=%fused_computation | custom fusion | bytes 1572876 | tf_op jit(solution)/shard_map/gather | solution.py:87
  108.1 95.0 %all-gather.4.cloned.1.call-done = bf16[6144,1024]{0,1:T(8,128)(2,1)} async-done(((bf16[384,1024]{0,1:T(8,128)(2,1)}), bf16[6144,1024]{0,1:T(8,128)(2,1)}) %all-gather.4.cloned.1.call-update) | async-done | bytes 12582928 | tf_op jit(solution)/shard_map/all_gather | solution.py:95
  203.1 101.1 %all-gather.8.cloned.1.call-done = bf16[6144,1024]{0,1:T(8,128)(2,1)} async-done(((bf16[384,1024]{0,1:T(8,128)(2,1)}), bf16[6144,1024]{0,1:T(8,128)(2,1)}) %all-gather.8.cloned.1.call-update) | async-done | bytes 12582928 | tf_op jit(solution)/shard_map/all_gather | solution.py:96
  304.2 95.2 %while.21 = (s32[]{:T(128)}, f32[8,384]{1,0:T(8,128)S(1)}, f32[8,384]{1,0:T(8,128)S(1)}, f32[8,384,128]{2,1,0:T(8,128)S(1)}, s32[6,1]{0,1:T(1,128)S(1)}, /*index...) while((s32[]{:T(128)}, f32[8,384]{1,0:T(8,128)S(1)}, ...), condition=%wide.region_8.9_spmd.clone, body=%wide.region_1.8_spmd.clone.sunk | while | flops 1242089472 | bytes 43108736 | solution.py:70
  304.7 0.8 and_and_fusion.2
  305.5 2.1 constant_dynamic-slice_fusion.3
  307.6 2.1 fusion.32
  309.8 2.2 fusion.33
  312.1 4.0 fusion.35
  316.6 0.8 and_and_fusion.2
  317.4 2.1 constant_dynamic-slice_fusion.3
  319.5 2.1 fusion.32
  321.7 2.2 fusion.33
  324.0 4.0 fusion.35
  328.5 0.8 and_and_fusion.2
  329.3 2.1 constant_dynamic-slice_fusion.3
  331.4 2.1 fusion.32
  333.6 2.2 fusion.33
  335.9 4.0 fusion.35
  340.4 0.8 and_and_fusion.2
  341.2 2.1 constant_dynamic-slice_fusion.3
  343.3 2.1 fusion.32
  345.5 2.2 fusion.33
  347.7 4.0 fusion.35
  353.1 2.1 constant_dynamic-slice_fusion.3
  355.2 2.1 fusion.32
  357.3 2.2 fusion.33
  359.6 4.0 fusion.35
  364.1 0.8 and_and_fusion.2
  364.9 2.1 constant_dynamic-slice_fusion.3
  367.0 2.1 fusion.32
  369.2 2.2 fusion.33
  371.5 4.0 fusion.35
  376.0 0.8 and_and_fusion.2
  376.8 2.1 constant_dynamic-slice_fusion.3
  378.9 2.1 fusion.32
  381.1 2.2 fusion.33
  383.4 4.0 fusion.35
  387.9 0.8 and_and_fusion.2
  388.7 2.1 constant_dynamic-slice_fusion.3
  390.8 2.1 fusion.32
  393.0 2.2 fusion.33
  395.3 4.0 fusion.35
  400.0 8.5 %convolution_convert_fusion = bf16[384,4096]{1,0:T(8,128)(2,1)} fusion(bf16[384,1024]{0,1:T(8,128)(2,1)S(1)} %bitcast.62, bf16[1024,4096]{1,0:T(8,128)(2,1)} %param.12), kind=kOutput, calls=%fused_computation.35 | convolution fusion | flops 3222798336 | bytes 12320768 | tf_op jit(solution)/shard_map/dot_general | solution.py:105
  408.6 48.0 %reduce-scatter.2.cloned.1.call-done = bf16[192,4096]{1,0:T(8,128)(2,1)} async-done(((bf16[384,4096]{1,0:T(8,128)(2,1)}), bf16[192,4096]{1,0:T(8,128)(2,1)}) %reduce-scatter.2.cloned.1.call-update) | async-done | bytes 1572880 | tf_op jit(solution)/shard_map/reduce_scatter | solution.py:104
  (153 shorter events, 6.8 us)
Async XLA Ops:
  6.5 5.6 %copy-start.2 = (s32[6]{0:T(128)S(1)}, s32[6]{0:T(128)}, u32[]{:S(2)}) copy-start(s32[6]{0:T(128)} %param.13) | copy-start | bytes 76
  6.5 5.8 %copy-start.1 = (s32[48]{0:T(128)S(1)}, s32[48]{0:T(128)}, u32[]{:S(2)}) copy-start(s32[48]{0:T(128)} %param.15) | copy-start | bytes 580
  6.5 96.1 %all-gather.6.cloned.1.call-start = ((), (), s32[]{:S(2)}) async-start(), calls=%async_computation.2 | async-start | bytes 13369344 | tf_op jit(solution)/shard_map/all_gather | solution.py:86
  7.3 297.0 %copy-start = (s32[31,2]{0,1:T(2,128)S(1)}, s32[31,2]{0,1:T(2,128)}, u32[]{:S(2)}) copy-start(s32[31,2]{0,1:T(2,128)} %param.14) | copy-start | bytes 748
  7.3 195.9 %all-gather.4.cloned.1.call-start = ((), (), s32[]{:S(2)}) async-start(), calls=%async_computation.1 | async-start | bytes 13369344 | tf_op jit(solution)/shard_map/all_gather | solution.py:95
  9.6 294.6 %all-gather.8.cloned.1.call-start = ((), (), s32[]{:S(2)}) async-start(), calls=%async_computation.3 | async-start | bytes 13369344 | tf_op jit(solution)/shard_map/all_gather | solution.py:96
  12.0 444.6 %reduce-scatter.2.cloned.1.call-start = ((), (), s32[]{:S(2)}) async-start(), calls=%async_computation.4 | async-start | bytes 4718592 | tf_op jit(solution)/shard_map/reduce_scatter | solution.py:104
Sparse Core Ops, SparseCore 0:
  9.5 93.0 all-gather.5
  104.7 98.3 all-gather.3
  205.2 98.9 all-gather.7
  408.7 47.8 reduce-scatter.1
where the time goes:
time: 463 us
  waiting for transfers between devices  335 us (72%)
  matrix products  57.3 us (12%)
  other arithmetic  28.7 us (6%)
  local copies, waits for them, and re-layouts  27.4 us (6%)
  between operations  13.2 us (3%)
    all_gather x1, waiting for transfers between devices, shards(): lax.all_gather(values, 'context', axis=0, tiled=True)  101 us
    all_gather x1, waiting for transfers between devices, shards(): lax.all_gather(keys, 'context', axis=0, tiled=True)  95 us
    all_gather x1, waiting for transfers between devices, shards(): everyone = lax.all_gather(queries, 'context', axis=0, tiled=True)  90.2 us
    reduce_scatter x1, waiting for transfers between devices, shards(): lax.psum_scatter(jnp.dot(attended, out_weight, preferred_element_type=jnp...  48 us
    dot_general x8, matrix products, advance(): jnp.einsum('hrk,khd->hrd', weights.astype(jnp.bfloat16), block_values, pr...  31.6 us
    reduce_sum x8, other arithmetic, advance(): denominator = denominator * factor + jnp.sum(weights, axis=2)  18 us
    dot_general x8, matrix products, advance(): jnp.einsum('rhd,khd->hrk', query_heads, block_keys, preferred_element_typ...  17.2 us
    dynamic_slice x8, local copies, waits for them, and re-layouts, advance(): lax.dynamic_slice_in_dim(key_rows, offset_rows, block_len, 0)  16.8 us
  transfers between devices with their start and end apart: 4, of which 4 were waited for; matrix products, arithmetic and copies ran while one was open for 2% of the time, Pallas kernels for 0%

commit v1 on v0

v1 whole, which is shorter than its diff:
```python
import functools
import math

import jax
import jax.numpy as jnp
from jax import lax
from jax.experimental import pallas as pl
from jax.experimental.pallas import tpu as pltpu
from jax.sharding import Mesh, PartitionSpec as P

HD = 128
QB = 128
QTR = QB // 4
HALF = QB // 2
NCTX = 16
CHIP_BLOCKS = 3
NBLK = NCTX * CHIP_BLOCKS
HEADS = 8
ROWS = NBLK * HALF
NDOC = 6
NSPAN = 31
TILE = 4
TROWS = TILE * HALF
TPOS = TILE * QB
NTILE = NBLK // TILE
SCALE2 = math.log2(math.e) / math.sqrt(HD)
NEG = -1e30
BF = jnp.bfloat16
F32 = jnp.float32


def pack_kernel(core_ref, q_ref, k_ref, v_ref, own_ref, send_ref):
    core = core_ref[0]
    for out_ref, parity in ((own_ref, core), (send_ref, 1 - core)):
        for a, ref in enumerate((q_ref, k_ref, v_ref)):
            for group in range(2 * CHIP_BLOCKS):
                start = pl.multiple_of(group * HALF + parity * QTR, QTR)
                rows = ref[pl.ds(start, QTR), :]
                for h in range(HEADS):
                    out_ref[h, group * QTR : (group + 1) * QTR, a * HD : (a + 1) * HD] = rows[
                        :, h * HD : (h + 1) * HD
                    ]


def pack(core, q, k, v):
    out = jax.ShapeDtypeStruct((HEADS, CHIP_BLOCKS * HALF, 3 * HD), BF)
    vmem = pl.BlockSpec(memory_space=pltpu.VMEM)
    return pl.pallas_call(
        pack_kernel,
        out_shape=(out, out),
        in_specs=[pl.BlockSpec(memory_space=pltpu.SMEM), vmem, vmem, vmem],
        out_specs=(vmem, vmem),
        compiler_params=pltpu.CompilerParams(vmem_limit_bytes=32 << 20),
        name="pack",
    )(core, q, k, v)


def attend_kernel(ints_ref, y_ref, kvo_ref, o_ref, inv_ref):
    core = ints_ref[0]
    spans_at = 1 + NDOC
    assign_at = spans_at + 2 * NSPAN

    def invert(j, c):
        inv_ref[ints_ref[assign_at + j]] = j
        return c

    lax.fori_loop(0, NBLK, invert, 0)

    def half_pos(index, parity):
        return (index // HALF) * QB + ((index // QTR) % 2) * HALF + parity * QTR + index % QTR

    def query_tile(j, c):
        first = j * TPOS
        pos = half_pos(lax.broadcasted_iota(jnp.int32, (8, TROWS), 1), core) + first
        lo = jnp.zeros_like(pos)
        doc_end = jnp.full_like(pos, ints_ref[1])
        lo_first = jnp.int32(0)
        start = jnp.int32(0)
        for d in range(NDOC):
            end = start + ints_ref[1 + d]
            here = pos >= start
            lo = jnp.where(here, start, lo)
            doc_end = jnp.where(here, end, doc_end)
            lo_first = jnp.where(first >= start, start, lo_first)
            start = end

        def one_span(s, hi):
            a = ints_ref[spans_at + 2 * s]
            b = ints_ref[spans_at + 2 * s + 1]
            return jnp.where((pos >= a) & (pos < b), b, hi)

        hi = lax.fori_loop(0, NSPAN, one_span, pos + 1, unroll=True)
        hi = jnp.minimum(hi, doc_end)
        hi_last = jnp.max(hi)
        lo = lo[:1]
        hi = hi[:1]
        q = y_ref[pl.ds(pl.multiple_of(j * TROWS, TROWS), TROWS), :HD]
        key_iota = half_pos(lax.broadcasted_iota(jnp.int32, (TROWS, TROWS), 0), 0)

        def key_tile(t, carry):
            m, l, acc = carry
            rows = pl.ds(pl.multiple_of(t * TROWS, TROWS), TROWS)
            parts = (
                (y_ref[rows, HD : 2 * HD], y_ref[rows, 2 * HD :], core),
                (kvo_ref[rows, :HD], kvo_ref[rows, HD:], 1 - core),
            )
            scores = []
            for key, _, parity in parts:
                s = lax.dot_general(
                    key, q, (((1,), (1,)), ((), ())), preferred_element_type=F32
                ) * SCALE2
                base = t * TPOS + parity * QTR
                s = jnp.where((key_iota >= lo - base) & (key_iota < hi - base), s, NEG)
                scores.append(s)
            peak = jnp.maximum(
                jnp.max(scores[0], axis=0, keepdims=True), jnp.max(scores[1], axis=0, keepdims=True)
            )
            new_m = jnp.maximum(m, peak)
            factor = jnp.exp2(m - new_m)
            l = l * factor
            acc = acc * factor
            for s, (_, value, _) in zip(scores, parts):
                p = jnp.exp2(s - new_m)
                l = l + jnp.sum(p, axis=0, keepdims=True)
                acc = acc + lax.dot_general(
                    value, p.astype(BF), (((0,), (0,)), ((), ())), preferred_element_type=F32
                )
            return new_m, l, acc

        _, l, acc = lax.fori_loop(
            lo_first // TPOS,
            (hi_last + (TPOS - 1)) // TPOS,
            key_tile,
            (
                jnp.full((1, TROWS), NEG, F32),
                jnp.zeros((1, TROWS), F32),
                jnp.zeros((HD, TROWS), F32),
            ),
        )
        out = jnp.transpose(acc / l).astype(BF)
        for b in range(TILE):
            slot = inv_ref[j * TILE + b]
            chip = slot // CHIP_BLOCKS
            for u in range(2):
                group = (slot % CHIP_BLOCKS) * 2 + u
                o_ref[group // 3, chip, group % 3] = out[
                    b * HALF + u * QTR : b * HALF + (u + 1) * QTR
                ]
        return c

    lax.fori_loop(0, NTILE, query_tile, 0)


def attend(ints, y, kvo):
    vmem = pl.BlockSpec(memory_space=pltpu.VMEM)
    return pl.pallas_call(
        attend_kernel,
        out_shape=jax.ShapeDtypeStruct((2, NCTX, 3, QTR, HD), BF),
        in_specs=[pl.BlockSpec(memory_space=pltpu.SMEM), vmem, vmem],
        out_specs=vmem,
        scratch_shapes=[pltpu.SMEM((NBLK,), jnp.int32)],
        compiler_params=pltpu.CompilerParams(vmem_limit_bytes=32 << 20),
        name="attend",
    )(ints, y, kvo)


COLS = 512


def project_kernel(ids_ref, z_ref, zo_ref, w_ref, wf_ref, wr_ref, o_ref, a_ref):
    core = ids_ref[0]
    t_own = ids_ref[1]

    @pl.when(pl.program_id(0) == 0)
    def _():
        for side in range(2):
            src = t_own if side == 0 else 1 - t_own
            for n in range(HEADS):
                h = n if side == 0 else lax.rem(n + core * (HEADS // 2), HEADS)
                col = pl.ds((side * HEADS + n) * HD, HD)
                for g in range(3):
                    row = pl.multiple_of(g * HALF + core * QTR, QTR)
                    a_ref[pl.ds(row, QTR), col] = z_ref[src, core * HEADS + h, g]
                    row = pl.multiple_of(g * HALF + (1 - core) * QTR, QTR)
                    a_ref[pl.ds(row, QTR), col] = zo_ref[src, h, g]

    half = HEADS * HD
    acc = jnp.dot(a_ref[:, :half], w_ref[...], preferred_element_type=F32)
    acc += jnp.dot(a_ref[:, half : half + half // 2], wf_ref[...], preferred_element_type=F32)
    acc += jnp.dot(a_ref[:, half + half // 2 :], wr_ref[...], preferred_element_type=F32)
    o_ref[...] = acc.astype(BF)


def project(ids, z, zo, w, wf, wr):
    width = w.shape[1]
    half = HEADS * HD
    rows = 3 * HALF
    whole = lambda x: pl.BlockSpec(x.shape, lambda n: (0,) * x.ndim)
    return pl.pallas_call(
        project_kernel,
        grid=(width // COLS,),
        out_shape=jax.ShapeDtypeStruct((rows, width), BF),
        in_specs=[
            pl.BlockSpec(memory_space=pltpu.SMEM),
            whole(z),
            whole(zo),
            pl.BlockSpec((half, COLS), lambda n: (0, n)),
            pl.BlockSpec((half // 2, COLS), lambda n: (0, n)),
            pl.BlockSpec((half // 2, COLS), lambda n: (0, n)),
        ],
        out_specs=pl.BlockSpec((rows, COLS), lambda n: (0, n)),
        scratch_shapes=[pltpu.VMEM((rows, 2 * half), BF)],
        compiler_params=pltpu.CompilerParams(vmem_limit_bytes=48 << 20),
        name="project",
    )(ids, z, zo, w, wf, wr)


SWAP = [(0, 1), (1, 0)]


def shards(q, k, v, w, doc_lengths, spans, assignment):
    core = lax.axis_index("core").astype(jnp.int32)
    t_own = lax.axis_index("tensor").astype(jnp.int32)
    chip = lax.axis_index("context").astype(jnp.int32)

    depth = w.shape[0] // 2
    w_mine = lax.dynamic_slice_in_dim(w, core * depth, depth, 0)
    across = [(a * 2 + b, (1 - a) * 2 + 1 - b) for a in range(2) for b in range(2)]
    w_fetched = lax.ppermute(w_mine, ("z_lo", "tensor"), across)
    w_shared = lax.ppermute(w_fetched, "core", SWAP)

    ints = jnp.concatenate([doc_lengths, spans.reshape(-1), assignment])
    ints_other = lax.ppermute(ints, "core", SWAP)
    ints = jnp.where(chip // HEADS == core, ints, ints_other)
    ints = jnp.concatenate([core[None], ints])

    own, send = pack(core[None], q, k, v)
    recv = lax.ppermute(send, "core", SWAP)
    x = jnp.where(
        core == 0, jnp.concatenate([own, recv], axis=0), jnp.concatenate([recv, own], axis=0)
    )
    y = lax.all_to_all(x, "context", 0, 0, tiled=True).reshape(ROWS, 3 * HD)
    kvo = lax.ppermute(y[:, HD:], "core", SWAP)
    att = attend(ints, y, kvo)
    z = lax.all_to_all(
        att.reshape(2 * NCTX, 3, QTR, HD), ("tensor", "context"), 0, 0, tiled=True
    ).reshape(2, 2 * HEADS, 3, QTR, HD)
    z_send = lax.dynamic_slice_in_dim(z, (1 - core) * HEADS, HEADS, 1)
    zo = lax.ppermute(z_send, "core", SWAP)
    return project(jnp.stack([core, t_own]), z, zo, w, w_fetched, w_shared)


def solution(mesh):
    fine = Mesh(
        mesh.devices.reshape(2, 2, NCTX, 2), ("z_lo", "core", "context", "tensor")
    )
    dp = ("z_lo", "core")
    rows = P(dp + ("context",), "tensor")
    placed = (rows, rows, rows, P("tensor", None), P(dp), P(dp, None), P(dp))
    return jax.shard_map(
        shards,
        mesh=fine,
        in_specs=placed,
        out_specs=P(dp + ("context", "tensor"), None),
        check_vma=False,
    )
```

time: 463 us -> 175 us (0.38)
  waiting for transfers between devices: 335 us -> 105 us
  matrix products: 57.3 us -> 0 us
  Pallas kernels: 0 us -> 36.6 us
  other arithmetic: 28.7 us -> 2 us
  starting transfers between devices: 0.12 us -> 25.5 us
  local copies, waits for them, and re-layouts: 27.4 us -> 6.32 us
  between operations: 13.2 us -> 0.1 us
    all_gather x3 -> x0, waiting for transfers between devices: 286 us -> none  [the longest x1 101 us: shards(): lax.all_gather(values, 'context', axis=0, tiled=True)]
    ppermute x0 -> x6, waiting for transfers between devices: none -> 89.5 us  [the longest x1 78.3 us: shards(): w_fetched = lax.ppermute(w_mine, ('z_lo', 'tensor'), across)]
    dot_general x17 -> x0, matrix products: 57.3 us -> none  [the longest x8 31.6 us: advance(): jnp.einsum('hrk,khd->hrd', weights.astype(jnp.bfloat16), block_values, pr...]
    reduce_scatter x1 -> x0, waiting for transfers between devices: 48 us -> none  [shards(): lax.psum_scatter(jnp.dot(attended, out_weight, preferred_element_type=jnp...]
    pallas_call x0 -> x3, Pallas kernels: none -> 36.6 us  [the longest x1 25.5 us: attend(): pl.pallas_call(attend_kernel, out_shape=jax.ShapeDtypeStruct((2, NCTX, 3,...]
    reduce_sum x40 -> x0, other arithmetic: 20.9 us -> none  [the longest x8 18 us: advance(): denominator = denominator * factor + jnp.sum(weights, axis=2)]
    all_to_all x0 -> x2, starting transfers between devices: none -> 18 us  [the longest x1 11.3 us: shards(): lax.all_to_all(att.reshape(2 * NCTX, 3, QTR, HD), ('tensor', 'context'),...]
    all_to_all x0 -> x2, waiting for transfers between devices: none -> 15.3 us  [the longest x1 15.3 us: shards(): lax.all_to_all(att.reshape(2 * NCTX, 3, QTR, HD), ('tensor', 'context'),...]
  transfers between devices with their start and end apart: 4 -> 8, of which waited for: 4 -> 6; matrix products, arithmetic and copies ran while one was open for 2% -> 2% of each run, Pallas kernels for 0% -> 15%
where the time goes in v1:
time: 175 us
  waiting for transfers between devices  105 us (60%)
  Pallas kernels  36.6 us (21%)
  starting transfers between devices  25.5 us (15%)
  local copies, waits for them, and re-layouts  6.32 us (4%)
  other arithmetic  2 us (1%)
    ppermute x1, waiting for transfers between devices, shards(): w_fetched = lax.ppermute(w_mine, ('z_lo', 'tensor'), across)  78.3 us
    pallas_call x1, Pallas kernels, attend(): pl.pallas_call(attend_kernel, out_shape=jax.ShapeDtypeStruct((2, NCTX, 3,...  25.5 us
    all_to_all x1, waiting for transfers between devices, shards(): lax.all_to_all(att.reshape(2 * NCTX, 3, QTR, HD), ('tensor', 'context'),...  15.3 us
    all_to_all x1, starting transfers between devices, shards(): lax.all_to_all(att.reshape(2 * NCTX, 3, QTR, HD), ('tensor', 'context'),...  11.3 us
    pallas_call x1, Pallas kernels, project(): pl.pallas_call(project_kernel, grid=(width // COLS,), out_shape=jax.Shape...  10.8 us
    all_to_all x1, starting transfers between devices, shards(): y = lax.all_to_all(x, 'context', 0, 0, tiled=True).reshape(ROWS, 3 * HD)  6.75 us
    dynamic_slice x1, local copies, waits for them, and re-layouts, shards(): w_mine = lax.dynamic_slice_in_dim(w, core * depth, depth, 0)  4.82 us
    ppermute x1, waiting for transfers between devices, shards(): ints_other = lax.ppermute(ints, 'core', SWAP)  4.7 us
  transfers between devices with their start and end apart: 8, of which 6 were waited for; matrix products, arithmetic and copies ran while one was open for 2% of the time, Pallas kernels for 15%

profile of v1, /device:TPU:1, one launch (start us, length us, event | category | flops | bytes accessed | tf_op | source)
XLA Modules:
  0.0 175.4 jit_solution(2415947867674439451)
XLA Ops:
  0.0 0.0 copy-start
  0.0 0.0 copy-start.1
  0.0 0.0 copy-start.2
  0.0 4.8 %constant_dynamic-slice_fusion = bf16[512,4096]{1,0:T(8,128)(2,1)} fusion(bf16[1024,4096]{1,0:T(8,128)(2,1)} %w_ref.1, s32[]{:T(128)S(6)} %select_n.33), kind=kLoop, calls=%fused_computation.5 | loop fusion | bytes 8388612 | tf_op jit(solution)/shard_map/dynamic_slice | solution.py:227
  4.8 4.6 %collective-permute-start.4 = (bf16[512,4096]{1,0:T(8,128)(2,1)}, bf16[512,4096]{1,0:T(8,128)(2,1)}, u32[]{:S(2)}, u32[]{:S(2)}) collective-permute-start(bf16[512,4096]{1,0:T(8,128)(2,1)} %constant_dynamic-slice_fusion), channel_id=1, source_target_pairs={{0,65},{1,64},{64,1},{65,0},{2,67},{3,66},{66,3},{67,2},{4,69},{5,... | collective-permute-start | bytes 12582920 | tf_op jit(solution)/shard_map/ppermute | solution.py:229
  9.4 0.0 copy-done
  9.4 0.0 copy-done.1
  9.4 0.0 copy-done.2
  9.4 0.3 pack.1
  9.7 1.0 collective-permute-start.1
  10.8 2.5 %collective-permute-done.1 = bf16[8,192,384]{2,1,0:T(8,128)(2,1)S(1)} collective-permute-done((bf16[8,192,384]{2,1,0:T(8,128)(2,1)S(1)}, bf16[8,192,384]{2,1,0:T(8,128)(2,1)S(1)}, u32[]{:S(2)}, u32[]{:S(2)}) %collective-permute-start.1) | collective-permute-done | bytes 1179680 | tf_op jit(solution)/shard_map/ppermute | solution.py:238
  13.3 1.7 maximum_select_fusion
  14.9 6.8 %all-to-all-start = ((bf16[16,192,384]{2,1,0:T(8,128)(2,1)}), bf16[16,192,384]{2,1,0:T(8,128)(2,1)S(1)}, u32[]{:S(2)}, u32[]{:S(2)}) async-start(bf16[16,192,384]{2,1,0:T(8,128)(2,1)} %maximum_select_fusion), calls=%async_computation | async-start | bytes 4718592 | tf_op jit(solution)/shard_map/all_to_all | solution.py:242
  21.7 0.0 copy-start.5
  21.7 0.0 copy-start.3
  21.7 0.0 copy-start.4
  21.7 78.3 %collective-permute-done.4.wf_ref = bf16[512,4096]{1,0:T(8,128)(2,1)} collective-permute-done((bf16[512,4096]{1,0:T(8,128)(2,1)}, bf16[512,4096]{1,0:T(8,128)(2,1)}, u32[]{:S(2)}, u32[]{:S(2)}) %collective-permute-start.4) | collective-permute-done | bytes 4194336 | tf_op jit(solution)/shard_map/ppermute | solution.py:229
  100.0 1.2 collective-permute-start.5
  101.3 0.0 all-to-all-done
  101.3 1.2 slice.4
  102.5 0.0 collective-permute-start.2
  102.5 0.0 copy-done.5
  102.5 0.1 copy.9
  102.6 0.1 reshape.12
  102.7 0.0 copy-done.3
  102.7 0.0 copy-done.4
  102.7 0.1 pad_add_fusion.1
  102.8 0.5 collective-permute-start
  103.3 4.7 %collective-permute-done = s32[116]{0:T(128)S(1)} collective-permute-done((s32[116]{0:T(128)S(1)}, s32[116]{0:T(128)S(1)}, u32[]{:S(2)}, u32[]{:S(2)}) %collective-permute-start) | collective-permute-done | bytes 496 | tf_op jit(solution)/shard_map/ppermute | solution.py:233
  108.0 0.1 broadcast_select_fusion
  108.1 0.1 pad_add_fusion.2.ints_ref
  108.2 2.4 %collective-permute-done.2.kvo_ref = bf16[3072,256]{1,0:T(8,128)(2,1)} collective-permute-done((bf16[3072,256]{1,0:T(8,128)(2,1)}, bf16[3072,256]{1,0:T(8,128)(2,1)}, u32[]{:S(2)}, u32[]{:S(2)}) %collective-permute-start.2) | collective-permute-done | bytes 1572896 | tf_op jit(solution)/shard_map/ppermute | solution.py:243
  110.6 25.5 %attend.1 = bf16[2,16,3,32,128]{4,3,2,1,0:T(8,128)(2,1)} custom-call(s32[117]{0:T(128)S(1)} %pad_add_fusion.2.ints_ref, bf16[3072,384]{1,0:T(8,128)(2,1)S(1)} %bitcast.6, bf16[3072,256]{1,0:T(8,128)(2,1)} %collective-permute-done.2.kvo_ref), custom_call_target="tpu_custom_call" | custom-call | tf_op jit(solution)/shard_map/attend/pallas_call | solution.py:156
  136.2 11.3 %all-to-all-start.1 = ((bf16[32,3,32,128]{3,2,1,0:T(8,128)(2,1)}), bf16[32,3,32,128]{3,2,1,0:T(8,128)(2,1)S(1)}, u32[]{:S(2)}, u32[]{:S(2)}) async-start(bf16[32,3,32,128]{3,2,1,0:T(8,128)(2,1)} %bitcast.3), calls=%async_computation.1 | async-start | bytes 1572864 | tf_op jit(solution)/shard_map/all_to_all | solution.py:245
  147.5 15.3 %all-to-all-done.1 = bf16[32,3,32,128]{3,2,1,0:T(8,128)(2,1)S(1)} async-done(((bf16[32,3,32,128]{3,2,1,0:T(8,128)(2,1)}), bf16[32,3,32,128]{3,2,1,0:T(8,128)(2,1)S(1)}, u32[]{:S(2)}, u32[]{:S(2)}) %all-to-all-start.1) | async-done | bytes 786464 | tf_op jit(solution)/shard_map/all_to_all | solution.py:245
  162.8 0.1 collective-permute-start.3
  162.9 0.1 pad_add_fusion.ids_ref
  163.0 1.6 collective-permute-done.3.zo_ref
  164.6 0.0 collective-permute-done.5.wr_ref
  164.6 10.8 %project.1 = bf16[192,4096]{1,0:T(8,128)(2,1)} custom-call(s32[2]{0:T(128)S(1)} %pad_add_fusion.ids_ref, bf16[2,16,3,32,128]{4,3,2,1,0:T(8,128)(2,1)S(1)} %bitcast.8, bf16[2,8,3,32,128]{4,3,2,1,0:T(8,128)(2,1)S(1)} %collective-permute-done.3.zo_ref, bf16[1024,4096]{1,0:T(8,128)(2,1)} %w_ref.1, bf16[512,4096]{1,0:T(8,128)(2,1)} %collective-permute-done.4.wf_ref, ...), custom_call_target="tpu_custom_call" | custom-call | tf_op jit(solution)/shard_map/project/pallas_call | solution.py:199
  (1 shorter events, 0.0 us)
Async XLA Ops:
  0.0 9.4 %copy-start = (bf16[384,1024]{1,0:T(8,128)(2,1)S(1)}, bf16[384,1024]{1,0:T(8,128)(2,1)}, u32[]{:S(2)}) copy-start(bf16[384,1024]{1,0:T(8,128)(2,1)} %q_ref.1) | copy-start | bytes 2359300
  0.0 9.4 %copy-start.1 = (bf16[384,1024]{1,0:T(8,128)(2,1)S(1)}, bf16[384,1024]{1,0:T(8,128)(2,1)}, u32[]{:S(2)}) copy-start(bf16[384,1024]{1,0:T(8,128)(2,1)} %k_ref.1) | copy-start | bytes 2359300
  0.0 9.4 %copy-start.2 = (bf16[384,1024]{1,0:T(8,128)(2,1)S(1)}, bf16[384,1024]{1,0:T(8,128)(2,1)}, u32[]{:S(2)}) copy-start(bf16[384,1024]{1,0:T(8,128)(2,1)} %v_ref.1) | copy-start | bytes 2359300
  4.8 95.2 %collective-permute-start.4 = (bf16[512,4096]{1,0:T(8,128)(2,1)}, bf16[512,4096]{1,0:T(8,128)(2,1)}, u32[]{:S(2)}, u32[]{:S(2)}) collective-permute-start(bf16[512,4096]{1,0:T(8,128)(2,1)} %constant_dynamic-slice_fusion), channel_id=1, source_target_pairs={{0,65},{1,64},{64,1},{65,0},{2,67},{3,66},{66,3},{67,2},{4,69},{5,... | collective-permute-start | bytes 12582920 | tf_op jit(solution)/shard_map/ppermute | solution.py:229
  9.7 3.5 %collective-permute-start.1 = (bf16[8,192,384]{2,1,0:T(8,128)(2,1)S(1)}, bf16[8,192,384]{2,1,0:T(8,128)(2,1)S(1)}, u32[]{:S(2)}, u32[]{:S(2)}) collective-permute-start(bf16[8,192,384]{2,1,0:T(8,128)(2,1)S(1)} %get-tuple-element.8), channel_id=1, source_target_pairs={{0,32},{32,0},{1,33},{33,1},{2,34},{34,2},{3,35},{35,3},{4,36},{36... | collective-permute-start | bytes 3538952 | tf_op jit(solution)/shard_map/ppermute | solution.py:238
  14.9 86.3 %all-to-all-start = ((bf16[16,192,384]{2,1,0:T(8,128)(2,1)}), bf16[16,192,384]{2,1,0:T(8,128)(2,1)S(1)}, u32[]{:S(2)}, u32[]{:S(2)}) async-start(bf16[16,192,384]{2,1,0:T(8,128)(2,1)} %maximum_select_fusion), calls=%async_computation | async-start | bytes 4718592 | tf_op jit(solution)/shard_map/all_to_all | solution.py:242
  21.7 80.8 %copy-start.5 = (s32[31,2]{0,1:T(2,128)S(1)}, s32[31,2]{0,1:T(2,128)}, u32[]{:S(2)}) copy-start(s32[31,2]{0,1:T(2,128)} %param.12) | copy-start | bytes 748
  21.7 81.0 %copy-start.3 = (s32[48]{0:T(128)S(1)}, s32[48]{0:T(128)}, u32[]{:S(2)}) copy-start(s32[48]{0:T(128)} %param.13) | copy-start | bytes 580
  21.7 81.0 %copy-start.4 = (s32[6]{0:T(128)S(1)}, s32[6]{0:T(128)}, u32[]{:S(2)}) copy-start(s32[6]{0:T(128)} %param.11) | copy-start | bytes 76
  100.0 64.6 %collective-permute-start.5 = (bf16[512,4096]{1,0:T(8,128)(2,1)}, bf16[512,4096]{1,0:T(8,128)(2,1)}, u32[]{:S(2)}, u32[]{:S(2)}) collective-permute-start(bf16[512,4096]{1,0:T(8,128)(2,1)} %collective-permute-done.4.wf_ref), channel_id=1, source_target_pairs={{0,32},{32,0},{1,33},{33,1},{2,34},{34,2},{3,35},{35,3},{4,36},{36... | collective-permute-start | bytes 12582920 | tf_op jit(solution)/shard_map/ppermute | solution.py:230
  102.5 8.1 %collective-permute-start.2 = (bf16[3072,256]{1,0:T(8,128)(2,1)}, bf16[3072,256]{1,0:T(8,128)(2,1)}, u32[]{:S(2)}, u32[]{:S(2)}) collective-permute-start(bf16[3072,256]{1,0:T(8,128)(2,1)} %slice.4), channel_id=1, source_target_pairs={{0,32},{32,0},{1,33},{33,1},{2,34},{34,2},{3,35},{35,3},{4,36},{36... | collective-permute-start | bytes 4718600 | tf_op jit(solution)/shard_map/ppermute | solution.py:243
  102.8 5.2 %collective-permute-start = (s32[116]{0:T(128)S(1)}, s32[116]{0:T(128)S(1)}, u32[]{:S(2)}, u32[]{:S(2)}) collective-permute-start(s32[116]{0:T(128)S(1)} %pad_add_fusion.1), channel_id=1, source_target_pairs={{0,32},{32,0},{1,33},{33,1},{2,34},{34,2},{3,35},{35,3},{4,36},{36... | collective-permute-start | bytes 1400 | tf_op jit(solution)/shard_map/ppermute | solution.py:233
  136.2 26.6 %all-to-all-start.1 = ((bf16[32,3,32,128]{3,2,1,0:T(8,128)(2,1)}), bf16[32,3,32,128]{3,2,1,0:T(8,128)(2,1)S(1)}, u32[]{:S(2)}, u32[]{:S(2)}) async-start(bf16[32,3,32,128]{3,2,1,0:T(8,128)(2,1)} %bitcast.3), calls=%async_computation.1 | async-start | bytes 1572864 | tf_op jit(solution)/shard_map/all_to_all | solution.py:245
  162.8 1.8 %collective-permute-start.3 = (bf16[2,8,3,32,128]{4,3,2,1,0:T(8,128)(2,1)S(1)}, bf16[2,8,3,32,128]{4,3,2,1,0:T(8,128)(2,1)S(1)}, u32[]{:S(2)}, u32[]{:S(2)}) collective-permute-start(bf16[2,8,3,32,128]{4,3,2,1,0:T(8,128)(2,1)S(1)} %constant_dynamic-slice_fusion.1), channel_id=1, source_target_pairs={{0,32},{32,0},{1,33},{33,1},{2,34},{34,2},{3,35},{35,3},{4,36},{36... | collective-permute-start | bytes 1179656 | tf_op jit(solution)/shard_map/ppermute | solution.py:249

commit v2 on v1

v2 whole, which is shorter than its diff:
```python
import functools
import math

import jax
import jax.numpy as jnp
from jax import lax
from jax.experimental import pallas as pl
from jax.experimental.pallas import tpu as pltpu
from jax.sharding import Mesh, PartitionSpec as P

HD = 128
QB = 128
QTR = QB // 4
HALF = QB // 2
NCTX = 16
CHIP_BLOCKS = 3
NBLK = NCTX * CHIP_BLOCKS
HEADS = 8
ROWS = NBLK * HALF
NDOC = 6
NSPAN = 31
TILE = 4
TROWS = TILE * HALF
TPOS = TILE * QB
NTILE = NBLK // TILE
SCALE2 = math.log2(math.e) / math.sqrt(HD)
NEG = -1e30
BF = jnp.bfloat16
F32 = jnp.float32


def pack_kernel(core_ref, q_ref, k_ref, v_ref, own_ref, send_ref):
    core = core_ref[0]
    for out_ref, parity in ((own_ref, core), (send_ref, 1 - core)):
        for a, ref in enumerate((q_ref, k_ref, v_ref)):
            for group in range(2 * CHIP_BLOCKS):
                start = pl.multiple_of(group * HALF + parity * QTR, QTR)
                rows = ref[pl.ds(start, QTR), :]
                for h in range(HEADS):
                    out_ref[h, group * QTR : (group + 1) * QTR, a * HD : (a + 1) * HD] = rows[
                        :, h * HD : (h + 1) * HD
                    ]


def pack(core, q, k, v):
    out = jax.ShapeDtypeStruct((HEADS, CHIP_BLOCKS * HALF, 3 * HD), BF)
    vmem = pl.BlockSpec(memory_space=pltpu.VMEM)
    return pl.pallas_call(
        pack_kernel,
        out_shape=(out, out),
        in_specs=[pl.BlockSpec(memory_space=pltpu.SMEM), vmem, vmem, vmem],
        out_specs=(vmem, vmem),
        compiler_params=pltpu.CompilerParams(vmem_limit_bytes=32 << 20),
        name="pack",
    )(core, q, k, v)


def prepare_kernel(ints_ref, kdoc_ref, qdoc_ref, hi_ref, meta_ref):
    core = ints_ref[0]
    spans_at = 1 + NDOC
    assign_at = spans_at + 2 * NSPAN

    def half_pos(index, parity):
        return 2 * index - (index & (QTR - 1)) + parity * QTR

    lane = lax.broadcasted_iota(jnp.int32, (8, HD), 1)
    starts, start = [], jnp.int32(0)
    first = jnp.zeros((8, HD), jnp.int32)
    last = jnp.zeros((8, HD), jnp.int32)
    for d in range(NDOC):
        end = start + ints_ref[1 + d]
        first = jnp.where(lane == d, start, first)
        last = jnp.where(lane == d, end, last)
        starts.append(start)
        start = end
    first, last = first[:1], last[:1]
    used = lane[:1] < NDOC
    for c in range(NCTX):
        rows = slice(c * CHIP_BLOCKS * HALF, (c + 1) * CHIP_BLOCKS * HALF)
        index = lax.broadcasted_iota(jnp.int32, (CHIP_BLOCKS * HALF, HD), 0)
        base = half_pos(index, 0) + c * CHIP_BLOCKS * QB
        for n, parity in enumerate((core, 1 - core)):
            pos = base + parity * QTR
            inside = (pos >= first) & (pos < last)
            kdoc_ref[n, rows, :] = jnp.where(inside, 1.0, 0.0).astype(BF)
            if n == 0:
                qdoc_ref[rows, :] = jnp.where(inside | ~used, 0.0, NEG).astype(BF)

    def query_tile(j, c):
        tile_first = j * TPOS
        pos = half_pos(lax.broadcasted_iota(jnp.int32, (8, TROWS), 1), core) + tile_first

        def one_span(s, hi):
            a = ints_ref[spans_at + 2 * s]
            b = ints_ref[spans_at + 2 * s + 1]
            return jnp.where((pos >= a) & (pos < b), b, hi)

        hi = lax.fori_loop(0, NSPAN, one_span, pos + 1, unroll=True)
        hi_ref[j] = hi - tile_first
        lo_first = jnp.int32(0)
        for d in range(NDOC):
            lo_first = jnp.where(tile_first >= starts[d], starts[d], lo_first)
        before = j - lo_first // TPOS
        after = jnp.where(jnp.max(hi) > tile_first + TPOS, 1, 0)
        after = jnp.where(j == NTILE - 1, 0, after)
        meta_ref[j] = 2 * before + after
        return c

    lax.fori_loop(0, NTILE, query_tile, 0)

    def invert(j, c):
        meta_ref[NTILE + ints_ref[assign_at + j]] = j
        return c

    lax.fori_loop(0, NBLK, invert, 0)


def prepare(ints):
    vmem = pl.BlockSpec(memory_space=pltpu.VMEM)
    smem = pl.BlockSpec(memory_space=pltpu.SMEM)
    return pl.pallas_call(
        prepare_kernel,
        out_shape=(
            jax.ShapeDtypeStruct((2, ROWS, HD), BF),
            jax.ShapeDtypeStruct((ROWS, HD), BF),
            jax.ShapeDtypeStruct((NTILE, 8, TROWS), jnp.int32),
            jax.ShapeDtypeStruct((NTILE + NBLK,), jnp.int32),
        ),
        in_specs=[smem],
        out_specs=(vmem, vmem, vmem, smem),
        compiler_params=pltpu.CompilerParams(vmem_limit_bytes=32 << 20),
        name="prepare",
    )(ints)


AHEAD = 2 * HALF
MAXBEFORE = 3


def attend_kernel(core_ref, meta_ref, y_ref, kvo_ref, kdoc_ref, qdoc_ref, hi_ref, o_ref):
    core = core_ref[0]

    def half_pos(index):
        return 2 * index - (index & (QTR - 1))

    def query_tile(j, c):
        qrows = pl.ds(pl.multiple_of(j * TROWS, TROWS), TROWS)
        q = jnp.concatenate([y_ref[qrows, :HD], qdoc_ref[qrows, :]], axis=1)

        def run(before, after):
            start = pl.multiple_of((j - before) * TROWS, TROWS)
            count = (before + 1) * TROWS + after * AHEAD
            rows = pl.ds(start, count)
            own = (y_ref[rows, HD : 2 * HD], y_ref[rows, 2 * HD :], kdoc_ref[0, rows, :], core)
            other = (kvo_ref[rows, :HD], kvo_ref[rows, HD:], kdoc_ref[1, rows, :], 1 - core)
            scores = []
            tail = before * TROWS
            key_pos = half_pos(lax.broadcasted_iota(jnp.int32, (count - tail, TROWS), 0))
            for key, _, doc, parity in (own, other):
                s = lax.dot_general(
                    jnp.concatenate([key, doc], axis=1),
                    q,
                    (((1,), (1,)), ((), ())),
                    preferred_element_type=F32,
                )
                end = jnp.where(key_pos < hi_ref[j, :1, :] - parity * QTR, s[tail:], NEG)
                scores.append([s[:tail], end] if before else [end])
            peak = functools.reduce(
                jnp.maximum, [jnp.max(s, axis=0, keepdims=True) for part in scores for s in part]
            )
            l = jnp.zeros((1, TROWS), F32)
            acc = jnp.zeros((HD, TROWS), F32)
            for part, (_, value, _, _) in zip(scores, (own, other)):
                weights = []
                for s in part:
                    p = jnp.exp2((s - peak) * SCALE2)
                    l = l + jnp.sum(p, axis=0, keepdims=True)
                    weights.append(p.astype(BF))
                p = jnp.concatenate(weights, axis=0) if before else weights[0]
                acc = acc + lax.dot_general(
                    value, p, (((0,), (0,)), ((), ())), preferred_element_type=F32
                )
            out = jnp.transpose(acc / l).astype(BF)
            for b in range(TILE):
                slot = meta_ref[NTILE + j * TILE + b]
                chip = slot // CHIP_BLOCKS
                for u in range(2):
                    group = (slot % CHIP_BLOCKS) * 2 + u
                    o_ref[group // 3, chip, group % 3] = out[
                        b * HALF + u * QTR : b * HALF + (u + 1) * QTR
                    ]

        case = meta_ref[j]
        for before in range(MAXBEFORE + 1):
            for after in range(2):
                pl.when(case == 2 * before + after)(functools.partial(run, before, after))
        return c

    lax.fori_loop(0, NTILE, query_tile, 0)


def attend(core, meta, y, kvo, kdoc, qdoc, hi):
    vmem = pl.BlockSpec(memory_space=pltpu.VMEM)
    smem = pl.BlockSpec(memory_space=pltpu.SMEM)
    return pl.pallas_call(
        attend_kernel,
        out_shape=jax.ShapeDtypeStruct((2, NCTX, 3, QTR, HD), BF),
        in_specs=[smem, smem] + [vmem] * 5,
        out_specs=vmem,
        compiler_params=pltpu.CompilerParams(vmem_limit_bytes=40 << 20),
        name="attend",
    )(core, meta, y, kvo, kdoc, qdoc, hi)


COLS = 512
CTX = ("y", "x")
NLINE = 4
CHUNKS = 1
PIECE = HEADS * HD // NLINE // CHUNKS
PHEADS = PIECE // HD


def project_kernel(ids_ref, z_ref, zo_ref, w_ref, *refs):
    count = (len(refs) - 3) // 2
    weights, (o_ref, a_ref, b_ref) = (refs[:count], refs[count : 2 * count]), refs[2 * count :]
    core, t_own = ids_ref[0], ids_ref[1]
    step = pl.program_id(0)

    @pl.when(step == 0)
    def _():
        def head(ref, at, src, h):
            col = slice(at * HD, (at + 1) * HD)
            for g in range(3):
                row = pl.multiple_of(g * HALF + core * QTR, QTR)
                ref[pl.ds(row, QTR), col] = z_ref[src, core * HEADS + h, g]
                row = pl.multiple_of(g * HALF + (1 - core) * QTR, QTR)
                ref[pl.ds(row, QTR), col] = zo_ref[src, h, g]

        for h in range(HEADS):
            head(a_ref, h, t_own, h)
        for half in range(2):
            for n in range(CHUNKS * NLINE):
                piece = (n & -NLINE) + ((ids_ref[2 + half] + n) & (NLINE - 1))
                for h in range(PHEADS):
                    head(b_ref.at[half], n * PHEADS + h, 1 - t_own, piece * PHEADS + h)

    own = HEADS * HD

    def run(half):
        acc = jnp.dot(a_ref[:, :own], w_ref[...], preferred_element_type=F32)
        at = 0
        for ref in weights[half]:
            depth = ref.shape[0]
            acc += jnp.dot(
                b_ref[half, :, at : at + depth], ref[...], preferred_element_type=F32
            )
            at += depth
        o_ref[...] = acc.astype(BF)

    steps = pl.num_programs(0) // 2
    pl.when(step < steps)(functools.partial(run, 0))
    pl.when(step >= steps)(functools.partial(run, 1))


def project(ids, z, zo, w, mine, other):
    width = w.shape[1]
    rows = 3 * HALF
    steps = width // COLS // 2
    whole = lambda x: pl.BlockSpec(x.shape, lambda n, ids: (0,) * x.ndim)
    column = lambda n, ids: (0, (n + ids[0] * steps) & (2 * steps - 1))
    first = lambda n, ids: (0, jnp.minimum(n, steps - 1))
    second = lambda n, ids: (0, jnp.maximum(n - steps, 0))
    return pl.pallas_call(
        project_kernel,
        grid_spec=pltpu.PrefetchScalarGridSpec(
            num_scalar_prefetch=1,
            grid=(2 * steps,),
            in_specs=[whole(z), whole(zo), pl.BlockSpec((HEADS * HD, COLS), column)]
            + [pl.BlockSpec((m.shape[0], COLS), first) for m in mine]
            + [pl.BlockSpec((m.shape[0], COLS), second) for m in other],
            out_specs=pl.BlockSpec((rows, COLS), column),
            scratch_shapes=[
                pltpu.VMEM((rows, HEADS * HD), BF),
                pltpu.VMEM((2, rows, HEADS * HD), BF),
            ],
        ),
        out_shape=jax.ShapeDtypeStruct((rows, width), BF),
        compiler_params=pltpu.CompilerParams(vmem_limit_bytes=48 << 20),
        name="project",
    )(ids, z, zo, w, *mine, *other)


SWAP = [(0, 1), (1, 0)]


def swap(x):
    return lax.ppermute(x, "core", SWAP)


def after(values, *others):
    return lax.optimization_barrier((values,) + others)[0]


def along_line(x, step):
    pairs = []
    for y in range(NLINE):
        for x_at in range(NLINE):
            for core in range(2):
                to = (y, (x_at - step) % NLINE) if core == 0 else ((y - step) % NLINE, x_at)
                index = lambda y, x: (core * NLINE + y) * NLINE + x
                pairs.append((index(y, x_at), index(*to)))
    return lax.ppermute(x, ("core",) + CTX, pairs)


def shards(q, k, v, w, doc_lengths, spans, assignment):
    core = lax.axis_index("core").astype(jnp.int32)
    t_own = lax.axis_index("tensor").astype(jnp.int32)
    x_at = lax.axis_index("x").astype(jnp.int32)
    y_at = lax.axis_index("y").astype(jnp.int32)
    chip = y_at * NLINE + x_at

    across = [(a * 2 + b, (1 - a) * 2 + 1 - b) for a in range(2) for b in range(2)]
    from_z = lambda x: lax.ppermute(x, ("z_lo", "tensor"), across)
    half = w.shape[1] // 2
    line = jnp.where(core == 0, x_at, y_at)
    fetched = [
        from_z(lax.dynamic_slice(w, (PIECE * (c * NLINE + line), core * half), (PIECE, half)))
        for c in range(CHUNKS)
    ]

    ints = jnp.concatenate([doc_lengths, spans.reshape(-1), assignment])
    ints = jnp.where(chip // HEADS == core, ints, swap(ints))
    ints = jnp.concatenate([core[None], ints])

    own, send = pack(core[None], q, k, v)
    recv = swap(send)
    x = jnp.where(
        core == 0, jnp.concatenate([own, recv], axis=0), jnp.concatenate([recv, own], axis=0)
    )
    y = lax.all_to_all(x, CTX, 0, 0, tiled=True).reshape(ROWS, 3 * HD)
    kdoc, qdoc, hi, meta = prepare(ints)
    y, kdoc, qdoc, hi, meta = lax.optimization_barrier((y, kdoc, qdoc, hi, meta))
    y, fetched = lax.optimization_barrier((y, fetched))
    kvo = swap(y[:, HD:])

    pieces = [[piece] + [along_line(piece, step) for step in (1, 2, 3)] for piece in fetched]
    att = attend(core[None], meta, y, kvo, kdoc, qdoc, hi)
    att, pieces = lax.optimization_barrier((att, pieces))
    mine = sum(pieces, [])
    other = [swap(p) for p in mine]
    z = lax.all_to_all(
        att.reshape(2 * NCTX, 3, QTR, HD), ("tensor",) + CTX, 0, 0, tiled=True
    ).reshape(2, 2 * HEADS, 3, QTR, HD)
    zo = swap(lax.dynamic_slice_in_dim(z, (1 - core) * HEADS, HEADS, 1))
    lines = jnp.where(core == 0, jnp.stack([x_at, y_at]), jnp.stack([y_at, x_at]))
    ids = jnp.concatenate([jnp.stack([core, t_own]), lines])
    return project(ids, z, zo, w, mine, other)


def solution(mesh):
    fine = Mesh(
        mesh.devices.reshape(2, 2, NLINE, NLINE, 2), ("z_lo", "core", "y", "x", "tensor")
    )
    dp = ("z_lo", "core")
    rows = P(dp + CTX, "tensor")
    placed = (rows, rows, rows, P("tensor", None), P(dp), P(dp, None), P(dp))
    return jax.shard_map(
        shards,
        mesh=fine,
        in_specs=placed,
        out_specs=P(dp + CTX + ("tensor",), None),
        check_vma=False,
    )
```

time: 175 us -> 123 us (0.70)
  waiting for transfers between devices: 105 us -> 46.9 us
  local copies, waits for them, and re-layouts: 6.32 us -> 12.3 us
  Pallas kernels: 36.6 us -> 31.2 us
  starting transfers between devices: 25.5 us -> 28.9 us
    ppermute x6 -> x12, waiting for transfers between devices: 89.5 us -> 16 us  [the longest x3 9.99 us: along_line(): return lax.ppermute(x, ('core',) + CTX, pairs)]
    all_to_all x2, waiting for transfers between devices: 15.3 us -> 30.9 us  [the longest x1 20.4 us: shards(): y = lax.all_to_all(x, CTX, 0, 0, tiled=True).reshape(ROWS, 3 * HD)]
    pallas_call x1, Pallas kernels: 25.5 us -> 14.6 us  [attend(): pl.pallas_call(attend_kernel, out_shape=jax.ShapeDtypeStruct((2, NCTX, 3,...]
    unnamed x13 -> x33, local copies, waits for them, and re-layouts: 0.13 us -> 8.96 us
    ppermute x6 -> x12, starting transfers between devices: 7.47 us -> 15.5 us  [the longest x8 9.88 us: swap(): return lax.ppermute(x, 'core', SWAP)]
    pallas_call x1 -> x2, Pallas kernels: 10.8 us -> 16.2 us  [the longest x1 10.9 us: project(): pl.pallas_call(project_kernel, grid_spec=pltpu.PrefetchScalarGridSpec(num...]
    all_to_all x2, starting transfers between devices: 18 us -> 13.4 us  [the longest x1 6.98 us: shards(): y = lax.all_to_all(x, CTX, 0, 0, tiled=True).reshape(ROWS, 3 * HD)]
    dynamic_slice x2, local copies, waits for them, and re-layouts: 4.85 us -> 3.1 us  [the longest x1 2.31 us: shards(): lax.dynamic_slice(w, (PIECE * (c * NLINE + line), core * half), (PIECE, h...]
  transfers between devices with their start and end apart: 8 -> 14, of which waited for: 6 -> 7; matrix products, arithmetic and copies ran while one was open for 2% -> 3% of each run, Pallas kernels for 15% -> 16%
where the time goes in v2:
time: 123 us
  waiting for transfers between devices  46.9 us (38%)
  Pallas kernels  31.2 us (25%)
  starting transfers between devices  28.9 us (23%)
  local copies, waits for them, and re-layouts  12.3 us (10%)
  other arithmetic  3.24 us (3%)
    all_to_all x1, waiting for transfers between devices, shards(): y = lax.all_to_all(x, CTX, 0, 0, tiled=True).reshape(ROWS, 3 * HD)  20.4 us
    pallas_call x1, Pallas kernels, attend(): pl.pallas_call(attend_kernel, out_shape=jax.ShapeDtypeStruct((2, NCTX, 3,...  14.6 us
    pallas_call x1, Pallas kernels, project(): pl.pallas_call(project_kernel, grid_spec=pltpu.PrefetchScalarGridSpec(num...  10.9 us
    all_to_all x1, waiting for transfers between devices, shards(): lax.all_to_all(att.reshape(2 * NCTX, 3, QTR, HD), ('tensor',) + CTX, 0, 0...  10.5 us
    ppermute x3, waiting for transfers between devices, along_line(): return lax.ppermute(x, ('core',) + CTX, pairs)  9.99 us
    ppermute x8, starting transfers between devices, swap(): return lax.ppermute(x, 'core', SWAP)  9.88 us
    unnamed x33, local copies, waits for them, and re-layouts  8.96 us
    all_to_all x1, starting transfers between devices, shards(): y = lax.all_to_all(x, CTX, 0, 0, tiled=True).reshape(ROWS, 3 * HD)  6.98 us
  transfers between devices with their start and end apart: 14, of which 7 were waited for; matrix products, arithmetic and copies ran while one was open for 3% of the time, Pallas kernels for 16%

profile of v2, /device:TPU:1, one launch (start us, length us, event | category | flops | bytes accessed | tf_op | source)
XLA Modules:
  0.0 122.6 jit_solution(16429674400998802204)
XLA Ops:
  0.0 1.1 copy-done.8
  1.1 1.1 copy-done.9
  2.3 1.1 copy-done.10
  3.4 0.3 pack.1
  3.7 1.5 %collective-permute-start = (bf16[8,192,384]{2,1,0:T(8,128)(2,1)S(1)}, bf16[8,192,384]{2,1,0:T(8,128)(2,1)}, u32[]{:S(2)}, u32[]{:S(2)}) collective-permute-start(bf16[8,192,384]{2,1,0:T(8,128)(2,1)S(1)} %get-tuple-element.24), channel_id=1, source_target_pairs={{0,32},{32,0},{1,33},{33,1},{2,34},{34,2},{3,35},{35,3},{4,36},{36... | collective-permute-start | bytes 3538952 | tf_op jit(solution)/shard_map/ppermute | solution.py:297
  5.2 2.6 %collective-permute-done = bf16[8,192,384]{2,1,0:T(8,128)(2,1)} collective-permute-done((bf16[8,192,384]{2,1,0:T(8,128)(2,1)S(1)}, bf16[8,192,384]{2,1,0:T(8,128)(2,1)}, u32[]{:S(2)}, u32[]{:S(2)}) %collective-permute-start) | collective-permute-done | bytes 1179680 | tf_op jit(solution)/shard_map/ppermute | solution.py:297
  7.8 2.9 %maximum_select_fusion = bf16[16,192,384]{2,1,0:T(8,128)(2,1)} fusion(bf16[8,192,384]{2,1,0:T(8,128)(2,1)} %collective-permute-done, bf16[8,192,384]{2,1,0:T(8,128)(2,1)S(1)} %get-tuple-element.23, pred[]{:T(512)S(6)} %eq.8), kind=kLoop, calls=%fused_computation | loop fusion | flops 3538944 | bytes 4718593 | tf_op jit(solution)/shard_map/jit(_where)/select_n | solution.py:337
  10.7 7.0 %all-to-all-start = ((bf16[16,192,384]{2,1,0:T(8,128)(2,1)}), bf16[16,192,384]{2,1,0:T(8,128)(2,1)S(1)}, u32[]{:S(2)}, u32[]{:S(2)}) async-start(bf16[16,192,384]{2,1,0:T(8,128)(2,1)} %maximum_select_fusion), calls=%async_computation | async-start | bytes 4718592 | tf_op jit(solution)/shard_map/all_to_all | solution.py:340
  17.7 2.3 %dynamic_slice.6 = bf16[256,2048]{1,0:T(8,128)(2,1)} dynamic-slice(bf16[1024,4096]{1,0:T(8,128)(2,1)} %w_ref.1, s32[]{:T(128)S(6)} %select_n.49, s32[]{:T(128)S(6)} %select_n.50), dynamic_slice_sizes={256,2048} | dynamic-slice | bytes 2097156 | tf_op jit(solution)/shard_map/dynamic_slice | solution.py:327
  20.0 3.8 %collective-permute-start.2 = (bf16[256,2048]{1,0:T(8,128)(2,1)}, bf16[256,2048]{1,0:T(8,128)(2,1)S(1)}, u32[]{:S(2)}, u32[]{:S(2)}) collective-permute-start(bf16[256,2048]{1,0:T(8,128)(2,1)} %dynamic_slice.6), channel_id=1, source_target_pairs={{0,65},{1,64},{64,1},{65,0},{2,67},{3,66},{66,3},{67,2},{4,69},{5,... | collective-permute-start | bytes 3145736 | tf_op jit(solution)/shard_map/ppermute | solution.py:323
  23.8 0.1 copy.9
  23.9 0.1 reshape.13
  24.0 0.1 pad_add_fusion.1
  24.1 1.0 collective-permute-start.1
  25.0 0.8 collective-permute-done.1
  25.8 0.1 broadcast_select_fusion
  25.9 0.1 pad_add_fusion.2.ints_ref
  26.0 5.3 %prepare.1 = (bf16[2,3072,128]{2,1,0:T(8,128)(2,1)S(1)}, bf16[3072,128]{1,0:T(8,128)(2,1)S(1)}, s32[12,8,256]{2,1,0:T(8,128)S(1)}, s32[60]{0:T(128)S(1)}) custom-call(s32[117]{0:T(128)S(1)} %pad_add_fusion.2.ints_ref), custom_call_target="tpu_custom_call" | custom-call | tf_op jit(solution)/shard_map/prepare/pallas_call | solution.py:121
  31.3 0.0 copy-start
  31.3 1.1 copy-done
  32.4 0.9 copy-done.11
  33.3 20.4 %all-to-all-done = bf16[16,192,384]{2,1,0:T(8,128)(2,1)S(1)} async-done(((bf16[16,192,384]{2,1,0:T(8,128)(2,1)}), bf16[16,192,384]{2,1,0:T(8,128)(2,1)S(1)}, u32[]{:S(2)}, u32[]{:S(2)}) %all-to-all-start) | async-done | bytes 2359328 | tf_op jit(solution)/shard_map/all_to_all | solution.py:340
  53.7 0.1 slice.3
  53.8 1.6 %collective-permute-start.3 = (bf16[3072,256]{1,0:T(8,128)(2,1)S(1)}, bf16[3072,256]{1,0:T(8,128)(2,1)S(1)}, u32[]{:S(2)}, u32[]{:S(2)}) collective-permute-start(bf16[3072,256]{1,0:T(8,128)(2,1)S(1)} %slice.3), channel_id=1, source_target_pairs={{0,32},{32,0},{1,33},{33,1},{2,34},{34,2},{3,35},{35,3},{4,36},{36... | collective-permute-start | bytes 4718600 | tf_op jit(solution)/shard_map/ppermute | solution.py:297
  55.4 1.3 %collective-permute-start.4 = (bf16[256,2048]{1,0:T(8,128)(2,1)S(1)}, bf16[256,2048]{1,0:T(8,128)(2,1)S(1)}, u32[]{:S(2)}, u32[]{:S(2)}) collective-permute-start(bf16[256,2048]{1,0:T(8,128)(2,1)S(1)} %collective-permute-done.2.refs_0_), channel_id=1, source_target_pairs={{0,6},{32,56},{2,0},{34,58},{4,2},{36,60},{6,4},{38,62},{8,14},{40... | collective-permute-start | bytes 3145736 | tf_op jit(solution)/shard_map/ppermute | solution.py:312
  56.7 0.3 collective-permute-start.5
  57.0 0.3 collective-permute-start.6
  57.3 1.2 collective-permute-done.3.kvo_ref
  58.4 14.6 %attend.1 = bf16[2,16,3,32,128]{4,3,2,1,0:T(8,128)(2,1)} custom-call(s32[1]{0:T(128)} %bitcast.core_ref, s32[60]{0:T(128)S(1)} %get-tuple-element.29.meta_ref, bf16[3072,384]{1,0:T(8,128)(2,1)S(1)} %bitcast.8, bf16[3072,256]{1,0:T(8,128)(2,1)S(1)} %collective-permute-done.3.kvo_ref, bf16[2,3072,128]{2,1,0:T(8,128)(2,1)S(1)} %copy-done.1, ...), custom_call_target="tpu_custom_call" | custom-call | tf_op jit(solution)/shard_map/attend/pallas_call | solution.py:205
  73.1 0.0 collective-permute-done.4.refs_1_
  73.1 0.0 collective-permute-done.5.refs_2_
  73.1 10.0 %collective-permute-done.6.refs_3_ = bf16[256,2048]{1,0:T(8,128)(2,1)S(1)} collective-permute-done((bf16[256,2048]{1,0:T(8,128)(2,1)S(1)}, bf16[256,2048]{1,0:T(8,128)(2,1)S(1)}, u32[]{:S(2)}, u32[]{:S(2)}) %collective-permute-start.6) | collective-permute-done | bytes 1048608 | tf_op jit(solution)/shard_map/ppermute | solution.py:312
  83.1 1.0 copy-done.6
  84.1 6.4 %all-to-all-start.1 = ((bf16[32,3,32,128]{3,2,1,0:T(8,128)(2,1)}), bf16[32,3,32,128]{3,2,1,0:T(8,128)(2,1)S(1)}, u32[]{:S(2)}, u32[]{:S(2)}) async-start(bf16[32,3,32,128]{3,2,1,0:T(8,128)(2,1)} %bitcast.5), calls=%async_computation.1 | async-start | bytes 1572864 | tf_op jit(solution)/shard_map/all_to_all | solution.py:351
  90.5 2.0 %collective-permute-start.10 = (bf16[256,2048]{1,0:T(8,128)(2,1)}, bf16[256,2048]{1,0:T(8,128)(2,1)}, u32[]{:S(2)}, u32[]{:S(2)}) collective-permute-start(bf16[256,2048]{1,0:T(8,128)(2,1)} %copy-done.4), channel_id=1, source_target_pairs={{0,32},{32,0},{1,33},{33,1},{2,34},{34,2},{3,35},{35,3},{4,36},{36... | collective-permute-start | bytes 3145736 | tf_op jit(solution)/shard_map/ppermute | solution.py:297
  92.5 0.1 collective-permute-start.11
  92.6 0.4 collective-permute-start.8
  93.0 0.1 collective-permute-start.9
  93.1 10.5 %all-to-all-done.1 = bf16[32,3,32,128]{3,2,1,0:T(8,128)(2,1)S(1)} async-done(((bf16[32,3,32,128]{3,2,1,0:T(8,128)(2,1)}), bf16[32,3,32,128]{3,2,1,0:T(8,128)(2,1)S(1)}, u32[]{:S(2)}, u32[]{:S(2)}) %all-to-all-start.1) | async-done | bytes 786464 | tf_op jit(solution)/shard_map/all_to_all | solution.py:351
  103.6 0.8 constant_dynamic-slice_fusion
  104.4 3.3 %collective-permute-start.7 = (bf16[2,8,3,32,128]{4,3,2,1,0:T(8,128)(2,1)}, bf16[2,8,3,32,128]{4,3,2,1,0:T(8,128)(2,1)S(1)}, u32[]{:S(2)}, u32[]{:S(2)}) collective-permute-start(bf16[2,8,3,32,128]{4,3,2,1,0:T(8,128)(2,1)} %constant_dynamic-slice_fusion), channel_id=1, source_target_pairs={{0,32},{32,0},{1,33},{33,1},{2,34},{34,2},{3,35},{35,3},{4,36},{36... | collective-permute-start | bytes 1179656 | tf_op jit(solution)/shard_map/ppermute | solution.py:297
  107.7 0.1 broadcast_select_fusion.1
  107.8 0.1 pad_add_fusion.ids_ref
  107.8 0.0 collective-permute-done.10.refs_6_
  107.9 1.4 %collective-permute-done.7.zo_ref = bf16[2,8,3,32,128]{4,3,2,1,0:T(8,128)(2,1)S(1)} collective-permute-done((bf16[2,8,3,32,128]{4,3,2,1,0:T(8,128)(2,1)}, bf16[2,8,3,32,128]{4,3,2,1,0:T(8,128)(2,1)S(1)}, u32[]{:S(2)}, u32[]{:S(2)}) %collective-permute-start.7) | collective-permute-done | bytes 393248 | tf_op jit(solution)/shard_map/ppermute | solution.py:297
  109.2 1.2 copy-done.5
  110.5 1.2 copy-done.7
  111.7 10.9 %project.1 = bf16[192,4096]{1,0:T(8,128)(2,1)} custom-call(s32[4]{0:T(128)S(1)} %pad_add_fusion.ids_ref, bf16[2,16,3,32,128]{4,3,2,1,0:T(8,128)(2,1)S(1)} %bitcast.10, bf16[2,8,3,32,128]{4,3,2,1,0:T(8,128)(2,1)S(1)} %collective-permute-done.7.zo_ref, bf16[1024,4096]{1,0:T(8,128)(2,1)} %w_ref.1, bf16[256,2048]{1,0:T(8,128)(2,1)S(1)} %collective-permute-done.2.refs_0_, ...), custom_call_target="tpu_custom_call" | custom-call | tf_op jit(solution)/shard_map/project/pallas_call | solution.py:273
  (27 shorter events, 0.1 us)
Async XLA Ops:
  0.0 1.1 copy-start.8
  1.1 1.1 copy-start.9
  2.3 1.1 copy-start.10
  3.7 4.1 %collective-permute-start = (bf16[8,192,384]{2,1,0:T(8,128)(2,1)S(1)}, bf16[8,192,384]{2,1,0:T(8,128)(2,1)}, u32[]{:S(2)}, u32[]{:S(2)}) collective-permute-start(bf16[8,192,384]{2,1,0:T(8,128)(2,1)S(1)} %get-tuple-element.24), channel_id=1, source_target_pairs={{0,32},{32,0},{1,33},{33,1},{2,34},{34,2},{3,35},{35,3},{4,36},{36... | collective-permute-start | bytes 3538952 | tf_op jit(solution)/shard_map/ppermute | solution.py:297
  10.7 13.1 %copy-start.15 = (s32[31,2]{0,1:T(2,128)S(1)}, s32[31,2]{0,1:T(2,128)}, u32[]{:S(2)}) copy-start(s32[31,2]{0,1:T(2,128)} %param.12) | copy-start | bytes 748
  10.7 13.3 %copy-start.13 = (s32[48]{0:T(128)S(1)}, s32[48]{0:T(128)}, u32[]{:S(2)}) copy-start(s32[48]{0:T(128)} %param.13) | copy-start | bytes 580
  10.7 13.3 %copy-start.14 = (s32[6]{0:T(128)S(1)}, s32[6]{0:T(128)}, u32[]{:S(2)}) copy-start(s32[6]{0:T(128)} %param.11) | copy-start | bytes 76
  10.7 43.0 %all-to-all-start = ((bf16[16,192,384]{2,1,0:T(8,128)(2,1)}), bf16[16,192,384]{2,1,0:T(8,128)(2,1)S(1)}, u32[]{:S(2)}, u32[]{:S(2)}) async-start(bf16[16,192,384]{2,1,0:T(8,128)(2,1)} %maximum_select_fusion), calls=%async_computation | async-start | bytes 4718592 | tf_op jit(solution)/shard_map/all_to_all | solution.py:340
  20.0 33.7 %collective-permute-start.2 = (bf16[256,2048]{1,0:T(8,128)(2,1)}, bf16[256,2048]{1,0:T(8,128)(2,1)S(1)}, u32[]{:S(2)}, u32[]{:S(2)}) collective-permute-start(bf16[256,2048]{1,0:T(8,128)(2,1)} %dynamic_slice.6), channel_id=1, source_target_pairs={{0,65},{1,64},{64,1},{65,0},{2,67},{3,66},{66,3},{67,2},{4,69},{5,... | collective-permute-start | bytes 3145736 | tf_op jit(solution)/shard_map/ppermute | solution.py:323
  24.1 1.8 %collective-permute-start.1 = (s32[116]{0:T(128)S(1)}, s32[116]{0:T(128)S(1)}, u32[]{:S(2)}, u32[]{:S(2)}) collective-permute-start(s32[116]{0:T(128)S(1)} %pad_add_fusion.1), channel_id=1, source_target_pairs={{0,32},{32,0},{1,33},{33,1},{2,34},{34,2},{3,35},{35,3},{4,36},{36... | collective-permute-start | bytes 1400 | tf_op jit(solution)/shard_map/ppermute | solution.py:297
  31.3 1.1 copy-start
  32.4 0.9 copy-start.11
  53.7 4.7 %copy-start.1 = (bf16[2,3072,128]{2,1,0:T(8,128)(2,1)S(1)}, bf16[2,3072,128]{2,1,0:T(8,128)(2,1)}, u32[]{:S(2)}) copy-start(bf16[2,3072,128]{2,1,0:T(8,128)(2,1)} %copy-done) | copy-start | bytes 4718596
  53.7 4.7 %copy-start.12 = (bf16[3072,128]{1,0:T(8,128)(2,1)S(1)}, bf16[3072,128]{1,0:T(8,128)(2,1)}, u32[]{:S(2)}) copy-start(bf16[3072,128]{1,0:T(8,128)(2,1)} %copy-done.11) | copy-start | bytes 2359300
  53.8 4.6 %collective-permute-start.3 = (bf16[3072,256]{1,0:T(8,128)(2,1)S(1)}, bf16[3072,256]{1,0:T(8,128)(2,1)S(1)}, u32[]{:S(2)}, u32[]{:S(2)}) collective-permute-start(bf16[3072,256]{1,0:T(8,128)(2,1)S(1)} %slice.3), channel_id=1, source_target_pairs={{0,32},{32,0},{1,33},{33,1},{2,34},{34,2},{3,35},{35,3},{4,36},{36... | collective-permute-start | bytes 4718600 | tf_op jit(solution)/shard_map/ppermute | solution.py:297
  55.4 17.7 %collective-permute-start.4 = (bf16[256,2048]{1,0:T(8,128)(2,1)S(1)}, bf16[256,2048]{1,0:T(8,128)(2,1)S(1)}, u32[]{:S(2)}, u32[]{:S(2)}) collective-permute-start(bf16[256,2048]{1,0:T(8,128)(2,1)S(1)} %collective-permute-done.2.refs_0_), channel_id=1, source_target_pairs={{0,6},{32,56},{2,0},{34,58},{4,2},{36,60},{6,4},{38,62},{8,14},{40... | collective-permute-start | bytes 3145736 | tf_op jit(solution)/shard_map/ppermute | solution.py:312
  56.7 16.4 %collective-permute-start.5 = (bf16[256,2048]{1,0:T(8,128)(2,1)S(1)}, bf16[256,2048]{1,0:T(8,128)(2,1)S(1)}, u32[]{:S(2)}, u32[]{:S(2)}) collective-permute-start(bf16[256,2048]{1,0:T(8,128)(2,1)S(1)} %collective-permute-done.2.refs_0_), channel_id=1, source_target_pairs={{0,4},{32,48},{2,6},{34,50},{4,0},{36,52},{6,2},{38,54},{8,12},{40... | collective-permute-start | bytes 3145736 | tf_op jit(solution)/shard_map/ppermute | solution.py:312
  57.0 26.1 %collective-permute-start.6 = (bf16[256,2048]{1,0:T(8,128)(2,1)S(1)}, bf16[256,2048]{1,0:T(8,128)(2,1)S(1)}, u32[]{:S(2)}, u32[]{:S(2)}) collective-permute-start(bf16[256,2048]{1,0:T(8,128)(2,1)S(1)} %collective-permute-done.2.refs_0_), channel_id=1, source_target_pairs={{0,2},{32,40},{2,4},{34,42},{4,6},{36,44},{6,0},{38,46},{8,10},{40... | collective-permute-start | bytes 3145736 | tf_op jit(solution)/shard_map/ppermute | solution.py:312
  73.1 10.0 %copy-start.2 = (bf16[256,2048]{1,0:T(8,128)(2,1)}, bf16[256,2048]{1,0:T(8,128)(2,1)S(1)}, u32[]{:S(2)}) copy-start(bf16[256,2048]{1,0:T(8,128)(2,1)S(1)} %collective-permute-done.4.refs_1_) | copy-start | bytes 3145732
  73.1 10.0 %copy-start.4 = (bf16[256,2048]{1,0:T(8,128)(2,1)}, bf16[256,2048]{1,0:T(8,128)(2,1)S(1)}, u32[]{:S(2)}) copy-start(bf16[256,2048]{1,0:T(8,128)(2,1)S(1)} %collective-permute-done.5.refs_2_) | copy-start | bytes 3145732
  83.1 1.0 copy-start.6
  84.0 25.2 %copy-start.3 = (bf16[256,2048]{1,0:T(8,128)(2,1)S(1)}, bf16[256,2048]{1,0:T(8,128)(2,1)}, u32[]{:S(2)}) copy-start(bf16[256,2048]{1,0:T(8,128)(2,1)} %copy-done.2) | copy-start | bytes 3145732
  84.1 19.6 %all-to-all-start.1 = ((bf16[32,3,32,128]{3,2,1,0:T(8,128)(2,1)}), bf16[32,3,32,128]{3,2,1,0:T(8,128)(2,1)S(1)}, u32[]{:S(2)}, u32[]{:S(2)}) async-start(bf16[32,3,32,128]{3,2,1,0:T(8,128)(2,1)} %bitcast.5), calls=%async_computation.1 | async-start | bytes 1572864 | tf_op jit(solution)/shard_map/all_to_all | solution.py:351
  90.5 17.4 %collective-permute-start.10 = (bf16[256,2048]{1,0:T(8,128)(2,1)}, bf16[256,2048]{1,0:T(8,128)(2,1)}, u32[]{:S(2)}, u32[]{:S(2)}) collective-permute-start(bf16[256,2048]{1,0:T(8,128)(2,1)} %copy-done.4), channel_id=1, source_target_pairs={{0,32},{32,0},{1,33},{33,1},{2,34},{34,2},{3,35},{35,3},{4,36},{36... | collective-permute-start | bytes 3145736 | tf_op jit(solution)/shard_map/ppermute | solution.py:297
  92.5 15.4 %collective-permute-start.11 = (bf16[256,2048]{1,0:T(8,128)(2,1)}, bf16[256,2048]{1,0:T(8,128)(2,1)}, u32[]{:S(2)}, u32[]{:S(2)}) collective-permute-start(bf16[256,2048]{1,0:T(8,128)(2,1)} %copy-done.6), channel_id=1, source_target_pairs={{0,32},{32,0},{1,33},{33,1},{2,34},{34,2},{3,35},{35,3},{4,36},{36... | collective-permute-start | bytes 3145736 | tf_op jit(solution)/shard_map/ppermute | solution.py:297
  92.6 15.3 %collective-permute-start.8 = (bf16[256,2048]{1,0:T(8,128)(2,1)S(1)}, bf16[256,2048]{1,0:T(8,128)(2,1)}, u32[]{:S(2)}, u32[]{:S(2)}) collective-permute-start(bf16[256,2048]{1,0:T(8,128)(2,1)S(1)} %collective-permute-done.2.refs_0_), channel_id=1, source_target_pairs={{0,32},{32,0},{1,33},{33,1},{2,34},{34,2},{3,35},{35,3},{4,36},{36... | collective-permute-start | bytes 3145736 | tf_op jit(solution)/shard_map/ppermute | solution.py:297
  93.0 14.9 %collective-permute-start.9 = (bf16[256,2048]{1,0:T(8,128)(2,1)}, bf16[256,2048]{1,0:T(8,128)(2,1)}, u32[]{:S(2)}, u32[]{:S(2)}) collective-permute-start(bf16[256,2048]{1,0:T(8,128)(2,1)} %copy-done.2), channel_id=1, source_target_pairs={{0,32},{32,0},{1,33},{33,1},{2,34},{34,2},{3,35},{35,3},{4,36},{36... | collective-permute-start | bytes 3145736 | tf_op jit(solution)/shard_map/ppermute | solution.py:297
  104.4 4.8 %collective-permute-start.7 = (bf16[2,8,3,32,128]{4,3,2,1,0:T(8,128)(2,1)}, bf16[2,8,3,32,128]{4,3,2,1,0:T(8,128)(2,1)S(1)}, u32[]{:S(2)}, u32[]{:S(2)}) collective-permute-start(bf16[2,8,3,32,128]{4,3,2,1,0:T(8,128)(2,1)} %constant_dynamic-slice_fusion), channel_id=1, source_target_pairs={{0,32},{32,0},{1,33},{33,1},{2,34},{34,2},{3,35},{35,3},{4,36},{36... | collective-permute-start | bytes 1179656 | tf_op jit(solution)/shard_map/ppermute | solution.py:297
  109.2 1.2 copy-start.5
  110.5 1.2 copy-start.7

commit v3 on v2

--- a/solution.py
+++ b/solution.py
@@ -29,30 +29,62 @@
 F32 = jnp.float32
 
 
-def pack_kernel(core_ref, q_ref, k_ref, v_ref, own_ref, send_ref):
+def pack_kernel(core_ref, q_hbm, k_hbm, v_hbm, own_ref, send_ref, buf, sems):
     core = core_ref[0]
-    for out_ref, parity in ((own_ref, core), (send_ref, 1 - core)):
-        for a, ref in enumerate((q_ref, k_ref, v_ref)):
-            for group in range(2 * CHIP_BLOCKS):
-                start = pl.multiple_of(group * HALF + parity * QTR, QTR)
-                rows = ref[pl.ds(start, QTR), :]
-                for h in range(HEADS):
-                    out_ref[h, group * QTR : (group + 1) * QTR, a * HD : (a + 1) * HD] = rows[
-                        :, h * HD : (h + 1) * HD
-                    ]
+    copies = []
+    for block in range(CHIP_BLOCKS):
+        rows = slice(block * QB, (block + 1) * QB)
+        for a, ref in enumerate((q_hbm, k_hbm, v_hbm)):
+            copy = pltpu.make_async_copy(ref.at[rows], buf.at[a, rows], sems.at[block, a])
+            copy.start()
+            copies.append(copy)
+    for block in range(CHIP_BLOCKS):
+        for a in range(3):
+            copies[block * 3 + a].wait()
+            for out_ref, parity in ((own_ref, core), (send_ref, 1 - core)):
+                for group in (2 * block, 2 * block + 1):
+                    start = pl.multiple_of(group * HALF + parity * QTR, QTR)
+                    rows = buf[a, pl.ds(start, QTR), :]
+                    for h in range(HEADS):
+                        out_ref[
+                            h, group * QTR : (group + 1) * QTR, a * HD : (a + 1) * HD
+                        ] = rows[:, h * HD : (h + 1) * HD]
 
 
 def pack(core, q, k, v):
     out = jax.ShapeDtypeStruct((HEADS, CHIP_BLOCKS * HALF, 3 * HD), BF)
     vmem = pl.BlockSpec(memory_space=pltpu.VMEM)
+    hbm = pl.BlockSpec(memory_space=pltpu.HBM)
     return pl.pallas_call(
         pack_kernel,
         out_shape=(out, out),
-        in_specs=[pl.BlockSpec(memory_space=pltpu.SMEM), vmem, vmem, vmem],
+        in_specs=[pl.BlockSpec(memory_space=pltpu.SMEM), hbm, hbm, hbm],
         out_specs=(vmem, vmem),
-        compiler_params=pltpu.CompilerParams(vmem_limit_bytes=32 << 20),
+        scratch_shapes=[
+            pltpu.VMEM((3,) + q.shape, BF),
+            pltpu.SemaphoreType.DMA((CHIP_BLOCKS, 3)),
+        ],
+        compiler_params=pltpu.CompilerParams(vmem_limit_bytes=12 << 20),
         name="pack",
     )(core, q, k, v)
+
+
+def merge_kernel(core_ref, own_ref, recv_ref, o_ref):
+    core = core_ref[0]
+    o_ref[pl.ds(core * HEADS, HEADS)] = own_ref[...]
+    o_ref[pl.ds((1 - core) * HEADS, HEADS)] = recv_ref[...]
+
+
+def merge(core, own, recv):
+    vmem = pl.BlockSpec(memory_space=pltpu.VMEM)
+    return pl.pallas_call(
+        merge_kernel,
+        out_shape=jax.ShapeDtypeStruct((2 * HEADS,) + own.shape[1:], BF),
+        in_specs=[pl.BlockSpec(memory_space=pltpu.SMEM), vmem, vmem],
+        out_specs=vmem,
+        compiler_params=pltpu.CompilerParams(vmem_limit_bytes=12 << 20),
+        name="merge",
+    )(core, own, recv)
 
 
 def prepare_kernel(ints_ref, kdoc_ref, qdoc_ref, hi_ref, meta_ref):
@@ -128,7 +160,7 @@
         ),
         in_specs=[smem],
         out_specs=(vmem, vmem, vmem, smem),
-        compiler_params=pltpu.CompilerParams(vmem_limit_bytes=32 << 20),
+        compiler_params=pltpu.CompilerParams(vmem_limit_bytes=12 << 20),
         name="prepare",
     )(ints)
 
@@ -207,87 +239,128 @@
         out_shape=jax.ShapeDtypeStruct((2, NCTX, 3, QTR, HD), BF),
         in_specs=[smem, smem] + [vmem] * 5,
         out_specs=vmem,
-        compiler_params=pltpu.CompilerParams(vmem_limit_bytes=40 << 20),
+        compiler_params=pltpu.CompilerParams(vmem_limit_bytes=14 << 20),
         name="attend",
     )(core, meta, y, kvo, kdoc, qdoc, hi)
 
 
-COLS = 512
+SHARED = 1536
+LOADS = 8
+DIRECT = (256, 256)
 CTX = ("y", "x")
 NLINE = 4
-CHUNKS = 1
-PIECE = HEADS * HD // NLINE // CHUNKS
+PIECE = HEADS * HD // NLINE
 PHEADS = PIECE // HD
 
 
 def project_kernel(ids_ref, z_ref, zo_ref, w_ref, *refs):
-    count = (len(refs) - 3) // 2
-    weights, (o_ref, a_ref, b_ref) = (refs[:count], refs[count : 2 * count]), refs[2 * count :]
+    count = NLINE + len(DIRECT)
+    sides = (refs[:count], refs[count : 2 * count])
+    o_ref, a_ref, b_ref = refs[2 * count : 2 * count + 3]
+    bufs, (acc_ref, w_buf, sems) = refs[2 * count + 3 : -3], refs[-3:]
     core, t_own = ids_ref[0], ids_ref[1]
-    step = pl.program_id(0)
-
-    @pl.when(step == 0)
-    def _():
-        def head(ref, at, src, h):
-            col = slice(at * HD, (at + 1) * HD)
-            for g in range(3):
-                row = pl.multiple_of(g * HALF + core * QTR, QTR)
-                ref[pl.ds(row, QTR), col] = z_ref[src, core * HEADS + h, g]
-                row = pl.multiple_of(g * HALF + (1 - core) * QTR, QTR)
-                ref[pl.ds(row, QTR), col] = zo_ref[src, h, g]
-
-        for h in range(HEADS):
-            head(a_ref, h, t_own, h)
-        for half in range(2):
-            for n in range(CHUNKS * NLINE):
-                piece = (n & -NLINE) + ((ids_ref[2 + half] + n) & (NLINE - 1))
-                for h in range(PHEADS):
-                    head(b_ref.at[half], n * PHEADS + h, 1 - t_own, piece * PHEADS + h)
-
-    own = HEADS * HD
-
-    def run(half):
-        acc = jnp.dot(a_ref[:, :own], w_ref[...], preferred_element_type=F32)
-        at = 0
-        for ref in weights[half]:
-            depth = ref.shape[0]
-            acc += jnp.dot(
-                b_ref[half, :, at : at + depth], ref[...], preferred_element_type=F32
-            )
-            at += depth
-        o_ref[...] = acc.astype(BF)
-
-    steps = pl.num_programs(0) // 2
-    pl.when(step < steps)(functools.partial(run, 0))
-    pl.when(step >= steps)(functools.partial(run, 1))
+    half = w_ref.shape[1] // 2
+
+    loads = []
+    rows = w_ref.shape[0] // LOADS
+    for n in range(LOADS):
+        part = slice(n * rows, (n + 1) * rows)
+        loads.append(pltpu.make_async_copy(w_ref.at[part], w_buf.at[part], sems.at[2, n]))
+        loads[-1].start()
+
+    steps = []
+    for side in range(2):
+        first = (core if side == 0 else 1 - core) * half
+        start = 0
+        for n, width in enumerate((SHARED,) + DIRECT):
+            column = pl.ds(pl.multiple_of(first + start, HD), width)
+            steps.append((side, n, column, slice(side * half + start, side * half + start + width)))
+            start += width
+
+    def head(ref, at, src, h):
+        col = slice(at * HD, (at + 1) * HD)
+        for g in range(3):
+            row = pl.multiple_of(g * HALF + core * QTR, QTR)
+            ref[pl.ds(row, QTR), col] = z_ref[src, core * HEADS + h, g]
+            row = pl.multiple_of(g * HALF + (1 - core) * QTR, QTR)
+            ref[pl.ds(row, QTR), col] = zo_ref[src, h, g]
+
+    for h in range(HEADS):
+        head(a_ref, h, t_own, h)
+        head(b_ref.at[2], h, 1 - t_own, h)
+    for side in range(2):
+        for n in range(NLINE):
+            piece = (ids_ref[2 + side] + n) & (NLINE - 1)
+            for h in range(PHEADS):
+                head(b_ref.at[side], n * PHEADS + h, 1 - t_own, piece * PHEADS + h)
+
+    for side, n, _, place in steps:
+        if n == 0:
+            acc = 0.0
+            for m in range(NLINE):
+                acc += jnp.dot(
+                    b_ref[side, :, m * PIECE : (m + 1) * PIECE],
+                    sides[side][m][...],
+                    preferred_element_type=F32,
+                )
+        else:
+            acc = jnp.dot(b_ref[2], sides[side][NLINE + n - 1][...], preferred_element_type=F32)
+        acc_ref[:, place] = acc
+    for copy in loads:
+        copy.wait()
+    stores = []
+    for side, n, column, place in steps:
+        acc = acc_ref[:, place] + jnp.dot(
+            a_ref[...], w_buf[:, column], preferred_element_type=F32
+        )
+        buf = bufs[n].at[side]
+        buf[...] = acc.astype(BF)
+        store = pltpu.make_async_copy(buf, o_ref.at[:, column], sems.at[side, n])
+        store.start()
+        stores.append(store)
+    for store in stores:
+        store.wait()
 
 
 def project(ids, z, zo, w, mine, other):
     width = w.shape[1]
+    depth = HEADS * HD
     rows = 3 * HALF
-    steps = width // COLS // 2
-    whole = lambda x: pl.BlockSpec(x.shape, lambda n, ids: (0,) * x.ndim)
-    column = lambda n, ids: (0, (n + ids[0] * steps) & (2 * steps - 1))
-    first = lambda n, ids: (0, jnp.minimum(n, steps - 1))
-    second = lambda n, ids: (0, jnp.maximum(n - steps, 0))
+    parts = mine + other
+    widths = (SHARED,) + DIRECT
+    vmem = pl.BlockSpec(memory_space=pltpu.VMEM)
+    hbm = pl.BlockSpec(memory_space=pltpu.HBM)
     return pl.pallas_call(
         project_kernel,
-        grid_spec=pltpu.PrefetchScalarGridSpec(
-            num_scalar_prefetch=1,
-            grid=(2 * steps,),
-            in_specs=[whole(z), whole(zo), pl.BlockSpec((HEADS * HD, COLS), column)]
-            + [pl.BlockSpec((m.shape[0], COLS), first) for m in mine]
-            + [pl.BlockSpec((m.shape[0], COLS), second) for m in other],
-            out_specs=pl.BlockSpec((rows, COLS), column),
-            scratch_shapes=[
-                pltpu.VMEM((rows, HEADS * HD), BF),
-                pltpu.VMEM((2, rows, HEADS * HD), BF),
-            ],
-        ),
+        in_specs=[pl.BlockSpec(memory_space=pltpu.SMEM), vmem, vmem, hbm] + [vmem] * len(parts),
+        out_specs=hbm,
         out_shape=jax.ShapeDtypeStruct((rows, width), BF),
-        compiler_params=pltpu.CompilerParams(vmem_limit_bytes=48 << 20),
+        scratch_shapes=[pltpu.VMEM((rows, depth), BF), pltpu.VMEM((3, rows, depth), BF)]
+        + [pltpu.VMEM((2, rows, n), BF) for n in widths]
+        + [
+            pltpu.VMEM((rows, width), F32),
+            pltpu.VMEM((depth, width), BF),
+            pltpu.SemaphoreType.DMA((3, LOADS)),
+        ],
+        compiler_params=pltpu.CompilerParams(vmem_limit_bytes=24 << 20),
         name="project",
-    )(ids, z, zo, w, *mine, *other)
+    )(ids, z, zo, w, *parts)
+
+
+def pick_kernel(core_ref, z_ref, o_ref):
+    o_ref[...] = z_ref[:, pl.ds((1 - core_ref[0]) * HEADS, HEADS)]
+
+
+def pick(core, z):
+    vmem = pl.BlockSpec(memory_space=pltpu.VMEM)
+    return pl.pallas_call(
+        pick_kernel,
+        out_shape=jax.ShapeDtypeStruct((2, HEADS) + z.shape[2:], BF),
+        in_specs=[pl.BlockSpec(memory_space=pltpu.SMEM), vmem],
+        out_specs=vmem,
+        compiler_params=pltpu.CompilerParams(vmem_limit_bytes=4 << 20),
+        name="pick",
+    )(core, z)
 
 
 SWAP = [(0, 1), (1, 0)]
@@ -295,6 +368,10 @@
 
 def swap(x):
     return lax.ppermute(x, "core", SWAP)
+
+
+def in_vmem(x):
+    return pltpu.with_memory_space_constraint(x, pltpu.VMEM)
 
 
 def after(values, *others):
@@ -323,38 +400,40 @@
     from_z = lambda x: lax.ppermute(x, ("z_lo", "tensor"), across)
     half = w.shape[1] // 2
     line = jnp.where(core == 0, x_at, y_at)
-    fetched = [
-        from_z(lax.dynamic_slice(w, (PIECE * (c * NLINE + line), core * half), (PIECE, half)))
-        for c in range(CHUNKS)
-    ]
+    piece = from_z(lax.dynamic_slice(w, (PIECE * line, core * half), (PIECE, SHARED)))
+    direct, at = [], core * half + SHARED
+    for width in DIRECT:
+        direct.append(lax.dynamic_slice(w, (0, at), (w.shape[0], width)))
+        at += width
+    first = from_z(after(direct[0], piece))
 
     ints = jnp.concatenate([doc_lengths, spans.reshape(-1), assignment])
     ints = jnp.where(chip // HEADS == core, ints, swap(ints))
     ints = jnp.concatenate([core[None], ints])
 
+    q, k, v = (pltpu.with_memory_space_constraint(x, pltpu.HBM) for x in (q, k, v))
     own, send = pack(core[None], q, k, v)
     recv = swap(send)
-    x = jnp.where(
-        core == 0, jnp.concatenate([own, recv], axis=0), jnp.concatenate([recv, own], axis=0)
-    )
+    x = merge(core[None], own, recv)
     y = lax.all_to_all(x, CTX, 0, 0, tiled=True).reshape(ROWS, 3 * HD)
     kdoc, qdoc, hi, meta = prepare(ints)
     y, kdoc, qdoc, hi, meta = lax.optimization_barrier((y, kdoc, qdoc, hi, meta))
-    y, fetched = lax.optimization_barrier((y, fetched))
+    y, piece, first = lax.optimization_barrier((y, piece, first))
+    second = from_z(after(direct[1], first))
     kvo = swap(y[:, HD:])
 
-    pieces = [[piece] + [along_line(piece, step) for step in (1, 2, 3)] for piece in fetched]
+    pieces = [piece] + [along_line(piece, step) for step in (1, 2, 3)]
     att = attend(core[None], meta, y, kvo, kdoc, qdoc, hi)
-    att, pieces = lax.optimization_barrier((att, pieces))
-    mine = sum(pieces, [])
+    att, mine = lax.optimization_barrier((att, pieces + [first, second]))
     other = [swap(p) for p in mine]
     z = lax.all_to_all(
         att.reshape(2 * NCTX, 3, QTR, HD), ("tensor",) + CTX, 0, 0, tiled=True
     ).reshape(2, 2 * HEADS, 3, QTR, HD)
-    zo = swap(lax.dynamic_slice_in_dim(z, (1 - core) * HEADS, HEADS, 1))
+    zo = swap(pick(core[None], z))
     lines = jnp.where(core == 0, jnp.stack([x_at, y_at]), jnp.stack([y_at, x_at]))
     ids = jnp.concatenate([jnp.stack([core, t_own]), lines])
-    return project(ids, z, zo, w, mine, other)
+    mine, other = ([in_vmem(p) for p in side] for side in (mine, other))
+    return project(ids, z, zo, pltpu.with_memory_space_constraint(w, pltpu.HBM), mine, other)
 
 
 def solution(mesh):

time: 123 us -> 112 us (0.911)
  waiting for transfers between devices: 46.9 us -> 36.3 us
  starting transfers between devices: 28.9 us -> 33.3 us
  other arithmetic: 3.24 us -> 0.38 us
  local copies, waits for them, and re-layouts: 12.3 us -> 9.95 us
    all_to_all x1, waiting for transfers between devices: 20.4 us -> 0.01 us  [shards(): y = lax.all_to_all(x, CTX, 0, 0, tiled=True).reshape(ROWS, 3 * HD)]
    ppermute x1 -> x3, waiting for transfers between devices: 0.01 us -> 16.2 us  [shards(): from_z = lambda x: lax.ppermute(x, ('z_lo', 'tensor'), across)]
    ppermute x3, waiting for transfers between devices: 9.99 us -> 3.02 us  [along_line(): return lax.ppermute(x, ('core',) + CTX, pairs)]
    ppermute x1 -> x3, starting transfers between devices: 3.76 us -> 8.46 us  [shards(): from_z = lambda x: lax.ppermute(x, ('z_lo', 'tensor'), across)]
    unnamed x33 -> x27, local copies, waits for them, and re-layouts: 8.96 us -> 5.42 us
    select_n x1 -> x0, other arithmetic: 2.86 us -> none  [shards(): jnp.where(core == 0, jnp.concatenate([own, recv], axis=0), jnp.concatenat...]
    all_to_all x1, waiting for transfers between devices: 10.5 us -> 12.7 us  [shards(): lax.all_to_all(att.reshape(2 * NCTX, 3, QTR, HD), ('tensor',) + CTX, 0, 0...]
    all_to_all x1, starting transfers between devices: 6.42 us -> 4.78 us  [shards(): lax.all_to_all(att.reshape(2 * NCTX, 3, QTR, HD), ('tensor',) + CTX, 0, 0...]
  transfers between devices with their start and end apart: 14 -> 18, of which waited for: 7 -> 7; matrix products, arithmetic and copies ran while one was open for 3% -> 4% of each run, Pallas kernels for 16% -> 18%
where the time goes in v3:
time: 112 us
  waiting for transfers between devices  36.3 us (32%)
  starting transfers between devices  33.3 us (30%)
  Pallas kernels  31.5 us (28%)
  local copies, waits for them, and re-layouts  9.95 us (9%)
    ppermute x3, waiting for transfers between devices, shards(): from_z = lambda x: lax.ppermute(x, ('z_lo', 'tensor'), across)  16.2 us
    pallas_call x1, Pallas kernels, attend(): pl.pallas_call(attend_kernel, out_shape=jax.ShapeDtypeStruct((2, NCTX, 3,...  14.6 us
    all_to_all x1, waiting for transfers between devices, shards(): lax.all_to_all(att.reshape(2 * NCTX, 3, QTR, HD), ('tensor',) + CTX, 0, 0...  12.7 us
    ppermute x10, starting transfers between devices, swap(): return lax.ppermute(x, 'core', SWAP)  9.87 us
    pallas_call x1, Pallas kernels, project(): pl.pallas_call(project_kernel, in_specs=[pl.BlockSpec(memory_space=pltpu....  9.67 us
    ppermute x3, starting transfers between devices, shards(): from_z = lambda x: lax.ppermute(x, ('z_lo', 'tensor'), across)  8.46 us
    all_to_all x1, starting transfers between devices, shards(): y = lax.all_to_all(x, CTX, 0, 0, tiled=True).reshape(ROWS, 3 * HD)  6.84 us
    unnamed x27, local copies, waits for them, and re-layouts  5.42 us
  transfers between devices with their start and end apart: 18, of which 7 were waited for; matrix products, arithmetic and copies ran while one was open for 4% of the time, Pallas kernels for 18%

profile of v3, /device:TPU:1, one launch (start us, length us, event | category | flops | bytes accessed | tf_op | source)
XLA Modules:
  0.0 111.9 jit_solution(14429487353719329779)
XLA Ops:
  0.0 1.7 %pack.1 = (bf16[8,192,384]{2,1,0:T(8,128)(2,1)S(1)}, bf16[8,192,384]{2,1,0:T(8,128)(2,1)S(1)}) custom-call(s32[1]{0:T(128)} %bitcast.core_ref, bf16[384,1024]{1,0:T(8,128)(2,1)} %q_hbm.1, bf16[384,1024]{1,0:T(8,128)(2,1)} %k_hbm.1, bf16[384,1024]{1,0:T(8,128)(2,1)} %v_hbm.1), custom_call_target="tpu_custom_call" | custom-call | tf_op jit(solution)/shard_map/pack/pallas_call | solution.py:58
  1.7 1.5 %collective-permute-start = (bf16[8,192,384]{2,1,0:T(8,128)(2,1)S(1)}, bf16[8,192,384]{2,1,0:T(8,128)(2,1)S(1)}, u32[]{:S(2)}, u32[]{:S(2)}) collective-permute-start(bf16[8,192,384]{2,1,0:T(8,128)(2,1)S(1)} %get-tuple-element.29), channel_id=1, source_target_pairs={{0,32},{32,0},{1,33},{33,1},{2,34},{34,2},{3,35},{35,3},{4,36},{36... | collective-permute-start | bytes 3538952 | tf_op jit(solution)/shard_map/ppermute | solution.py:370
  3.2 2.5 %collective-permute-done.recv_ref = bf16[8,192,384]{2,1,0:T(8,128)(2,1)S(1)} collective-permute-done((bf16[8,192,384]{2,1,0:T(8,128)(2,1)S(1)}, bf16[8,192,384]{2,1,0:T(8,128)(2,1)S(1)}, u32[]{:S(2)}, u32[]{:S(2)}) %collective-permute-start) | collective-permute-done | bytes 1179680 | tf_op jit(solution)/shard_map/ppermute | solution.py:370
  5.7 0.2 merge.1
  5.9 1.4 %copy-done = bf16[16,192,384]{2,1,0:T(8,128)(2,1)} copy-done((bf16[16,192,384]{2,1,0:T(8,128)(2,1)}, bf16[16,192,384]{2,1,0:T(8,128)(2,1)S(1)}, u32[]{:S(2)}) %copy-start) | copy-done | bytes 2359320
  7.3 6.8 %all-to-all-start = ((bf16[16,192,384]{2,1,0:T(8,128)(2,1)}), bf16[16,192,384]{2,1,0:T(8,128)(2,1)S(1)}, u32[]{:S(2)}, u32[]{:S(2)}) async-start(bf16[16,192,384]{2,1,0:T(8,128)(2,1)} %copy-done), calls=%async_computation | async-start | bytes 4718592 | tf_op jit(solution)/shard_map/all_to_all | solution.py:418
  14.2 0.0 copy-start.12
  14.2 0.0 copy-start.10
  14.2 0.0 copy-start.11
  14.2 2.1 %dynamic_slice.9 = bf16[256,1536]{1,0:T(8,128)(2,1)} dynamic-slice(bf16[1024,4096]{1,0:T(8,128)(2,1)} %w_ref.1, s32[]{:T(128)S(6)} %select_n.42, s32[]{:T(128)S(6)} %select_n.43), dynamic_slice_sizes={256,1536} | dynamic-slice | bytes 1572868 | tf_op jit(solution)/shard_map/dynamic_slice | solution.py:403
  16.3 3.8 %collective-permute-start.2 = (bf16[256,1536]{1,0:T(8,128)(2,1)}, bf16[256,1536]{1,0:T(8,128)(2,1)S(1)}, u32[]{:S(2)}, u32[]{:S(2)}) collective-permute-start(bf16[256,1536]{1,0:T(8,128)(2,1)} %dynamic_slice.9), channel_id=1, source_target_pairs={{0,65},{1,64},{64,1},{65,0},{2,67},{3,66},{66,3},{67,2},{4,69},{5,... | collective-permute-start | bytes 2359304 | tf_op jit(solution)/shard_map/ppermute | solution.py:400
  20.0 2.3 %constant_dynamic-slice_fusion = (bf16[1024,256]{1,0:T(8,128)(2,1)}, bf16[1024,256]{1,0:T(8,128)(2,1)}) fusion(bf16[1024,4096]{1,0:T(8,128)(2,1)} %w_ref.1, s32[]{:T(128)S(6)} %select_n.45, s32[]{:T(128)S(6)} %select_n.44), kind=kLoop, calls=%fused_computation.5 | loop fusion | bytes 2097160 | tf_op jit(solution)/shard_map/dynamic_slice | solution.py:406
  22.3 15.2 %collective-permute-done.2.refs_0_ = bf16[256,1536]{1,0:T(8,128)(2,1)S(1)} collective-permute-done((bf16[256,1536]{1,0:T(8,128)(2,1)}, bf16[256,1536]{1,0:T(8,128)(2,1)S(1)}, u32[]{:S(2)}, u32[]{:S(2)}) %collective-permute-start.2) | collective-permute-done | bytes 786464 | tf_op jit(solution)/shard_map/ppermute | solution.py:400
  37.5 2.4 %collective-permute-start.3 = (bf16[1024,256]{1,0:T(8,128)(2,1)}, bf16[1024,256]{1,0:T(8,128)(2,1)}, u32[]{:S(2)}, u32[]{:S(2)}) collective-permute-start(bf16[1024,256]{1,0:T(8,128)(2,1)} %get-tuple-element.36), channel_id=1, source_target_pairs={{0,65},{1,64},{64,1},{65,0},{2,67},{3,66},{66,3},{67,2},{4,69},{5,... | collective-permute-start | bytes 1572872 | tf_op jit(solution)/shard_map/ppermute | solution.py:400
  39.9 0.1 copy.9
  40.0 0.1 reshape.13
  40.1 0.1 pad_add_fusion.1
  40.2 1.8 %collective-permute-start.1 = (s32[116]{0:T(128)S(1)}, s32[116]{0:T(128)S(1)}, u32[]{:S(2)}, u32[]{:S(2)}) collective-permute-start(s32[116]{0:T(128)S(1)} %pad_add_fusion.1), channel_id=1, source_target_pairs={{0,32},{32,0},{1,33},{33,1},{2,34},{34,2},{3,35},{35,3},{4,36},{36... | collective-permute-start | bytes 1400 | tf_op jit(solution)/shard_map/ppermute | solution.py:370
  42.0 0.8 collective-permute-done.1
  42.8 0.1 broadcast_select_fusion
  42.9 0.1 pad_add_fusion.2.ints_ref
  43.0 5.3 %prepare.1 = (bf16[2,3072,128]{2,1,0:T(8,128)(2,1)S(1)}, bf16[3072,128]{1,0:T(8,128)(2,1)S(1)}, s32[12,8,256]{2,1,0:T(8,128)S(1)}, s32[60]{0:T(128)S(1)}) custom-call(s32[117]{0:T(128)S(1)} %pad_add_fusion.2.ints_ref), custom_call_target="tpu_custom_call" | custom-call | tf_op jit(solution)/shard_map/prepare/pallas_call | solution.py:153
  48.3 1.1 %copy-done.1 = bf16[2,3072,128]{2,1,0:T(8,128)(2,1)} copy-done((bf16[2,3072,128]{2,1,0:T(8,128)(2,1)}, bf16[2,3072,128]{2,1,0:T(8,128)(2,1)S(1)}, u32[]{:S(2)}) %copy-start.1) | copy-done | bytes 1572888
  49.4 0.9 copy-done.5
  50.3 0.9 collective-permute-done.3.refs_4_
  51.3 0.1 slice.3
  51.4 2.2 %collective-permute-start.4 = (bf16[3072,256]{1,0:T(8,128)(2,1)S(1)}, bf16[3072,256]{1,0:T(8,128)(2,1)S(1)}, u32[]{:S(2)}, u32[]{:S(2)}) collective-permute-start(bf16[3072,256]{1,0:T(8,128)(2,1)S(1)} %slice.3), channel_id=1, source_target_pairs={{0,32},{32,0},{1,33},{33,1},{2,34},{34,2},{3,35},{35,3},{4,36},{36... | collective-permute-start | bytes 4718600 | tf_op jit(solution)/shard_map/ppermute | solution.py:370
  53.6 2.2 %collective-permute-start.5 = (bf16[256,1536]{1,0:T(8,128)(2,1)S(1)}, bf16[256,1536]{1,0:T(8,128)(2,1)S(1)}, u32[]{:S(2)}, u32[]{:S(2)}) collective-permute-start(bf16[256,1536]{1,0:T(8,128)(2,1)S(1)} %collective-permute-done.2.refs_0_), channel_id=1, source_target_pairs={{0,6},{32,56},{2,0},{34,58},{4,2},{36,60},{6,4},{38,62},{8,14},{40... | collective-permute-start | bytes 2359304 | tf_op jit(solution)/shard_map/ppermute | solution.py:389
  55.8 0.6 collective-permute-start.6
  56.4 0.6 collective-permute-start.7
  57.0 2.4 %collective-permute-start.8 = (bf16[1024,256]{1,0:T(8,128)(2,1)S(1)}, bf16[1024,256]{1,0:T(8,128)(2,1)}, u32[]{:S(2)}, u32[]{:S(2)}) collective-permute-start(bf16[1024,256]{1,0:T(8,128)(2,1)S(1)} %copy-done.9), channel_id=1, source_target_pairs={{0,65},{1,64},{64,1},{65,0},{2,67},{3,66},{66,3},{67,2},{4,69},{5,... | collective-permute-start | bytes 1572872 | tf_op jit(solution)/shard_map/ppermute | solution.py:400
  59.3 14.6 %attend.1 = bf16[2,16,3,32,128]{4,3,2,1,0:T(8,128)(2,1)} custom-call(s32[1]{0:T(128)} %bitcast.core_ref, s32[60]{0:T(128)S(1)} %get-tuple-element.34.meta_ref, bf16[3072,384]{1,0:T(8,128)(2,1)S(1)} %bitcast.8, bf16[3072,256]{1,0:T(8,128)(2,1)S(1)} %collective-permute-done.4.kvo_ref, bf16[2,3072,128]{2,1,0:T(8,128)(2,1)S(1)} %copy-done.2, ...), custom_call_target="tpu_custom_call" | custom-call | tf_op jit(solution)/shard_map/attend/pallas_call | solution.py:237
  74.0 3.0 %collective-permute-done.7.refs_3_ = bf16[256,1536]{1,0:T(8,128)(2,1)} collective-permute-done((bf16[256,1536]{1,0:T(8,128)(2,1)S(1)}, bf16[256,1536]{1,0:T(8,128)(2,1)}, u32[]{:S(2)}, u32[]{:S(2)}) %collective-permute-start.7) | collective-permute-done | bytes 786464 | tf_op jit(solution)/shard_map/ppermute | solution.py:389
  77.0 1.2 %collective-permute-start.14 = (bf16[1024,256]{1,0:T(8,128)(2,1)}, bf16[1024,256]{1,0:T(8,128)(2,1)S(1)}, u32[]{:S(2)}, u32[]{:S(2)}) collective-permute-start(bf16[1024,256]{1,0:T(8,128)(2,1)} %collective-permute-done.3.refs_4_), channel_id=1, source_target_pairs={{0,32},{32,0},{1,33},{33,1},{2,34},{34,2},{3,35},{35,3},{4,36},{36... | collective-permute-start | bytes 1572872 | tf_op jit(solution)/shard_map/ppermute | solution.py:370
  78.2 4.8 %all-to-all-start.1 = ((bf16[32,3,32,128]{3,2,1,0:T(8,128)(2,1)}), bf16[32,3,32,128]{3,2,1,0:T(8,128)(2,1)S(1)}, u32[]{:S(2)}, u32[]{:S(2)}) async-start(bf16[32,3,32,128]{3,2,1,0:T(8,128)(2,1)} %bitcast.5), calls=%async_computation.1 | async-start | bytes 1572864 | tf_op jit(solution)/shard_map/all_to_all | solution.py:429
  83.0 0.4 collective-permute-start.15
  83.4 0.2 collective-permute-start.10
  83.6 0.3 collective-permute-start.11
  83.9 0.2 collective-permute-start.12
  84.1 0.8 copy-done.7
  84.9 0.3 collective-permute-start.13
  85.2 12.7 %all-to-all-done.1 = bf16[32,3,32,128]{3,2,1,0:T(8,128)(2,1)S(1)} async-done(((bf16[32,3,32,128]{3,2,1,0:T(8,128)(2,1)}), bf16[32,3,32,128]{3,2,1,0:T(8,128)(2,1)S(1)}, u32[]{:S(2)}, u32[]{:S(2)}) %all-to-all-start.1) | async-done | bytes 786464 | tf_op jit(solution)/shard_map/all_to_all | solution.py:429
  97.9 1.7 %collective-permute-start.9 = (bf16[2,8,3,32,128]{4,3,2,1,0:T(8,128)(2,1)S(1)}, bf16[2,8,3,32,128]{4,3,2,1,0:T(8,128)(2,1)S(1)}, u32[]{:S(2)}, u32[]{:S(2)}) collective-permute-start(bf16[2,8,3,32,128]{4,3,2,1,0:T(8,128)(2,1)S(1)} %pick.1), channel_id=1, source_target_pairs={{0,32},{32,0},{1,33},{33,1},{2,34},{34,2},{3,35},{35,3},{4,36},{36... | collective-permute-start | bytes 1179656 | tf_op jit(solution)/shard_map/ppermute | solution.py:370
  99.7 0.1 broadcast_select_fusion.1
  99.7 0.1 pad_add_fusion.ids_ref
  99.8 1.2 %collective-permute-done.9.zo_ref = bf16[2,8,3,32,128]{4,3,2,1,0:T(8,128)(2,1)S(1)} collective-permute-done((bf16[2,8,3,32,128]{4,3,2,1,0:T(8,128)(2,1)S(1)}, bf16[2,8,3,32,128]{4,3,2,1,0:T(8,128)(2,1)S(1)}, u32[]{:S(2)}, u32[]{:S(2)}) %collective-permute-start.9) | collective-permute-done | bytes 393248 | tf_op jit(solution)/shard_map/ppermute | solution.py:370
  101.0 1.0 copy-done.8
  102.0 9.7 %project.1 = bf16[192,4096]{1,0:T(8,128)(2,1)} custom-call(s32[4]{0:T(128)S(1)} %pad_add_fusion.ids_ref, bf16[2,16,3,32,128]{4,3,2,1,0:T(8,128)(2,1)S(1)} %bitcast.10, bf16[2,8,3,32,128]{4,3,2,1,0:T(8,128)(2,1)S(1)} %collective-permute-done.9.zo_ref, bf16[1024,4096]{1,0:T(8,128)(2,1)} %w_ref.1, bf16[256,1536]{1,0:T(8,128)(2,1)S(1)} %collective-permute-done.2.refs_0_, ...), custom_call_target="tpu_custom_call" | custom-call | tf_op jit(solution)/shard_map/project/pallas_call | solution.py:333
  (30 shorter events, 0.1 us)
Async XLA Ops:
  1.7 4.0 %collective-permute-start = (bf16[8,192,384]{2,1,0:T(8,128)(2,1)S(1)}, bf16[8,192,384]{2,1,0:T(8,128)(2,1)S(1)}, u32[]{:S(2)}, u32[]{:S(2)}) collective-permute-start(bf16[8,192,384]{2,1,0:T(8,128)(2,1)S(1)} %get-tuple-element.29), channel_id=1, source_target_pairs={{0,32},{32,0},{1,33},{33,1},{2,34},{34,2},{3,35},{35,3},{4,36},{36... | collective-permute-start | bytes 3538952 | tf_op jit(solution)/shard_map/ppermute | solution.py:370
  5.9 1.4 %copy-start = (bf16[16,192,384]{2,1,0:T(8,128)(2,1)}, bf16[16,192,384]{2,1,0:T(8,128)(2,1)S(1)}, u32[]{:S(2)}) copy-start(bf16[16,192,384]{2,1,0:T(8,128)(2,1)S(1)} %merge.1) | copy-start | bytes 7077892
  7.3 43.0 %all-to-all-start = ((bf16[16,192,384]{2,1,0:T(8,128)(2,1)}), bf16[16,192,384]{2,1,0:T(8,128)(2,1)S(1)}, u32[]{:S(2)}, u32[]{:S(2)}) async-start(bf16[16,192,384]{2,1,0:T(8,128)(2,1)} %copy-done), calls=%async_computation | async-start | bytes 4718592 | tf_op jit(solution)/shard_map/all_to_all | solution.py:418
  14.2 25.7 %copy-start.12 = (s32[31,2]{0,1:T(2,128)S(1)}, s32[31,2]{0,1:T(2,128)}, u32[]{:S(2)}) copy-start(s32[31,2]{0,1:T(2,128)} %param.12) | copy-start | bytes 748
  14.2 25.9 %copy-start.10 = (s32[48]{0:T(128)S(1)}, s32[48]{0:T(128)}, u32[]{:S(2)}) copy-start(s32[48]{0:T(128)} %param.13) | copy-start | bytes 580
  14.2 25.9 %copy-start.11 = (s32[6]{0:T(128)S(1)}, s32[6]{0:T(128)}, u32[]{:S(2)}) copy-start(s32[6]{0:T(128)} %param.11) | copy-start | bytes 76
  16.3 21.3 %collective-permute-start.2 = (bf16[256,1536]{1,0:T(8,128)(2,1)}, bf16[256,1536]{1,0:T(8,128)(2,1)S(1)}, u32[]{:S(2)}, u32[]{:S(2)}) collective-permute-start(bf16[256,1536]{1,0:T(8,128)(2,1)} %dynamic_slice.9), channel_id=1, source_target_pairs={{0,65},{1,64},{64,1},{65,0},{2,67},{3,66},{66,3},{67,2},{4,69},{5,... | collective-permute-start | bytes 2359304 | tf_op jit(solution)/shard_map/ppermute | solution.py:400
  37.5 13.7 %collective-permute-start.3 = (bf16[1024,256]{1,0:T(8,128)(2,1)}, bf16[1024,256]{1,0:T(8,128)(2,1)}, u32[]{:S(2)}, u32[]{:S(2)}) collective-permute-start(bf16[1024,256]{1,0:T(8,128)(2,1)} %get-tuple-element.36), channel_id=1, source_target_pairs={{0,65},{1,64},{64,1},{65,0},{2,67},{3,66},{66,3},{67,2},{4,69},{5,... | collective-permute-start | bytes 1572872 | tf_op jit(solution)/shard_map/ppermute | solution.py:400
  40.2 2.6 %collective-permute-start.1 = (s32[116]{0:T(128)S(1)}, s32[116]{0:T(128)S(1)}, u32[]{:S(2)}, u32[]{:S(2)}) collective-permute-start(s32[116]{0:T(128)S(1)} %pad_add_fusion.1), channel_id=1, source_target_pairs={{0,32},{32,0},{1,33},{33,1},{2,34},{34,2},{3,35},{35,3},{4,36},{36... | collective-permute-start | bytes 1400 | tf_op jit(solution)/shard_map/ppermute | solution.py:370
  48.3 1.1 %copy-start.1 = (bf16[2,3072,128]{2,1,0:T(8,128)(2,1)}, bf16[2,3072,128]{2,1,0:T(8,128)(2,1)S(1)}, u32[]{:S(2)}) copy-start(bf16[2,3072,128]{2,1,0:T(8,128)(2,1)S(1)} %get-tuple-element.38.kdoc_ref) | copy-start | bytes 4718596
  49.4 0.9 copy-start.5
  50.3 6.7 %copy-start.9 = (bf16[1024,256]{1,0:T(8,128)(2,1)S(1)}, bf16[1024,256]{1,0:T(8,128)(2,1)}, u32[]{:S(2)}) copy-start(bf16[1024,256]{1,0:T(8,128)(2,1)} %get-tuple-element.43) | copy-start | bytes 1572868
  50.3 9.0 %copy-start.2 = (bf16[2,3072,128]{2,1,0:T(8,128)(2,1)S(1)}, bf16[2,3072,128]{2,1,0:T(8,128)(2,1)}, u32[]{:S(2)}) copy-start(bf16[2,3072,128]{2,1,0:T(8,128)(2,1)} %copy-done.1) | copy-start | bytes 4718596
  50.3 9.0 %copy-start.6 = (bf16[3072,128]{1,0:T(8,128)(2,1)S(1)}, bf16[3072,128]{1,0:T(8,128)(2,1)}, u32[]{:S(2)}) copy-start(bf16[3072,128]{1,0:T(8,128)(2,1)} %copy-done.5) | copy-start | bytes 2359300
  51.4 8.0 %collective-permute-start.4 = (bf16[3072,256]{1,0:T(8,128)(2,1)S(1)}, bf16[3072,256]{1,0:T(8,128)(2,1)S(1)}, u32[]{:S(2)}, u32[]{:S(2)}) collective-permute-start(bf16[3072,256]{1,0:T(8,128)(2,1)S(1)} %slice.3), channel_id=1, source_target_pairs={{0,32},{32,0},{1,33},{33,1},{2,34},{34,2},{3,35},{35,3},{4,36},{36... | collective-permute-start | bytes 4718600 | tf_op jit(solution)/shard_map/ppermute | solution.py:370
  53.6 20.4 %collective-permute-start.5 = (bf16[256,1536]{1,0:T(8,128)(2,1)S(1)}, bf16[256,1536]{1,0:T(8,128)(2,1)S(1)}, u32[]{:S(2)}, u32[]{:S(2)}) collective-permute-start(bf16[256,1536]{1,0:T(8,128)(2,1)S(1)} %collective-permute-done.2.refs_0_), channel_id=1, source_target_pairs={{0,6},{32,56},{2,0},{34,58},{4,2},{36,60},{6,4},{38,62},{8,14},{40... | collective-permute-start | bytes 2359304 | tf_op jit(solution)/shard_map/ppermute | solution.py:389
  55.8 18.1 %collective-permute-start.6 = (bf16[256,1536]{1,0:T(8,128)(2,1)S(1)}, bf16[256,1536]{1,0:T(8,128)(2,1)}, u32[]{:S(2)}, u32[]{:S(2)}) collective-permute-start(bf16[256,1536]{1,0:T(8,128)(2,1)S(1)} %collective-permute-done.2.refs_0_), channel_id=1, source_target_pairs={{0,4},{32,48},{2,6},{34,50},{4,0},{36,52},{6,2},{38,54},{8,12},{40... | collective-permute-start | bytes 2359304 | tf_op jit(solution)/shard_map/ppermute | solution.py:389
  56.4 20.6 %collective-permute-start.7 = (bf16[256,1536]{1,0:T(8,128)(2,1)S(1)}, bf16[256,1536]{1,0:T(8,128)(2,1)}, u32[]{:S(2)}, u32[]{:S(2)}) collective-permute-start(bf16[256,1536]{1,0:T(8,128)(2,1)S(1)} %collective-permute-done.2.refs_0_), channel_id=1, source_target_pairs={{0,2},{32,40},{2,4},{34,42},{4,6},{36,44},{6,0},{38,46},{8,10},{40... | collective-permute-start | bytes 2359304 | tf_op jit(solution)/shard_map/ppermute | solution.py:389
  57.0 17.0 %collective-permute-start.8 = (bf16[1024,256]{1,0:T(8,128)(2,1)S(1)}, bf16[1024,256]{1,0:T(8,128)(2,1)}, u32[]{:S(2)}, u32[]{:S(2)}) collective-permute-start(bf16[1024,256]{1,0:T(8,128)(2,1)S(1)} %copy-done.9), channel_id=1, source_target_pairs={{0,65},{1,64},{64,1},{65,0},{2,67},{3,66},{66,3},{67,2},{4,69},{5,... | collective-permute-start | bytes 1572872 | tf_op jit(solution)/shard_map/ppermute | solution.py:400
  74.0 3.0 %copy-start.3 = (bf16[256,1536]{1,0:T(8,128)(2,1)}, bf16[256,1536]{1,0:T(8,128)(2,1)S(1)}, u32[]{:S(2)}) copy-start(bf16[256,1536]{1,0:T(8,128)(2,1)S(1)} %collective-permute-done.5.refs_1_) | copy-start | bytes 2359300
  77.0 7.1 %collective-permute-start.14 = (bf16[1024,256]{1,0:T(8,128)(2,1)}, bf16[1024,256]{1,0:T(8,128)(2,1)S(1)}, u32[]{:S(2)}, u32[]{:S(2)}) collective-permute-start(bf16[1024,256]{1,0:T(8,128)(2,1)} %collective-permute-done.3.refs_4_), channel_id=1, source_target_pairs={{0,32},{32,0},{1,33},{33,1},{2,34},{34,2},{3,35},{35,3},{4,36},{36... | collective-permute-start | bytes 1572872 | tf_op jit(solution)/shard_map/ppermute | solution.py:370
  78.2 5.4 %copy-start.4 = (bf16[256,1536]{1,0:T(8,128)(2,1)S(1)}, bf16[256,1536]{1,0:T(8,128)(2,1)}, u32[]{:S(2)}) copy-start(bf16[256,1536]{1,0:T(8,128)(2,1)} %copy-done.3) | copy-start | bytes 2359300
  78.2 19.7 %all-to-all-start.1 = ((bf16[32,3,32,128]{3,2,1,0:T(8,128)(2,1)}), bf16[32,3,32,128]{3,2,1,0:T(8,128)(2,1)S(1)}, u32[]{:S(2)}, u32[]{:S(2)}) async-start(bf16[32,3,32,128]{3,2,1,0:T(8,128)(2,1)} %bitcast.5), calls=%async_computation.1 | async-start | bytes 1572864 | tf_op jit(solution)/shard_map/all_to_all | solution.py:429
  83.0 14.9 %collective-permute-start.15 = (bf16[1024,256]{1,0:T(8,128)(2,1)}, bf16[1024,256]{1,0:T(8,128)(2,1)}, u32[]{:S(2)}, u32[]{:S(2)}) collective-permute-start(bf16[1024,256]{1,0:T(8,128)(2,1)} %collective-permute-done.8.refs_5_), channel_id=1, source_target_pairs={{0,32},{32,0},{1,33},{33,1},{2,34},{34,2},{3,35},{35,3},{4,36},{36... | collective-permute-start | bytes 1572872 | tf_op jit(solution)/shard_map/ppermute | solution.py:370
  83.4 16.4 %collective-permute-start.10 = (bf16[256,1536]{1,0:T(8,128)(2,1)S(1)}, bf16[256,1536]{1,0:T(8,128)(2,1)}, u32[]{:S(2)}, u32[]{:S(2)}) collective-permute-start(bf16[256,1536]{1,0:T(8,128)(2,1)S(1)} %collective-permute-done.2.refs_0_), channel_id=1, source_target_pairs={{0,32},{32,0},{1,33},{33,1},{2,34},{34,2},{3,35},{35,3},{4,36},{36... | collective-permute-start | bytes 2359304 | tf_op jit(solution)/shard_map/ppermute | solution.py:370
  83.6 16.2 %collective-permute-start.11 = (bf16[256,1536]{1,0:T(8,128)(2,1)S(1)}, bf16[256,1536]{1,0:T(8,128)(2,1)}, u32[]{:S(2)}, u32[]{:S(2)}) collective-permute-start(bf16[256,1536]{1,0:T(8,128)(2,1)S(1)} %copy-done.4), channel_id=1, source_target_pairs={{0,32},{32,0},{1,33},{33,1},{2,34},{34,2},{3,35},{35,3},{4,36},{36... | collective-permute-start | bytes 2359304 | tf_op jit(solution)/shard_map/ppermute | solution.py:370
  83.9 15.9 %collective-permute-start.12 = (bf16[256,1536]{1,0:T(8,128)(2,1)}, bf16[256,1536]{1,0:T(8,128)(2,1)}, u32[]{:S(2)}, u32[]{:S(2)}) collective-permute-start(bf16[256,1536]{1,0:T(8,128)(2,1)} %collective-permute-done.6.refs_2_), channel_id=1, source_target_pairs={{0,32},{32,0},{1,33},{33,1},{2,34},{34,2},{3,35},{35,3},{4,36},{36... | collective-permute-start | bytes 2359304 | tf_op jit(solution)/shard_map/ppermute | solution.py:370
  84.1 0.8 copy-start.7
  84.9 14.9 %collective-permute-start.13 = (bf16[256,1536]{1,0:T(8,128)(2,1)}, bf16[256,1536]{1,0:T(8,128)(2,1)}, u32[]{:S(2)}, u32[]{:S(2)}) collective-permute-start(bf16[256,1536]{1,0:T(8,128)(2,1)} %collective-permute-done.7.refs_3_), channel_id=1, source_target_pairs={{0,32},{32,0},{1,33},{33,1},{2,34},{34,2},{3,35},{35,3},{4,36},{36... | collective-permute-start | bytes 2359304 | tf_op jit(solution)/shard_map/ppermute | solution.py:370
  97.9 3.1 %collective-permute-start.9 = (bf16[2,8,3,32,128]{4,3,2,1,0:T(8,128)(2,1)S(1)}, bf16[2,8,3,32,128]{4,3,2,1,0:T(8,128)(2,1)S(1)}, u32[]{:S(2)}, u32[]{:S(2)}) collective-permute-start(bf16[2,8,3,32,128]{4,3,2,1,0:T(8,128)(2,1)S(1)} %pick.1), channel_id=1, source_target_pairs={{0,32},{32,0},{1,33},{33,1},{2,34},{34,2},{3,35},{35,3},{4,36},{36... | collective-permute-start | bytes 1179656 | tf_op jit(solution)/shard_map/ppermute | solution.py:370
  101.0 1.0 copy-start.8

commit v4 on v3

--- a/solution.py
+++ b/solution.py
@@ -244,7 +244,7 @@
     )(core, meta, y, kvo, kdoc, qdoc, hi)
 
 
-SHARED = 1536
+SHARED = (512, 1024)
 LOADS = 8
 DIRECT = (256, 256)
 CTX = ("y", "x")
@@ -254,28 +254,41 @@
 
 
 def project_kernel(ids_ref, z_ref, zo_ref, w_ref, *refs):
-    count = NLINE + len(DIRECT)
+    count = NLINE * len(SHARED) + len(DIRECT)
     sides = (refs[:count], refs[count : 2 * count])
     o_ref, a_ref, b_ref = refs[2 * count : 2 * count + 3]
-    bufs, (acc_ref, w_buf, sems) = refs[2 * count + 3 : -3], refs[-3:]
+    bufs, (acc_ref, w_buf, p_buf, sems) = refs[2 * count + 3 : -4], refs[-4:]
     core, t_own = ids_ref[0], ids_ref[1]
     half = w_ref.shape[1] // 2
 
-    loads = []
+    steps = []
+    for side in range(2):
+        first = (core if side == 0 else 1 - core) * half
+        start, part = 0, 0
+        for n, width in enumerate(SHARED + DIRECT):
+            column = pl.ds(pl.multiple_of(first + start, HD), width)
+            place = slice(side * half + start, side * half + start + width)
+            rows = PIECE if n < len(SHARED) else HEADS * HD
+            loads = []
+            for m in range(HEADS * HD // rows):
+                loads.append(
+                    pltpu.make_async_copy(
+                        sides[side][part],
+                        p_buf.at[m * rows : (m + 1) * rows, place],
+                        sems.at[side, part],
+                    )
+                )
+                loads[-1].start()
+                part += 1
+            steps.append((side, n, column, place, loads))
+            start += width
+
+    w_loads = []
     rows = w_ref.shape[0] // LOADS
     for n in range(LOADS):
         part = slice(n * rows, (n + 1) * rows)
-        loads.append(pltpu.make_async_copy(w_ref.at[part], w_buf.at[part], sems.at[2, n]))
-        loads[-1].start()
-
-    steps = []
-    for side in range(2):
-        first = (core if side == 0 else 1 - core) * half
-        start = 0
-        for n, width in enumerate((SHARED,) + DIRECT):
-            column = pl.ds(pl.multiple_of(first + start, HD), width)
-            steps.append((side, n, column, slice(side * half + start, side * half + start + width)))
-            start += width
+        w_loads.append(pltpu.make_async_copy(w_ref.at[part], w_buf.at[part], sems.at[2, n]))
+        w_loads[-1].start()
 
     def head(ref, at, src, h):
         col = slice(at * HD, (at + 1) * HD)
@@ -294,28 +307,21 @@
             for h in range(PHEADS):
                 head(b_ref.at[side], n * PHEADS + h, 1 - t_own, piece * PHEADS + h)
 
-    for side, n, _, place in steps:
-        if n == 0:
-            acc = 0.0
-            for m in range(NLINE):
-                acc += jnp.dot(
-                    b_ref[side, :, m * PIECE : (m + 1) * PIECE],
-                    sides[side][m][...],
-                    preferred_element_type=F32,
-                )
-        else:
-            acc = jnp.dot(b_ref[2], sides[side][NLINE + n - 1][...], preferred_element_type=F32)
-        acc_ref[:, place] = acc
-    for copy in loads:
-        copy.wait()
+    for side, n, _, place, loads in steps:
+        for load in loads:
+            load.wait()
+        left = b_ref[side] if n < len(SHARED) else b_ref[2]
+        acc_ref[:, place] = jnp.dot(left, p_buf[:, place], preferred_element_type=F32)
+    for load in w_loads:
+        load.wait()
     stores = []
-    for side, n, column, place in steps:
+    for side, n, column, place, _ in steps:
         acc = acc_ref[:, place] + jnp.dot(
             a_ref[...], w_buf[:, column], preferred_element_type=F32
         )
         buf = bufs[n].at[side]
         buf[...] = acc.astype(BF)
-        store = pltpu.make_async_copy(buf, o_ref.at[:, column], sems.at[side, n])
+        store = pltpu.make_async_copy(buf, o_ref.at[:, column], sems.at[3 + side, n])
         store.start()
         stores.append(store)
     for store in stores:
@@ -327,12 +333,12 @@
     depth = HEADS * HD
     rows = 3 * HALF
     parts = mine + other
-    widths = (SHARED,) + DIRECT
+    widths = SHARED + DIRECT
     vmem = pl.BlockSpec(memory_space=pltpu.VMEM)
     hbm = pl.BlockSpec(memory_space=pltpu.HBM)
     return pl.pallas_call(
         project_kernel,
-        in_specs=[pl.BlockSpec(memory_space=pltpu.SMEM), vmem, vmem, hbm] + [vmem] * len(parts),
+        in_specs=[pl.BlockSpec(memory_space=pltpu.SMEM), vmem, vmem] + [hbm] * (1 + len(parts)),
         out_specs=hbm,
         out_shape=jax.ShapeDtypeStruct((rows, width), BF),
         scratch_shapes=[pltpu.VMEM((rows, depth), BF), pltpu.VMEM((3, rows, depth), BF)]
@@ -340,9 +346,10 @@
         + [
             pltpu.VMEM((rows, width), F32),
             pltpu.VMEM((depth, width), BF),
-            pltpu.SemaphoreType.DMA((3, LOADS)),
+            pltpu.VMEM((depth, width), BF),
+            pltpu.SemaphoreType.DMA((5, max(LOADS, len(mine)))),
         ],
-        compiler_params=pltpu.CompilerParams(vmem_limit_bytes=24 << 20),
+        compiler_params=pltpu.CompilerParams(vmem_limit_bytes=32 << 20),
         name="project",
     )(ids, z, zo, w, *parts)
 
@@ -370,8 +377,8 @@
     return lax.ppermute(x, "core", SWAP)
 
 
-def in_vmem(x):
-    return pltpu.with_memory_space_constraint(x, pltpu.VMEM)
+def in_hbm(x):
+    return pltpu.with_memory_space_constraint(x, pltpu.HBM)
 
 
 def after(values, *others):
@@ -400,31 +407,37 @@
     from_z = lambda x: lax.ppermute(x, ("z_lo", "tensor"), across)
     half = w.shape[1] // 2
     line = jnp.where(core == 0, x_at, y_at)
-    piece = from_z(lax.dynamic_slice(w, (PIECE * line, core * half), (PIECE, SHARED)))
-    direct, at = [], core * half + SHARED
+    at = core * half
+    fetched = []
+    for width in SHARED:
+        fetched.append(from_z(lax.dynamic_slice(w, (PIECE * line, at), (PIECE, width))))
+        at += width
+    direct = []
     for width in DIRECT:
         direct.append(lax.dynamic_slice(w, (0, at), (w.shape[0], width)))
         at += width
-    first = from_z(after(direct[0], piece))
+    first = from_z(after(direct[0], fetched[0]))
+    share = lambda piece: [piece] + [along_line(piece, step) for step in (1, 2, 3)]
+    early = share(fetched[0])
 
     ints = jnp.concatenate([doc_lengths, spans.reshape(-1), assignment])
     ints = jnp.where(chip // HEADS == core, ints, swap(ints))
     ints = jnp.concatenate([core[None], ints])
 
-    q, k, v = (pltpu.with_memory_space_constraint(x, pltpu.HBM) for x in (q, k, v))
+    q, k, v = (in_hbm(x) for x in (q, k, v))
     own, send = pack(core[None], q, k, v)
     recv = swap(send)
     x = merge(core[None], own, recv)
     y = lax.all_to_all(x, CTX, 0, 0, tiled=True).reshape(ROWS, 3 * HD)
     kdoc, qdoc, hi, meta = prepare(ints)
     y, kdoc, qdoc, hi, meta = lax.optimization_barrier((y, kdoc, qdoc, hi, meta))
-    y, piece, first = lax.optimization_barrier((y, piece, first))
+    y, early, piece, first = lax.optimization_barrier((y, early, fetched[1], first))
     second = from_z(after(direct[1], first))
     kvo = swap(y[:, HD:])
 
-    pieces = [piece] + [along_line(piece, step) for step in (1, 2, 3)]
+    pieces = share(piece)
     att = attend(core[None], meta, y, kvo, kdoc, qdoc, hi)
-    att, mine = lax.optimization_barrier((att, pieces + [first, second]))
+    att, mine = lax.optimization_barrier((att, early + pieces + [first, second]))
     other = [swap(p) for p in mine]
     z = lax.all_to_all(
         att.reshape(2 * NCTX, 3, QTR, HD), ("tensor",) + CTX, 0, 0, tiled=True
@@ -432,8 +445,8 @@
     zo = swap(pick(core[None], z))
     lines = jnp.where(core == 0, jnp.stack([x_at, y_at]), jnp.stack([y_at, x_at]))
     ids = jnp.concatenate([jnp.stack([core, t_own]), lines])
-    mine, other = ([in_vmem(p) for p in side] for side in (mine, other))
-    return project(ids, z, zo, pltpu.with_memory_space_constraint(w, pltpu.HBM), mine, other)
+    mine, other = ([in_hbm(p) for p in side] for side in (mine, other))
+    return project(ids, z, zo, in_hbm(w), mine, other)
 
 
 def solution(mesh):

time: 112 us -> 112 us (level)
  starting transfers between devices: 33.3 us -> 42.6 us
  waiting for transfers between devices: 36.3 us -> 27.1 us
  local copies, waits for them, and re-layouts: 9.95 us -> 8.65 us
    ppermute x3 -> x4, waiting for transfers between devices: 16.2 us -> 1.85 us  [shards(): from_z = lambda x: lax.ppermute(x, ('z_lo', 'tensor'), across)]
    all_to_all x1, waiting for transfers between devices: 0.01 us -> 8.99 us  [shards(): y = lax.all_to_all(x, CTX, 0, 0, tiled=True).reshape(ROWS, 3 * HD)]
    ppermute x3 -> x6, starting transfers between devices: 3.39 us -> 9.28 us  [along_line(): return lax.ppermute(x, ('core',) + CTX, pairs)]
    ppermute x3 -> x6, waiting for transfers between devices: 3.02 us -> 0.02 us  [along_line(): return lax.ppermute(x, ('core',) + CTX, pairs)]
    all_to_all x1, waiting for transfers between devices: 12.7 us -> 10.3 us  [shards(): lax.all_to_all(att.reshape(2 * NCTX, 3, QTR, HD), ('tensor',) + CTX, 0, 0...]
    unnamed x27 -> x31, local copies, waits for them, and re-layouts: 5.42 us -> 3.29 us
    ppermute x3 -> x4, starting transfers between devices: 8.46 us -> 9.94 us  [shards(): from_z = lambda x: lax.ppermute(x, ('z_lo', 'tensor'), across)]
    ppermute x10 -> x14, waiting for transfers between devices: 4.48 us -> 5.91 us  [swap(): return lax.ppermute(x, 'core', SWAP)]
  transfers between devices with their start and end apart: 18 -> 26, of which waited for: 7 -> 9; matrix products, arithmetic and copies ran while one was open for 4% -> 5% of each run, Pallas kernels for 18% -> 18%
where the time goes in v4:
time: 112 us; the launch traced here: 111 us
  starting transfers between devices  42.6 us (38%)
  Pallas kernels  32 us (29%)
  waiting for transfers between devices  27.1 us (24%)
  local copies, waits for them, and re-layouts  8.65 us (8%)
    pallas_call x1, Pallas kernels, attend(): pl.pallas_call(attend_kernel, out_shape=jax.ShapeDtypeStruct((2, NCTX, 3,...  15.2 us
    ppermute x14, starting transfers between devices, swap(): return lax.ppermute(x, 'core', SWAP)  11 us
    all_to_all x1, waiting for transfers between devices, shards(): lax.all_to_all(att.reshape(2 * NCTX, 3, QTR, HD), ('tensor',) + CTX, 0, 0...  10.3 us
    ppermute x4, starting transfers between devices, shards(): from_z = lambda x: lax.ppermute(x, ('z_lo', 'tensor'), across)  9.94 us
    pallas_call x1, Pallas kernels, project(): pl.pallas_call(project_kernel, in_specs=[pl.BlockSpec(memory_space=pltpu....  9.58 us
    ppermute x6, starting transfers between devices, along_line(): return lax.ppermute(x, ('core',) + CTX, pairs)  9.28 us
    all_to_all x1, waiting for transfers between devices, shards(): y = lax.all_to_all(x, CTX, 0, 0, tiled=True).reshape(ROWS, 3 * HD)  8.99 us
    all_to_all x1, starting transfers between devices, shards(): y = lax.all_to_all(x, CTX, 0, 0, tiled=True).reshape(ROWS, 3 * HD)  6.84 us
  transfers between devices with their start and end apart: 26, of which 9 were waited for; matrix products, arithmetic and copies ran while one was open for 5% of the time, Pallas kernels for 18%

profile of v4, /device:TPU:1, one launch (start us, length us, event | category | flops | bytes accessed | tf_op | source)
XLA Modules:
  0.0 111.2 jit_solution(208072169778358087)
XLA Ops:
  0.0 1.7 %pack.1 = (bf16[8,192,384]{2,1,0:T(8,128)(2,1)S(1)}, bf16[8,192,384]{2,1,0:T(8,128)(2,1)S(1)}) custom-call(s32[1]{0:T(128)} %bitcast.core_ref, bf16[384,1024]{1,0:T(8,128)(2,1)} %q_hbm.1, bf16[384,1024]{1,0:T(8,128)(2,1)} %k_hbm.1, bf16[384,1024]{1,0:T(8,128)(2,1)} %v_hbm.1), custom_call_target="tpu_custom_call" | custom-call | tf_op jit(solution)/shard_map/pack/pallas_call | solution.py:58
  1.7 1.5 %collective-permute-start = (bf16[8,192,384]{2,1,0:T(8,128)(2,1)S(1)}, bf16[8,192,384]{2,1,0:T(8,128)(2,1)S(1)}, u32[]{:S(2)}, u32[]{:S(2)}) collective-permute-start(bf16[8,192,384]{2,1,0:T(8,128)(2,1)S(1)} %get-tuple-element.37), channel_id=1, source_target_pairs={{0,32},{32,0},{1,33},{33,1},{2,34},{34,2},{3,35},{35,3},{4,36},{36... | collective-permute-start | bytes 3538952 | tf_op jit(solution)/shard_map/ppermute | solution.py:377
  3.2 2.5 %collective-permute-done.recv_ref = bf16[8,192,384]{2,1,0:T(8,128)(2,1)S(1)} collective-permute-done((bf16[8,192,384]{2,1,0:T(8,128)(2,1)S(1)}, bf16[8,192,384]{2,1,0:T(8,128)(2,1)S(1)}, u32[]{:S(2)}, u32[]{:S(2)}) %collective-permute-start) | collective-permute-done | bytes 1179680 | tf_op jit(solution)/shard_map/ppermute | solution.py:377
  5.7 0.2 merge.1
  5.9 1.4 %copy-done = bf16[16,192,384]{2,1,0:T(8,128)(2,1)} copy-done((bf16[16,192,384]{2,1,0:T(8,128)(2,1)}, bf16[16,192,384]{2,1,0:T(8,128)(2,1)S(1)}, u32[]{:S(2)}) %copy-start) | copy-done | bytes 2359320
  7.3 6.8 %all-to-all-start = ((bf16[16,192,384]{2,1,0:T(8,128)(2,1)}), bf16[16,192,384]{2,1,0:T(8,128)(2,1)S(1)}, u32[]{:S(2)}, u32[]{:S(2)}) async-start(bf16[16,192,384]{2,1,0:T(8,128)(2,1)} %copy-done), calls=%async_computation | async-start | bytes 4718592 | tf_op jit(solution)/shard_map/all_to_all | solution.py:431
  14.2 1.0 dynamic_slice.12
  15.2 3.8 %collective-permute-start.2 = (bf16[256,512]{1,0:T(8,128)(2,1)S(1)}, bf16[256,512]{1,0:T(8,128)(2,1)S(1)}, u32[]{:S(2)}, u32[]{:S(2)}) collective-permute-start(bf16[256,512]{1,0:T(8,128)(2,1)S(1)} %dynamic_slice.12), channel_id=1, source_target_pairs={{0,65},{1,64},{64,1},{65,0},{2,67},{3,66},{66,3},{67,2},{4,69},{5,... | collective-permute-start | bytes 786440 | tf_op jit(solution)/shard_map/ppermute | solution.py:407
  19.0 1.9 %dynamic_slice.13 = bf16[256,1024]{1,0:T(8,128)(2,1)} dynamic-slice(bf16[1024,4096]{1,0:T(8,128)(2,1)} %w_ref.1, s32[]{:T(128)S(6)} %select_n.46, s32[]{:T(128)S(6)} %select_n.48), dynamic_slice_sizes={256,1024} | dynamic-slice | bytes 1048580 | tf_op jit(solution)/shard_map/dynamic_slice | solution.py:413
  20.9 2.3 %constant_dynamic-slice_fusion = (bf16[1024,256]{1,0:T(8,128)(2,1)}, bf16[1024,256]{1,0:T(8,128)(2,1)}) fusion(bf16[1024,4096]{1,0:T(8,128)(2,1)} %w_ref.1, s32[]{:T(128)S(6)} %select_n.50, s32[]{:T(128)S(6)} %select_n.49), kind=kLoop, calls=%fused_computation.5 | loop fusion | bytes 2097160 | tf_op jit(solution)/shard_map/dynamic_slice | solution.py:417
  23.2 1.8 %collective-permute-done.2.refs_0_ = bf16[256,512]{1,0:T(8,128)(2,1)S(1)} collective-permute-done((bf16[256,512]{1,0:T(8,128)(2,1)S(1)}, bf16[256,512]{1,0:T(8,128)(2,1)S(1)}, u32[]{:S(2)}, u32[]{:S(2)}) %collective-permute-start.2) | collective-permute-done | bytes 262176 | tf_op jit(solution)/shard_map/ppermute | solution.py:407
  25.1 2.3 %collective-permute-start.7 = (bf16[1024,256]{1,0:T(8,128)(2,1)}, bf16[1024,256]{1,0:T(8,128)(2,1)}, u32[]{:S(2)}, u32[]{:S(2)}) collective-permute-start(bf16[1024,256]{1,0:T(8,128)(2,1)} %get-tuple-element.44), channel_id=1, source_target_pairs={{0,65},{1,64},{64,1},{65,0},{2,67},{3,66},{66,3},{67,2},{4,69},{5,... | collective-permute-start | bytes 1572872 | tf_op jit(solution)/shard_map/ppermute | solution.py:407
  27.4 0.1 copy.9
  27.5 0.1 reshape.13
  27.7 3.0 %collective-permute-start.1 = (s32[116]{0:T(128)S(1)}, s32[116]{0:T(128)S(1)}, u32[]{:S(2)}, u32[]{:S(2)}) collective-permute-start(s32[116]{0:T(128)S(1)} %pad_add_fusion.1), channel_id=1, source_target_pairs={{0,32},{32,0},{1,33},{33,1},{2,34},{34,2},{3,35},{35,3},{4,36},{36... | collective-permute-start | bytes 1400 | tf_op jit(solution)/shard_map/ppermute | solution.py:377
  30.7 2.9 %collective-permute-start.3 = (bf16[256,512]{1,0:T(8,128)(2,1)S(1)}, bf16[256,512]{1,0:T(8,128)(2,1)}, u32[]{:S(2)}, u32[]{:S(2)}) collective-permute-start(bf16[256,512]{1,0:T(8,128)(2,1)S(1)} %collective-permute-done.2.refs_0_), channel_id=1, source_target_pairs={{0,6},{32,56},{2,0},{34,58},{4,2},{36,60},{6,4},{38,62},{8,14},{40... | collective-permute-start | bytes 786440 | tf_op jit(solution)/shard_map/ppermute | solution.py:396
  33.5 0.6 collective-permute-start.4
  34.1 0.6 collective-permute-start.5
  34.9 5.3 %prepare.1 = (bf16[2,3072,128]{2,1,0:T(8,128)(2,1)S(1)}, bf16[3072,128]{1,0:T(8,128)(2,1)S(1)}, s32[12,8,256]{2,1,0:T(8,128)S(1)}, s32[60]{0:T(128)S(1)}) custom-call(s32[117]{0:T(128)S(1)} %pad_add_fusion.2.ints_ref), custom_call_target="tpu_custom_call" | custom-call | tf_op jit(solution)/shard_map/prepare/pallas_call | solution.py:153
  40.2 1.1 %copy-done.1 = bf16[2,3072,128]{2,1,0:T(8,128)(2,1)} copy-done((bf16[2,3072,128]{2,1,0:T(8,128)(2,1)}, bf16[2,3072,128]{2,1,0:T(8,128)(2,1)S(1)}, u32[]{:S(2)}) %copy-start.1) | copy-done | bytes 1572888
  41.3 9.0 %all-to-all-done = bf16[16,192,384]{2,1,0:T(8,128)(2,1)S(1)} async-done(((bf16[16,192,384]{2,1,0:T(8,128)(2,1)}), bf16[16,192,384]{2,1,0:T(8,128)(2,1)S(1)}, u32[]{:S(2)}, u32[]{:S(2)}) %all-to-all-start) | async-done | bytes 2359328 | tf_op jit(solution)/shard_map/all_to_all | solution.py:431
  50.3 0.1 slice.3
  50.5 3.2 %collective-permute-start.8 = (bf16[3072,256]{1,0:T(8,128)(2,1)S(1)}, bf16[3072,256]{1,0:T(8,128)(2,1)S(1)}, u32[]{:S(2)}, u32[]{:S(2)}) collective-permute-start(bf16[3072,256]{1,0:T(8,128)(2,1)S(1)} %slice.3), channel_id=1, source_target_pairs={{0,32},{32,0},{1,33},{33,1},{2,34},{34,2},{3,35},{35,3},{4,36},{36... | collective-permute-start | bytes 4718600 | tf_op jit(solution)/shard_map/ppermute | solution.py:377
  53.6 3.7 %collective-permute-start.12 = (bf16[1024,256]{1,0:T(8,128)(2,1)S(1)}, bf16[1024,256]{1,0:T(8,128)(2,1)}, u32[]{:S(2)}, u32[]{:S(2)}) collective-permute-start(bf16[1024,256]{1,0:T(8,128)(2,1)S(1)} %copy-done.6), channel_id=1, source_target_pairs={{0,65},{1,64},{64,1},{65,0},{2,67},{3,66},{66,3},{67,2},{4,69},{5,... | collective-permute-start | bytes 1572872 | tf_op jit(solution)/shard_map/ppermute | solution.py:407
  57.4 2.6 %collective-permute-start.10 = (bf16[256,1024]{1,0:T(8,128)(2,1)}, bf16[256,1024]{1,0:T(8,128)(2,1)}, u32[]{:S(2)}, u32[]{:S(2)}) collective-permute-start(bf16[256,1024]{1,0:T(8,128)(2,1)} %collective-permute-done.6.refs_4_), channel_id=1, source_target_pairs={{0,4},{32,48},{2,6},{34,50},{4,0},{36,52},{6,2},{38,54},{8,12},{40... | collective-permute-start | bytes 1572872 | tf_op jit(solution)/shard_map/ppermute | solution.py:396
  59.9 2.7 %collective-permute-start.9 = (bf16[256,1024]{1,0:T(8,128)(2,1)}, bf16[256,1024]{1,0:T(8,128)(2,1)}, u32[]{:S(2)}, u32[]{:S(2)}) collective-permute-start(bf16[256,1024]{1,0:T(8,128)(2,1)} %collective-permute-done.6.refs_4_), channel_id=1, source_target_pairs={{0,6},{32,56},{2,0},{34,58},{4,2},{36,60},{6,4},{38,62},{8,14},{40... | collective-permute-start | bytes 1572872 | tf_op jit(solution)/shard_map/ppermute | solution.py:396
  62.6 15.2 %attend.1 = bf16[2,16,3,32,128]{4,3,2,1,0:T(8,128)(2,1)} custom-call(s32[1]{0:T(128)} %bitcast.core_ref, s32[60]{0:T(128)S(1)} %get-tuple-element.42.meta_ref, bf16[3072,384]{1,0:T(8,128)(2,1)S(1)} %bitcast.8, bf16[3072,256]{1,0:T(8,128)(2,1)S(1)} %collective-permute-done.8.kvo_ref, bf16[2,3072,128]{2,1,0:T(8,128)(2,1)S(1)} %copy-done.2, ...), custom_call_target="tpu_custom_call" | custom-call | tf_op jit(solution)/shard_map/attend/pallas_call | solution.py:237
  77.9 5.5 %all-to-all-start.1 = ((bf16[32,3,32,128]{3,2,1,0:T(8,128)(2,1)}), bf16[32,3,32,128]{3,2,1,0:T(8,128)(2,1)S(1)}, u32[]{:S(2)}, u32[]{:S(2)}) async-start(bf16[32,3,32,128]{3,2,1,0:T(8,128)(2,1)} %bitcast.5), calls=%async_computation.1 | async-start | bytes 1572864 | tf_op jit(solution)/shard_map/all_to_all | solution.py:442
  83.4 0.1 collective-permute-start.14
  83.5 0.5 collective-permute-start.18
  84.0 0.1 collective-permute-start.19
  84.1 0.4 collective-permute-start.15
  84.5 0.1 collective-permute-start.16
  84.6 0.4 collective-permute-done.14.refs_10_
  85.1 0.1 collective-permute-start.17
  85.2 0.6 copy-done.8
  85.8 1.4 %collective-permute-done.15.refs_11_ = bf16[256,512]{1,0:T(8,128)(2,1)S(1)} collective-permute-done((bf16[256,512]{1,0:T(8,128)(2,1)}, bf16[256,512]{1,0:T(8,128)(2,1)S(1)}, u32[]{:S(2)}, u32[]{:S(2)}) %collective-permute-start.15) | collective-permute-done | bytes 262176 | tf_op jit(solution)/shard_map/ppermute | solution.py:377
  87.1 0.1 collective-permute-start.20
  87.3 0.2 collective-permute-done.16.refs_12_
  87.5 0.1 collective-permute-start.21
  87.7 0.2 collective-permute-done.17.refs_13_
  87.9 0.1 collective-permute-start.22
  88.0 0.4 collective-permute-start.23
  88.4 10.3 %all-to-all-done.1 = bf16[32,3,32,128]{3,2,1,0:T(8,128)(2,1)S(1)} async-done(((bf16[32,3,32,128]{3,2,1,0:T(8,128)(2,1)}), bf16[32,3,32,128]{3,2,1,0:T(8,128)(2,1)S(1)}, u32[]{:S(2)}, u32[]{:S(2)}) %all-to-all-start.1) | async-done | bytes 786464 | tf_op jit(solution)/shard_map/all_to_all | solution.py:442
  98.8 1.3 %collective-permute-start.13 = (bf16[2,8,3,32,128]{4,3,2,1,0:T(8,128)(2,1)S(1)}, bf16[2,8,3,32,128]{4,3,2,1,0:T(8,128)(2,1)S(1)}, u32[]{:S(2)}, u32[]{:S(2)}) collective-permute-start(bf16[2,8,3,32,128]{4,3,2,1,0:T(8,128)(2,1)S(1)} %pick.1), channel_id=1, source_target_pairs={{0,32},{32,0},{1,33},{33,1},{2,34},{34,2},{3,35},{35,3},{4,36},{36... | collective-permute-start | bytes 1179656 | tf_op jit(solution)/shard_map/ppermute | solution.py:377
  100.2 0.1 pad_add_fusion.ids_ref
  100.3 1.2 %collective-permute-done.13.zo_ref = bf16[2,8,3,32,128]{4,3,2,1,0:T(8,128)(2,1)S(1)} collective-permute-done((bf16[2,8,3,32,128]{4,3,2,1,0:T(8,128)(2,1)S(1)}, bf16[2,8,3,32,128]{4,3,2,1,0:T(8,128)(2,1)S(1)}, u32[]{:S(2)}, u32[]{:S(2)}) %collective-permute-start.13) | collective-permute-done | bytes 393248 | tf_op jit(solution)/shard_map/ppermute | solution.py:377
  101.4 9.6 %project.1 = bf16[192,4096]{1,0:T(8,128)(2,1)} custom-call(s32[4]{0:T(128)S(1)} %pad_add_fusion.ids_ref, bf16[2,16,3,32,128]{4,3,2,1,0:T(8,128)(2,1)S(1)} %bitcast.10, bf16[2,8,3,32,128]{4,3,2,1,0:T(8,128)(2,1)S(1)} %collective-permute-done.13.zo_ref, bf16[1024,4096]{1,0:T(8,128)(2,1)} %w_ref.1, bf16[256,512]{1,0:T(8,128)(2,1)} %copy-done.7, ...), custom_call_target="tpu_custom_call" | custom-call | tf_op jit(solution)/shard_map/project/pallas_call | solution.py:339
  (51 shorter events, 0.5 us)
Async XLA Ops:
  1.7 4.0 %collective-permute-start = (bf16[8,192,384]{2,1,0:T(8,128)(2,1)S(1)}, bf16[8,192,384]{2,1,0:T(8,128)(2,1)S(1)}, u32[]{:S(2)}, u32[]{:S(2)}) collective-permute-start(bf16[8,192,384]{2,1,0:T(8,128)(2,1)S(1)} %get-tuple-element.37), channel_id=1, source_target_pairs={{0,32},{32,0},{1,33},{33,1},{2,34},{34,2},{3,35},{35,3},{4,36},{36... | collective-permute-start | bytes 3538952 | tf_op jit(solution)/shard_map/ppermute | solution.py:377
  5.9 1.4 %copy-start = (bf16[16,192,384]{2,1,0:T(8,128)(2,1)}, bf16[16,192,384]{2,1,0:T(8,128)(2,1)S(1)}, u32[]{:S(2)}) copy-start(bf16[16,192,384]{2,1,0:T(8,128)(2,1)S(1)} %merge.1) | copy-start | bytes 7077892
  7.3 43.0 %all-to-all-start = ((bf16[16,192,384]{2,1,0:T(8,128)(2,1)}), bf16[16,192,384]{2,1,0:T(8,128)(2,1)S(1)}, u32[]{:S(2)}, u32[]{:S(2)}) async-start(bf16[16,192,384]{2,1,0:T(8,128)(2,1)} %copy-done), calls=%async_computation | async-start | bytes 4718592 | tf_op jit(solution)/shard_map/all_to_all | solution.py:431
  15.2 9.9 %collective-permute-start.2 = (bf16[256,512]{1,0:T(8,128)(2,1)S(1)}, bf16[256,512]{1,0:T(8,128)(2,1)S(1)}, u32[]{:S(2)}, u32[]{:S(2)}) collective-permute-start(bf16[256,512]{1,0:T(8,128)(2,1)S(1)} %dynamic_slice.12), channel_id=1, source_target_pairs={{0,65},{1,64},{64,1},{65,0},{2,67},{3,66},{66,3},{67,2},{4,69},{5,... | collective-permute-start | bytes 786440 | tf_op jit(solution)/shard_map/ppermute | solution.py:407
  19.0 8.4 %copy-start.14 = (s32[31,2]{0,1:T(2,128)S(1)}, s32[31,2]{0,1:T(2,128)}, u32[]{:S(2)}) copy-start(s32[31,2]{0,1:T(2,128)} %param.12) | copy-start | bytes 748
  19.0 8.6 %copy-start.12 = (s32[48]{0:T(128)S(1)}, s32[48]{0:T(128)}, u32[]{:S(2)}) copy-start(s32[48]{0:T(128)} %param.13) | copy-start | bytes 580
  19.0 8.6 %copy-start.13 = (s32[6]{0:T(128)S(1)}, s32[6]{0:T(128)}, u32[]{:S(2)}) copy-start(s32[6]{0:T(128)} %param.11) | copy-start | bytes 76
  20.9 29.4 %collective-permute-start.6 = (bf16[256,1024]{1,0:T(8,128)(2,1)}, bf16[256,1024]{1,0:T(8,128)(2,1)}, u32[]{:S(2)}, u32[]{:S(2)}) collective-permute-start(bf16[256,1024]{1,0:T(8,128)(2,1)} %dynamic_slice.13), channel_id=1, source_target_pairs={{0,65},{1,64},{64,1},{65,0},{2,67},{3,66},{66,3},{67,2},{4,69},{5,... | collective-permute-start | bytes 1572872 | tf_op jit(solution)/shard_map/ppermute | solution.py:407
  25.1 58.4 %copy-start.7 = (bf16[256,512]{1,0:T(8,128)(2,1)}, bf16[256,512]{1,0:T(8,128)(2,1)S(1)}, u32[]{:S(2)}) copy-start(bf16[256,512]{1,0:T(8,128)(2,1)S(1)} %collective-permute-done.2.refs_0_) | copy-start | bytes 786436
  25.1 25.3 %collective-permute-start.7 = (bf16[1024,256]{1,0:T(8,128)(2,1)}, bf16[1024,256]{1,0:T(8,128)(2,1)}, u32[]{:S(2)}, u32[]{:S(2)}) collective-permute-start(bf16[1024,256]{1,0:T(8,128)(2,1)} %get-tuple-element.44), channel_id=1, source_target_pairs={{0,65},{1,64},{64,1},{65,0},{2,67},{3,66},{66,3},{67,2},{4,69},{5,... | collective-permute-start | bytes 1572872 | tf_op jit(solution)/shard_map/ppermute | solution.py:407
  27.7 6.4 %collective-permute-start.1 = (s32[116]{0:T(128)S(1)}, s32[116]{0:T(128)S(1)}, u32[]{:S(2)}, u32[]{:S(2)}) collective-permute-start(s32[116]{0:T(128)S(1)} %pad_add_fusion.1), channel_id=1, source_target_pairs={{0,32},{32,0},{1,33},{33,1},{2,34},{34,2},{3,35},{35,3},{4,36},{36... | collective-permute-start | bytes 1400 | tf_op jit(solution)/shard_map/ppermute | solution.py:377
  30.7 19.6 %collective-permute-start.3 = (bf16[256,512]{1,0:T(8,128)(2,1)S(1)}, bf16[256,512]{1,0:T(8,128)(2,1)}, u32[]{:S(2)}, u32[]{:S(2)}) collective-permute-start(bf16[256,512]{1,0:T(8,128)(2,1)S(1)} %collective-permute-done.2.refs_0_), channel_id=1, source_target_pairs={{0,6},{32,56},{2,0},{34,58},{4,2},{36,60},{6,4},{38,62},{8,14},{40... | collective-permute-start | bytes 786440 | tf_op jit(solution)/shard_map/ppermute | solution.py:396
  33.5 16.8 %collective-permute-start.4 = (bf16[256,512]{1,0:T(8,128)(2,1)S(1)}, bf16[256,512]{1,0:T(8,128)(2,1)}, u32[]{:S(2)}, u32[]{:S(2)}) collective-permute-start(bf16[256,512]{1,0:T(8,128)(2,1)S(1)} %collective-permute-done.2.refs_0_), channel_id=1, source_target_pairs={{0,4},{32,48},{2,6},{34,50},{4,0},{36,52},{6,2},{38,54},{8,12},{40... | collective-permute-start | bytes 786440 | tf_op jit(solution)/shard_map/ppermute | solution.py:396
  34.1 16.2 %collective-permute-start.5 = (bf16[256,512]{1,0:T(8,128)(2,1)S(1)}, bf16[256,512]{1,0:T(8,128)(2,1)}, u32[]{:S(2)}, u32[]{:S(2)}) collective-permute-start(bf16[256,512]{1,0:T(8,128)(2,1)S(1)} %collective-permute-done.2.refs_0_), channel_id=1, source_target_pairs={{0,2},{32,40},{2,4},{34,42},{4,6},{36,44},{6,0},{38,46},{8,10},{40... | collective-permute-start | bytes 786440 | tf_op jit(solution)/shard_map/ppermute | solution.py:396
  40.2 1.1 %copy-start.1 = (bf16[2,3072,128]{2,1,0:T(8,128)(2,1)}, bf16[2,3072,128]{2,1,0:T(8,128)(2,1)S(1)}, u32[]{:S(2)}) copy-start(bf16[2,3072,128]{2,1,0:T(8,128)(2,1)S(1)} %get-tuple-element.46.kdoc_ref) | copy-start | bytes 4718596
  50.3 3.3 %copy-start.6 = (bf16[1024,256]{1,0:T(8,128)(2,1)S(1)}, bf16[1024,256]{1,0:T(8,128)(2,1)}, u32[]{:S(2)}) copy-start(bf16[1024,256]{1,0:T(8,128)(2,1)} %get-tuple-element.55) | copy-start | bytes 1572868
  50.3 12.3 %copy-start.2 = (bf16[2,3072,128]{2,1,0:T(8,128)(2,1)S(1)}, bf16[2,3072,128]{2,1,0:T(8,128)(2,1)}, u32[]{:S(2)}) copy-start(bf16[2,3072,128]{2,1,0:T(8,128)(2,1)} %copy-done.1) | copy-start | bytes 4718596
  50.5 12.2 %collective-permute-start.8 = (bf16[3072,256]{1,0:T(8,128)(2,1)S(1)}, bf16[3072,256]{1,0:T(8,128)(2,1)S(1)}, u32[]{:S(2)}, u32[]{:S(2)}) collective-permute-start(bf16[3072,256]{1,0:T(8,128)(2,1)S(1)} %slice.3), channel_id=1, source_target_pairs={{0,32},{32,0},{1,33},{33,1},{2,34},{34,2},{3,35},{35,3},{4,36},{36... | collective-permute-start | bytes 4718600 | tf_op jit(solution)/shard_map/ppermute | solution.py:377
  53.6 24.2 %collective-permute-start.12 = (bf16[1024,256]{1,0:T(8,128)(2,1)S(1)}, bf16[1024,256]{1,0:T(8,128)(2,1)}, u32[]{:S(2)}, u32[]{:S(2)}) collective-permute-start(bf16[1024,256]{1,0:T(8,128)(2,1)S(1)} %copy-done.6), channel_id=1, source_target_pairs={{0,65},{1,64},{64,1},{65,0},{2,67},{3,66},{66,3},{67,2},{4,69},{5,... | collective-permute-start | bytes 1572872 | tf_op jit(solution)/shard_map/ppermute | solution.py:407
  57.4 20.5 %collective-permute-start.10 = (bf16[256,1024]{1,0:T(8,128)(2,1)}, bf16[256,1024]{1,0:T(8,128)(2,1)}, u32[]{:S(2)}, u32[]{:S(2)}) collective-permute-start(bf16[256,1024]{1,0:T(8,128)(2,1)} %collective-permute-done.6.refs_4_), channel_id=1, source_target_pairs={{0,4},{32,48},{2,6},{34,50},{4,0},{36,52},{6,2},{38,54},{8,12},{40... | collective-permute-start | bytes 1572872 | tf_op jit(solution)/shard_map/ppermute | solution.py:396
  59.9 17.9 %collective-permute-start.11 = (bf16[256,1024]{1,0:T(8,128)(2,1)}, bf16[256,1024]{1,0:T(8,128)(2,1)}, u32[]{:S(2)}, u32[]{:S(2)}) collective-permute-start(bf16[256,1024]{1,0:T(8,128)(2,1)} %collective-permute-done.6.refs_4_), channel_id=1, source_target_pairs={{0,2},{32,40},{2,4},{34,42},{4,6},{36,44},{6,0},{38,46},{8,10},{40... | collective-permute-start | bytes 1572872 | tf_op jit(solution)/shard_map/ppermute | solution.py:396
  59.9 17.9 %collective-permute-start.9 = (bf16[256,1024]{1,0:T(8,128)(2,1)}, bf16[256,1024]{1,0:T(8,128)(2,1)}, u32[]{:S(2)}, u32[]{:S(2)}) collective-permute-start(bf16[256,1024]{1,0:T(8,128)(2,1)} %collective-permute-done.6.refs_4_), channel_id=1, source_target_pairs={{0,6},{32,56},{2,0},{34,58},{4,2},{36,60},{6,4},{38,62},{8,14},{40... | collective-permute-start | bytes 1572872 | tf_op jit(solution)/shard_map/ppermute | solution.py:396
  77.9 20.9 %all-to-all-start.1 = ((bf16[32,3,32,128]{3,2,1,0:T(8,128)(2,1)}), bf16[32,3,32,128]{3,2,1,0:T(8,128)(2,1)S(1)}, u32[]{:S(2)}, u32[]{:S(2)}) async-start(bf16[32,3,32,128]{3,2,1,0:T(8,128)(2,1)} %bitcast.5), calls=%async_computation.1 | async-start | bytes 1572864 | tf_op jit(solution)/shard_map/all_to_all | solution.py:442
  83.4 1.6 %collective-permute-start.14 = (bf16[256,512]{1,0:T(8,128)(2,1)S(1)}, bf16[256,512]{1,0:T(8,128)(2,1)S(1)}, u32[]{:S(2)}, u32[]{:S(2)}) collective-permute-start(bf16[256,512]{1,0:T(8,128)(2,1)S(1)} %collective-permute-done.2.refs_0_), channel_id=1, source_target_pairs={{0,32},{32,0},{1,33},{33,1},{2,34},{34,2},{3,35},{35,3},{4,36},{36... | collective-permute-start | bytes 786440 | tf_op jit(solution)/shard_map/ppermute | solution.py:377
  83.5 4.5 %collective-permute-start.18 = (bf16[256,1024]{1,0:T(8,128)(2,1)}, bf16[256,1024]{1,0:T(8,128)(2,1)S(1)}, u32[]{:S(2)}, u32[]{:S(2)}) collective-permute-start(bf16[256,1024]{1,0:T(8,128)(2,1)} %collective-permute-done.6.refs_4_), channel_id=1, source_target_pairs={{0,32},{32,0},{1,33},{33,1},{2,34},{34,2},{3,35},{35,3},{4,36},{36... | collective-permute-start | bytes 1572872 | tf_op jit(solution)/shard_map/ppermute | solution.py:377
  84.0 14.8 %collective-permute-start.19 = (bf16[256,1024]{1,0:T(8,128)(2,1)}, bf16[256,1024]{1,0:T(8,128)(2,1)S(1)}, u32[]{:S(2)}, u32[]{:S(2)}) collective-permute-start(bf16[256,1024]{1,0:T(8,128)(2,1)} %collective-permute-done.9.refs_5_), channel_id=1, source_target_pairs={{0,32},{32,0},{1,33},{33,1},{2,34},{34,2},{3,35},{35,3},{4,36},{36... | collective-permute-start | bytes 1572872 | tf_op jit(solution)/shard_map/ppermute | solution.py:377
  84.1 3.0 %collective-permute-start.15 = (bf16[256,512]{1,0:T(8,128)(2,1)}, bf16[256,512]{1,0:T(8,128)(2,1)S(1)}, u32[]{:S(2)}, u32[]{:S(2)}) collective-permute-start(bf16[256,512]{1,0:T(8,128)(2,1)} %collective-permute-done.3.refs_1_), channel_id=1, source_target_pairs={{0,32},{32,0},{1,33},{33,1},{2,34},{34,2},{3,35},{35,3},{4,36},{36... | collective-permute-start | bytes 786440 | tf_op jit(solution)/shard_map/ppermute | solution.py:377
  84.5 3.0 %collective-permute-start.16 = (bf16[256,512]{1,0:T(8,128)(2,1)}, bf16[256,512]{1,0:T(8,128)(2,1)S(1)}, u32[]{:S(2)}, u32[]{:S(2)}) collective-permute-start(bf16[256,512]{1,0:T(8,128)(2,1)} %collective-permute-done.4.refs_2_), channel_id=1, source_target_pairs={{0,32},{32,0},{1,33},{33,1},{2,34},{34,2},{3,35},{35,3},{4,36},{36... | collective-permute-start | bytes 786440 | tf_op jit(solution)/shard_map/ppermute | solution.py:377
  85.0 0.7 copy-start.8
  85.1 2.8 %collective-permute-start.17 = (bf16[256,512]{1,0:T(8,128)(2,1)}, bf16[256,512]{1,0:T(8,128)(2,1)S(1)}, u32[]{:S(2)}, u32[]{:S(2)}) collective-permute-start(bf16[256,512]{1,0:T(8,128)(2,1)} %collective-permute-done.5.refs_3_), channel_id=1, source_target_pairs={{0,32},{32,0},{1,33},{33,1},{2,34},{34,2},{3,35},{35,3},{4,36},{36... | collective-permute-start | bytes 786440 | tf_op jit(solution)/shard_map/ppermute | solution.py:377
  87.1 11.6 %copy-start.9 = (bf16[256,512]{1,0:T(8,128)(2,1)}, bf16[256,512]{1,0:T(8,128)(2,1)S(1)}, u32[]{:S(2)}) copy-start(bf16[256,512]{1,0:T(8,128)(2,1)S(1)} %collective-permute-done.15.refs_11_) | copy-start | bytes 786436
  87.1 13.1 %collective-permute-start.20 = (bf16[256,1024]{1,0:T(8,128)(2,1)}, bf16[256,1024]{1,0:T(8,128)(2,1)S(1)}, u32[]{:S(2)}, u32[]{:S(2)}) collective-permute-start(bf16[256,1024]{1,0:T(8,128)(2,1)} %collective-permute-done.10.refs_6_), channel_id=1, source_target_pairs={{0,32},{32,0},{1,33},{33,1},{2,34},{34,2},{3,35},{35,3},{4,36},{36... | collective-permute-start | bytes 1572872 | tf_op jit(solution)/shard_map/ppermute | solution.py:377
  87.5 11.2 %copy-start.10 = (bf16[256,512]{1,0:T(8,128)(2,1)}, bf16[256,512]{1,0:T(8,128)(2,1)S(1)}, u32[]{:S(2)}) copy-start(bf16[256,512]{1,0:T(8,128)(2,1)S(1)} %collective-permute-done.16.refs_12_) | copy-start | bytes 786436
  87.5 12.7 %collective-permute-start.21 = (bf16[256,1024]{1,0:T(8,128)(2,1)}, bf16[256,1024]{1,0:T(8,128)(2,1)}, u32[]{:S(2)}, u32[]{:S(2)}) collective-permute-start(bf16[256,1024]{1,0:T(8,128)(2,1)} %collective-permute-done.11.refs_7_), channel_id=1, source_target_pairs={{0,32},{32,0},{1,33},{33,1},{2,34},{34,2},{3,35},{35,3},{4,36},{36... | collective-permute-start | bytes 1572872 | tf_op jit(solution)/shard_map/ppermute | solution.py:377
  87.9 10.9 %copy-start.11 = (bf16[256,512]{1,0:T(8,128)(2,1)}, bf16[256,512]{1,0:T(8,128)(2,1)S(1)}, u32[]{:S(2)}) copy-start(bf16[256,512]{1,0:T(8,128)(2,1)S(1)} %collective-permute-done.17.refs_13_) | copy-start | bytes 786436
  87.9 12.4 %collective-permute-start.22 = (bf16[1024,256]{1,0:T(8,128)(2,1)}, bf16[1024,256]{1,0:T(8,128)(2,1)}, u32[]{:S(2)}, u32[]{:S(2)}) collective-permute-start(bf16[1024,256]{1,0:T(8,128)(2,1)} %collective-permute-done.7.refs_8_), channel_id=1, source_target_pairs={{0,32},{32,0},{1,33},{33,1},{2,34},{34,2},{3,35},{35,3},{4,36},{36... | collective-permute-start | bytes 1572872 | tf_op jit(solution)/shard_map/ppermute | solution.py:377
  88.0 13.4 %copy-start.3 = (bf16[256,1024]{1,0:T(8,128)(2,1)}, bf16[256,1024]{1,0:T(8,128)(2,1)S(1)}, u32[]{:S(2)}) copy-start(bf16[256,1024]{1,0:T(8,128)(2,1)S(1)} %collective-permute-done.18.refs_14_) | copy-start | bytes 1572868
  88.0 12.2 %collective-permute-start.23 = (bf16[1024,256]{1,0:T(8,128)(2,1)}, bf16[1024,256]{1,0:T(8,128)(2,1)}, u32[]{:S(2)}, u32[]{:S(2)}) collective-permute-start(bf16[1024,256]{1,0:T(8,128)(2,1)} %collective-permute-done.12.refs_9_), channel_id=1, source_target_pairs={{0,32},{32,0},{1,33},{33,1},{2,34},{34,2},{3,35},{35,3},{4,36},{36... | collective-permute-start | bytes 1572872 | tf_op jit(solution)/shard_map/ppermute | solution.py:377
  98.8 2.6 %copy-start.4 = (bf16[256,1024]{1,0:T(8,128)(2,1)}, bf16[256,1024]{1,0:T(8,128)(2,1)S(1)}, u32[]{:S(2)}) copy-start(bf16[256,1024]{1,0:T(8,128)(2,1)S(1)} %collective-permute-done.19.refs_15_) | copy-start | bytes 1572868
  98.8 2.6 %collective-permute-start.13 = (bf16[2,8,3,32,128]{4,3,2,1,0:T(8,128)(2,1)S(1)}, bf16[2,8,3,32,128]{4,3,2,1,0:T(8,128)(2,1)S(1)}, u32[]{:S(2)}, u32[]{:S(2)}) collective-permute-start(bf16[2,8,3,32,128]{4,3,2,1,0:T(8,128)(2,1)S(1)} %pick.1), channel_id=1, source_target_pairs={{0,32},{32,0},{1,33},{33,1},{2,34},{34,2},{3,35},{35,3},{4,36},{36... | collective-permute-start | bytes 1179656 | tf_op jit(solution)/shard_map/ppermute | solution.py:377
  100.2 1.2 %copy-start.5 = (bf16[256,1024]{1,0:T(8,128)(2,1)}, bf16[256,1024]{1,0:T(8,128)(2,1)S(1)}, u32[]{:S(2)}) copy-start(bf16[256,1024]{1,0:T(8,128)(2,1)S(1)} %collective-permute-done.20.refs_16_) | copy-start | bytes 1572868

commit v5 on v4

--- a/solution.py
+++ b/solution.py
@@ -244,7 +244,7 @@
     )(core, meta, y, kvo, kdoc, qdoc, hi)
 
 
-SHARED = (512, 1024)
+SHARED = (256, 1280)
 LOADS = 8
 DIRECT = (256, 256)
 CTX = ("y", "x")

time: 112 us -> 110 us (0.982)
  starting transfers between devices: 42.6 us -> 40.4 us
    all_to_all x1, waiting for transfers between devices: 8.99 us -> 12 us  [shards(): y = lax.all_to_all(x, CTX, 0, 0, tiled=True).reshape(ROWS, 3 * HD)]
    ppermute x14, starting transfers between devices: 11 us -> 9.11 us  [swap(): return lax.ppermute(x, 'core', SWAP)]
    ppermute x4, waiting for transfers between devices: 1.85 us -> 0.01 us  [shards(): from_z = lambda x: lax.ppermute(x, ('z_lo', 'tensor'), across)]
    unnamed x31 -> x35, local copies, waits for them, and re-layouts: 3.29 us -> 3.13 us
  transfers between devices with their start and end apart: 26 -> 26, of which waited for: 9 -> 6; matrix products, arithmetic and copies ran while one was open for 5% -> 5% of each run, Pallas kernels for 18% -> 19%
where the time goes in v5:
time: 110 us
  starting transfers between devices  40.4 us (37%)
  Pallas kernels  32.2 us (29%)
  waiting for transfers between devices  27.7 us (25%)
  local copies, waits for them, and re-layouts  8.51 us (8%)
    pallas_call x1, Pallas kernels, attend(): pl.pallas_call(attend_kernel, out_shape=jax.ShapeDtypeStruct((2, NCTX, 3,...  15.2 us
    all_to_all x1, waiting for transfers between devices, shards(): y = lax.all_to_all(x, CTX, 0, 0, tiled=True).reshape(ROWS, 3 * HD)  12 us
    all_to_all x1, waiting for transfers between devices, shards(): lax.all_to_all(att.reshape(2 * NCTX, 3, QTR, HD), ('tensor',) + CTX, 0, 0...  10.8 us
    ppermute x4, starting transfers between devices, shards(): from_z = lambda x: lax.ppermute(x, ('z_lo', 'tensor'), across)  10.3 us
    pallas_call x1, Pallas kernels, project(): pl.pallas_call(project_kernel, in_specs=[pl.BlockSpec(memory_space=pltpu....  9.74 us
    ppermute x6, starting transfers between devices, along_line(): return lax.ppermute(x, ('core',) + CTX, pairs)  9.23 us
    ppermute x14, starting transfers between devices, swap(): return lax.ppermute(x, 'core', SWAP)  9.11 us
    all_to_all x1, starting transfers between devices, shards(): y = lax.all_to_all(x, CTX, 0, 0, tiled=True).reshape(ROWS, 3 * HD)  6.84 us
  transfers between devices with their start and end apart: 26, of which 6 were waited for; matrix products, arithmetic and copies ran while one was open for 5% of the time, Pallas kernels for 19%

profile of v5, /device:TPU:1, one launch (start us, length us, event | category | flops | bytes accessed | tf_op | source)
XLA Modules:
  0.0 109.6 jit_solution(13534282177214005409)
XLA Ops:
  0.0 1.7 %pack.1 = (bf16[8,192,384]{2,1,0:T(8,128)(2,1)S(1)}, bf16[8,192,384]{2,1,0:T(8,128)(2,1)S(1)}) custom-call(s32[1]{0:T(128)} %bitcast.core_ref, bf16[384,1024]{1,0:T(8,128)(2,1)} %q_hbm.1, bf16[384,1024]{1,0:T(8,128)(2,1)} %k_hbm.1, bf16[384,1024]{1,0:T(8,128)(2,1)} %v_hbm.1), custom_call_target="tpu_custom_call" | custom-call | tf_op jit(solution)/shard_map/pack/pallas_call | solution.py:58
  1.7 1.5 %collective-permute-start = (bf16[8,192,384]{2,1,0:T(8,128)(2,1)S(1)}, bf16[8,192,384]{2,1,0:T(8,128)(2,1)S(1)}, u32[]{:S(2)}, u32[]{:S(2)}) collective-permute-start(bf16[8,192,384]{2,1,0:T(8,128)(2,1)S(1)} %get-tuple-element.37), channel_id=1, source_target_pairs={{0,32},{32,0},{1,33},{33,1},{2,34},{34,2},{3,35},{35,3},{4,36},{36... | collective-permute-start | bytes 3538952 | tf_op jit(solution)/shard_map/ppermute | solution.py:377
  3.2 2.5 %collective-permute-done.recv_ref = bf16[8,192,384]{2,1,0:T(8,128)(2,1)S(1)} collective-permute-done((bf16[8,192,384]{2,1,0:T(8,128)(2,1)S(1)}, bf16[8,192,384]{2,1,0:T(8,128)(2,1)S(1)}, u32[]{:S(2)}, u32[]{:S(2)}) %collective-permute-start) | collective-permute-done | bytes 1179680 | tf_op jit(solution)/shard_map/ppermute | solution.py:377
  5.7 0.2 merge.1
  5.9 1.4 %copy-done = bf16[16,192,384]{2,1,0:T(8,128)(2,1)} copy-done((bf16[16,192,384]{2,1,0:T(8,128)(2,1)}, bf16[16,192,384]{2,1,0:T(8,128)(2,1)S(1)}, u32[]{:S(2)}) %copy-start) | copy-done | bytes 2359320
  7.3 6.8 %all-to-all-start = ((bf16[16,192,384]{2,1,0:T(8,128)(2,1)}), bf16[16,192,384]{2,1,0:T(8,128)(2,1)S(1)}, u32[]{:S(2)}, u32[]{:S(2)}) async-start(bf16[16,192,384]{2,1,0:T(8,128)(2,1)} %copy-done), calls=%async_computation | async-start | bytes 4718592 | tf_op jit(solution)/shard_map/all_to_all | solution.py:431
  14.2 0.9 dynamic_slice.12
  15.1 3.8 %collective-permute-start.2 = (bf16[256,256]{1,0:T(8,128)(2,1)S(1)}, bf16[256,256]{1,0:T(8,128)(2,1)S(1)}, u32[]{:S(2)}, u32[]{:S(2)}) collective-permute-start(bf16[256,256]{1,0:T(8,128)(2,1)S(1)} %dynamic_slice.12), channel_id=1, source_target_pairs={{0,65},{1,64},{64,1},{65,0},{2,67},{3,66},{66,3},{67,2},{4,69},{5,... | collective-permute-start | bytes 393224 | tf_op jit(solution)/shard_map/ppermute | solution.py:407
  18.9 2.0 %dynamic_slice.13 = bf16[256,1280]{1,0:T(8,128)(2,1)} dynamic-slice(bf16[1024,4096]{1,0:T(8,128)(2,1)} %w_ref.1, s32[]{:T(128)S(6)} %select_n.46, s32[]{:T(128)S(6)} %select_n.48), dynamic_slice_sizes={256,1280} | dynamic-slice | bytes 1310724 | tf_op jit(solution)/shard_map/dynamic_slice | solution.py:413
  21.0 2.2 %constant_dynamic-slice_fusion = (bf16[1024,256]{1,0:T(8,128)(2,1)}, bf16[1024,256]{1,0:T(8,128)(2,1)}) fusion(bf16[1024,4096]{1,0:T(8,128)(2,1)} %w_ref.1, s32[]{:T(128)S(6)} %select_n.50, s32[]{:T(128)S(6)} %select_n.49), kind=kLoop, calls=%fused_computation.5 | loop fusion | bytes 2097160 | tf_op jit(solution)/shard_map/dynamic_slice | solution.py:417
  23.2 2.7 %collective-permute-start.7 = (bf16[1024,256]{1,0:T(8,128)(2,1)}, bf16[1024,256]{1,0:T(8,128)(2,1)}, u32[]{:S(2)}, u32[]{:S(2)}) collective-permute-start(bf16[1024,256]{1,0:T(8,128)(2,1)} %get-tuple-element.44), channel_id=1, source_target_pairs={{0,65},{1,64},{64,1},{65,0},{2,67},{3,66},{66,3},{67,2},{4,69},{5,... | collective-permute-start | bytes 1572872 | tf_op jit(solution)/shard_map/ppermute | solution.py:407
  25.9 0.1 copy.9
  26.0 0.1 reshape.13
  26.1 0.1 pad_add_fusion.1
  26.2 1.5 %collective-permute-start.1 = (s32[116]{0:T(128)S(1)}, s32[116]{0:T(128)S(1)}, u32[]{:S(2)}, u32[]{:S(2)}) collective-permute-start(s32[116]{0:T(128)S(1)} %pad_add_fusion.1), channel_id=1, source_target_pairs={{0,32},{32,0},{1,33},{33,1},{2,34},{34,2},{3,35},{35,3},{4,36},{36... | collective-permute-start | bytes 1400 | tf_op jit(solution)/shard_map/ppermute | solution.py:377
  27.7 2.8 %collective-permute-start.3 = (bf16[256,256]{1,0:T(8,128)(2,1)S(1)}, bf16[256,256]{1,0:T(8,128)(2,1)S(1)}, u32[]{:S(2)}, u32[]{:S(2)}) collective-permute-start(bf16[256,256]{1,0:T(8,128)(2,1)S(1)} %collective-permute-done.2.refs_0_), channel_id=1, source_target_pairs={{0,6},{32,56},{2,0},{34,58},{4,2},{36,60},{6,4},{38,62},{8,14},{40... | collective-permute-start | bytes 393224 | tf_op jit(solution)/shard_map/ppermute | solution.py:396
  30.5 0.6 collective-permute-start.4
  31.1 0.6 collective-permute-start.5
  31.7 0.1 broadcast_select_fusion
  31.8 0.1 pad_add_fusion.2.ints_ref
  31.8 5.3 %prepare.1 = (bf16[2,3072,128]{2,1,0:T(8,128)(2,1)S(1)}, bf16[3072,128]{1,0:T(8,128)(2,1)S(1)}, s32[12,8,256]{2,1,0:T(8,128)S(1)}, s32[60]{0:T(128)S(1)}) custom-call(s32[117]{0:T(128)S(1)} %pad_add_fusion.2.ints_ref), custom_call_target="tpu_custom_call" | custom-call | tf_op jit(solution)/shard_map/prepare/pallas_call | solution.py:153
  37.2 1.1 %copy-done.1 = bf16[2,3072,128]{2,1,0:T(8,128)(2,1)} copy-done((bf16[2,3072,128]{2,1,0:T(8,128)(2,1)}, bf16[2,3072,128]{2,1,0:T(8,128)(2,1)S(1)}, u32[]{:S(2)}) %copy-start.1) | copy-done | bytes 1572888
  38.3 12.0 %all-to-all-done = bf16[16,192,384]{2,1,0:T(8,128)(2,1)S(1)} async-done(((bf16[16,192,384]{2,1,0:T(8,128)(2,1)}), bf16[16,192,384]{2,1,0:T(8,128)(2,1)S(1)}, u32[]{:S(2)}, u32[]{:S(2)}) %all-to-all-start) | async-done | bytes 2359328 | tf_op jit(solution)/shard_map/all_to_all | solution.py:431
  50.3 0.1 slice.3
  50.5 1.7 %collective-permute-start.8 = (bf16[3072,256]{1,0:T(8,128)(2,1)S(1)}, bf16[3072,256]{1,0:T(8,128)(2,1)S(1)}, u32[]{:S(2)}, u32[]{:S(2)}) collective-permute-start(bf16[3072,256]{1,0:T(8,128)(2,1)S(1)} %slice.3), channel_id=1, source_target_pairs={{0,32},{32,0},{1,33},{33,1},{2,34},{34,2},{3,35},{35,3},{4,36},{36... | collective-permute-start | bytes 4718600 | tf_op jit(solution)/shard_map/ppermute | solution.py:377
  52.2 2.6 %collective-permute-start.10 = (bf16[256,1280]{1,0:T(8,128)(2,1)}, bf16[256,1280]{1,0:T(8,128)(2,1)}, u32[]{:S(2)}, u32[]{:S(2)}) collective-permute-start(bf16[256,1280]{1,0:T(8,128)(2,1)} %collective-permute-done.6.refs_4_), channel_id=1, source_target_pairs={{0,4},{32,48},{2,6},{34,50},{4,0},{36,52},{6,2},{38,54},{8,12},{40... | collective-permute-start | bytes 1966088 | tf_op jit(solution)/shard_map/ppermute | solution.py:396
  54.7 2.7 %collective-permute-start.9 = (bf16[256,1280]{1,0:T(8,128)(2,1)}, bf16[256,1280]{1,0:T(8,128)(2,1)}, u32[]{:S(2)}, u32[]{:S(2)}) collective-permute-start(bf16[256,1280]{1,0:T(8,128)(2,1)} %collective-permute-done.6.refs_4_), channel_id=1, source_target_pairs={{0,6},{32,56},{2,0},{34,58},{4,2},{36,60},{6,4},{38,62},{8,14},{40... | collective-permute-start | bytes 1966088 | tf_op jit(solution)/shard_map/ppermute | solution.py:396
  57.4 3.8 %collective-permute-start.12 = (bf16[1024,256]{1,0:T(8,128)(2,1)S(1)}, bf16[1024,256]{1,0:T(8,128)(2,1)}, u32[]{:S(2)}, u32[]{:S(2)}) collective-permute-start(bf16[1024,256]{1,0:T(8,128)(2,1)S(1)} %copy-done.6), channel_id=1, source_target_pairs={{0,65},{1,64},{64,1},{65,0},{2,67},{3,66},{66,3},{67,2},{4,69},{5,... | collective-permute-start | bytes 1572872 | tf_op jit(solution)/shard_map/ppermute | solution.py:407
  61.2 15.2 %attend.1 = bf16[2,16,3,32,128]{4,3,2,1,0:T(8,128)(2,1)} custom-call(s32[1]{0:T(128)} %bitcast.core_ref, s32[60]{0:T(128)S(1)} %get-tuple-element.42.meta_ref, bf16[3072,384]{1,0:T(8,128)(2,1)S(1)} %bitcast.8, bf16[3072,256]{1,0:T(8,128)(2,1)S(1)} %collective-permute-done.8.kvo_ref, bf16[2,3072,128]{2,1,0:T(8,128)(2,1)S(1)} %copy-done.2, ...), custom_call_target="tpu_custom_call" | custom-call | tf_op jit(solution)/shard_map/attend/pallas_call | solution.py:237
  76.5 0.1 collective-permute-start.22
  76.6 4.9 %all-to-all-start.1 = ((bf16[32,3,32,128]{3,2,1,0:T(8,128)(2,1)}), bf16[32,3,32,128]{3,2,1,0:T(8,128)(2,1)S(1)}, u32[]{:S(2)}, u32[]{:S(2)}) async-start(bf16[32,3,32,128]{3,2,1,0:T(8,128)(2,1)} %bitcast.5), calls=%async_computation.1 | async-start | bytes 1572864 | tf_op jit(solution)/shard_map/all_to_all | solution.py:442
  81.5 0.4 collective-permute-start.14
  81.9 0.2 collective-permute-start.23
  82.1 0.3 collective-permute-start.15
  82.4 0.2 collective-permute-start.16
  82.6 0.3 collective-permute-done.14.refs_10_
  82.9 0.3 collective-permute-start.17
  83.2 0.9 collective-permute-done.15.refs_11_
  84.2 0.2 collective-permute-start.18
  84.4 0.4 copy-done.12
  84.8 0.2 collective-permute-start.19
  85.0 0.3 collective-permute-start.20
  85.3 0.2 collective-permute-start.21
  85.6 10.8 %all-to-all-done.1 = bf16[32,3,32,128]{3,2,1,0:T(8,128)(2,1)S(1)} async-done(((bf16[32,3,32,128]{3,2,1,0:T(8,128)(2,1)}), bf16[32,3,32,128]{3,2,1,0:T(8,128)(2,1)S(1)}, u32[]{:S(2)}, u32[]{:S(2)}) %all-to-all-start.1) | async-done | bytes 786464 | tf_op jit(solution)/shard_map/all_to_all | solution.py:442
  96.4 1.9 %collective-permute-start.13 = (bf16[2,8,3,32,128]{4,3,2,1,0:T(8,128)(2,1)S(1)}, bf16[2,8,3,32,128]{4,3,2,1,0:T(8,128)(2,1)S(1)}, u32[]{:S(2)}, u32[]{:S(2)}) collective-permute-start(bf16[2,8,3,32,128]{4,3,2,1,0:T(8,128)(2,1)S(1)} %pick.1), channel_id=1, source_target_pairs={{0,32},{32,0},{1,33},{33,1},{2,34},{34,2},{3,35},{35,3},{4,36},{36... | collective-permute-start | bytes 1179656 | tf_op jit(solution)/shard_map/ppermute | solution.py:377
  98.4 0.1 pad_add_fusion.ids_ref
  98.6 1.1 %collective-permute-done.13.zo_ref = bf16[2,8,3,32,128]{4,3,2,1,0:T(8,128)(2,1)S(1)} collective-permute-done((bf16[2,8,3,32,128]{4,3,2,1,0:T(8,128)(2,1)S(1)}, bf16[2,8,3,32,128]{4,3,2,1,0:T(8,128)(2,1)S(1)}, u32[]{:S(2)}, u32[]{:S(2)}) %collective-permute-start.13) | collective-permute-done | bytes 393248 | tf_op jit(solution)/shard_map/ppermute | solution.py:377
  99.7 9.7 %project.1 = bf16[192,4096]{1,0:T(8,128)(2,1)} custom-call(s32[4]{0:T(128)S(1)} %pad_add_fusion.ids_ref, bf16[2,16,3,32,128]{4,3,2,1,0:T(8,128)(2,1)S(1)} %bitcast.10, bf16[2,8,3,32,128]{4,3,2,1,0:T(8,128)(2,1)S(1)} %collective-permute-done.13.zo_ref, bf16[1024,4096]{1,0:T(8,128)(2,1)} %w_ref.1, bf16[256,256]{1,0:T(8,128)(2,1)} %copy-done.7, ...), custom_call_target="tpu_custom_call" | custom-call | tf_op jit(solution)/shard_map/project/pallas_call | solution.py:339
  (55 shorter events, 0.2 us)
Async XLA Ops:
  1.7 4.0 %collective-permute-start = (bf16[8,192,384]{2,1,0:T(8,128)(2,1)S(1)}, bf16[8,192,384]{2,1,0:T(8,128)(2,1)S(1)}, u32[]{:S(2)}, u32[]{:S(2)}) collective-permute-start(bf16[8,192,384]{2,1,0:T(8,128)(2,1)S(1)} %get-tuple-element.37), channel_id=1, source_target_pairs={{0,32},{32,0},{1,33},{33,1},{2,34},{34,2},{3,35},{35,3},{4,36},{36... | collective-permute-start | bytes 3538952 | tf_op jit(solution)/shard_map/ppermute | solution.py:377
  5.9 1.4 %copy-start = (bf16[16,192,384]{2,1,0:T(8,128)(2,1)}, bf16[16,192,384]{2,1,0:T(8,128)(2,1)S(1)}, u32[]{:S(2)}) copy-start(bf16[16,192,384]{2,1,0:T(8,128)(2,1)S(1)} %merge.1) | copy-start | bytes 7077892
  7.3 43.0 %all-to-all-start = ((bf16[16,192,384]{2,1,0:T(8,128)(2,1)}), bf16[16,192,384]{2,1,0:T(8,128)(2,1)S(1)}, u32[]{:S(2)}, u32[]{:S(2)}) async-start(bf16[16,192,384]{2,1,0:T(8,128)(2,1)} %copy-done), calls=%async_computation | async-start | bytes 4718592 | tf_op jit(solution)/shard_map/all_to_all | solution.py:431
  15.1 8.1 %collective-permute-start.2 = (bf16[256,256]{1,0:T(8,128)(2,1)S(1)}, bf16[256,256]{1,0:T(8,128)(2,1)S(1)}, u32[]{:S(2)}, u32[]{:S(2)}) collective-permute-start(bf16[256,256]{1,0:T(8,128)(2,1)S(1)} %dynamic_slice.12), channel_id=1, source_target_pairs={{0,65},{1,64},{64,1},{65,0},{2,67},{3,66},{66,3},{67,2},{4,69},{5,... | collective-permute-start | bytes 393224 | tf_op jit(solution)/shard_map/ppermute | solution.py:407
  18.9 6.9 %copy-start.16 = (s32[31,2]{0,1:T(2,128)S(1)}, s32[31,2]{0,1:T(2,128)}, u32[]{:S(2)}) copy-start(s32[31,2]{0,1:T(2,128)} %param.12) | copy-start | bytes 748
  18.9 7.1 %copy-start.14 = (s32[48]{0:T(128)S(1)}, s32[48]{0:T(128)}, u32[]{:S(2)}) copy-start(s32[48]{0:T(128)} %param.13) | copy-start | bytes 580
  18.9 7.2 %copy-start.15 = (s32[6]{0:T(128)S(1)}, s32[6]{0:T(128)}, u32[]{:S(2)}) copy-start(s32[6]{0:T(128)} %param.11) | copy-start | bytes 76
  20.9 29.4 %collective-permute-start.6 = (bf16[256,1280]{1,0:T(8,128)(2,1)}, bf16[256,1280]{1,0:T(8,128)(2,1)}, u32[]{:S(2)}, u32[]{:S(2)}) collective-permute-start(bf16[256,1280]{1,0:T(8,128)(2,1)} %dynamic_slice.13), channel_id=1, source_target_pairs={{0,65},{1,64},{64,1},{65,0},{2,67},{3,66},{66,3},{67,2},{4,69},{5,... | collective-permute-start | bytes 1966088 | tf_op jit(solution)/shard_map/ppermute | solution.py:407
  23.2 53.2 %copy-start.7 = (bf16[256,256]{1,0:T(8,128)(2,1)}, bf16[256,256]{1,0:T(8,128)(2,1)S(1)}, u32[]{:S(2)}) copy-start(bf16[256,256]{1,0:T(8,128)(2,1)S(1)} %collective-permute-done.2.refs_0_) | copy-start | bytes 393220
  23.2 27.1 %collective-permute-start.7 = (bf16[1024,256]{1,0:T(8,128)(2,1)}, bf16[1024,256]{1,0:T(8,128)(2,1)}, u32[]{:S(2)}, u32[]{:S(2)}) collective-permute-start(bf16[1024,256]{1,0:T(8,128)(2,1)} %get-tuple-element.44), channel_id=1, source_target_pairs={{0,65},{1,64},{64,1},{65,0},{2,67},{3,66},{66,3},{67,2},{4,69},{5,... | collective-permute-start | bytes 1572872 | tf_op jit(solution)/shard_map/ppermute | solution.py:407
  26.2 4.9 %collective-permute-start.1 = (s32[116]{0:T(128)S(1)}, s32[116]{0:T(128)S(1)}, u32[]{:S(2)}, u32[]{:S(2)}) collective-permute-start(s32[116]{0:T(128)S(1)} %pad_add_fusion.1), channel_id=1, source_target_pairs={{0,32},{32,0},{1,33},{33,1},{2,34},{34,2},{3,35},{35,3},{4,36},{36... | collective-permute-start | bytes 1400 | tf_op jit(solution)/shard_map/ppermute | solution.py:377
  27.7 22.6 %collective-permute-start.3 = (bf16[256,256]{1,0:T(8,128)(2,1)S(1)}, bf16[256,256]{1,0:T(8,128)(2,1)S(1)}, u32[]{:S(2)}, u32[]{:S(2)}) collective-permute-start(bf16[256,256]{1,0:T(8,128)(2,1)S(1)} %collective-permute-done.2.refs_0_), channel_id=1, source_target_pairs={{0,6},{32,56},{2,0},{34,58},{4,2},{36,60},{6,4},{38,62},{8,14},{40... | collective-permute-start | bytes 393224 | tf_op jit(solution)/shard_map/ppermute | solution.py:396
  30.5 19.8 %collective-permute-start.4 = (bf16[256,256]{1,0:T(8,128)(2,1)S(1)}, bf16[256,256]{1,0:T(8,128)(2,1)}, u32[]{:S(2)}, u32[]{:S(2)}) collective-permute-start(bf16[256,256]{1,0:T(8,128)(2,1)S(1)} %collective-permute-done.2.refs_0_), channel_id=1, source_target_pairs={{0,4},{32,48},{2,6},{34,50},{4,0},{36,52},{6,2},{38,54},{8,12},{40... | collective-permute-start | bytes 393224 | tf_op jit(solution)/shard_map/ppermute | solution.py:396
  31.1 19.2 %collective-permute-start.5 = (bf16[256,256]{1,0:T(8,128)(2,1)S(1)}, bf16[256,256]{1,0:T(8,128)(2,1)}, u32[]{:S(2)}, u32[]{:S(2)}) collective-permute-start(bf16[256,256]{1,0:T(8,128)(2,1)S(1)} %collective-permute-done.2.refs_0_), channel_id=1, source_target_pairs={{0,2},{32,40},{2,4},{34,42},{4,6},{36,44},{6,0},{38,46},{8,10},{40... | collective-permute-start | bytes 393224 | tf_op jit(solution)/shard_map/ppermute | solution.py:396
  37.1 1.1 %copy-start.1 = (bf16[2,3072,128]{2,1,0:T(8,128)(2,1)}, bf16[2,3072,128]{2,1,0:T(8,128)(2,1)S(1)}, u32[]{:S(2)}) copy-start(bf16[2,3072,128]{2,1,0:T(8,128)(2,1)S(1)} %get-tuple-element.46.kdoc_ref) | copy-start | bytes 4718596
  50.3 7.1 %copy-start.6 = (bf16[1024,256]{1,0:T(8,128)(2,1)S(1)}, bf16[1024,256]{1,0:T(8,128)(2,1)}, u32[]{:S(2)}) copy-start(bf16[1024,256]{1,0:T(8,128)(2,1)} %get-tuple-element.55) | copy-start | bytes 1572868
  50.3 10.9 %copy-start.2 = (bf16[2,3072,128]{2,1,0:T(8,128)(2,1)S(1)}, bf16[2,3072,128]{2,1,0:T(8,128)(2,1)}, u32[]{:S(2)}) copy-start(bf16[2,3072,128]{2,1,0:T(8,128)(2,1)} %copy-done.1) | copy-start | bytes 4718596
  50.3 7.1 %copy-start.9 = (bf16[256,256]{1,0:T(8,128)(2,1)}, bf16[256,256]{1,0:T(8,128)(2,1)S(1)}, u32[]{:S(2)}) copy-start(bf16[256,256]{1,0:T(8,128)(2,1)S(1)} %collective-permute-done.3.refs_1_) | copy-start | bytes 393220
  50.5 10.7 %collective-permute-start.8 = (bf16[3072,256]{1,0:T(8,128)(2,1)S(1)}, bf16[3072,256]{1,0:T(8,128)(2,1)S(1)}, u32[]{:S(2)}, u32[]{:S(2)}) collective-permute-start(bf16[3072,256]{1,0:T(8,128)(2,1)S(1)} %slice.3), channel_id=1, source_target_pairs={{0,32},{32,0},{1,33},{33,1},{2,34},{34,2},{3,35},{35,3},{4,36},{36... | collective-permute-start | bytes 4718600 | tf_op jit(solution)/shard_map/ppermute | solution.py:377
  52.2 24.3 %collective-permute-start.10 = (bf16[256,1280]{1,0:T(8,128)(2,1)}, bf16[256,1280]{1,0:T(8,128)(2,1)}, u32[]{:S(2)}, u32[]{:S(2)}) collective-permute-start(bf16[256,1280]{1,0:T(8,128)(2,1)} %collective-permute-done.6.refs_4_), channel_id=1, source_target_pairs={{0,4},{32,48},{2,6},{34,50},{4,0},{36,52},{6,2},{38,54},{8,12},{40... | collective-permute-start | bytes 1966088 | tf_op jit(solution)/shard_map/ppermute | solution.py:396
  54.7 21.7 %collective-permute-start.11 = (bf16[256,1280]{1,0:T(8,128)(2,1)}, bf16[256,1280]{1,0:T(8,128)(2,1)}, u32[]{:S(2)}, u32[]{:S(2)}) collective-permute-start(bf16[256,1280]{1,0:T(8,128)(2,1)} %collective-permute-done.6.refs_4_), channel_id=1, source_target_pairs={{0,2},{32,40},{2,4},{34,42},{4,6},{36,44},{6,0},{38,46},{8,10},{40... | collective-permute-start | bytes 1966088 | tf_op jit(solution)/shard_map/ppermute | solution.py:396
  54.7 21.7 %collective-permute-start.9 = (bf16[256,1280]{1,0:T(8,128)(2,1)}, bf16[256,1280]{1,0:T(8,128)(2,1)}, u32[]{:S(2)}, u32[]{:S(2)}) collective-permute-start(bf16[256,1280]{1,0:T(8,128)(2,1)} %collective-permute-done.6.refs_4_), channel_id=1, source_target_pairs={{0,6},{32,56},{2,0},{34,58},{4,2},{36,60},{6,4},{38,62},{8,14},{40... | collective-permute-start | bytes 1966088 | tf_op jit(solution)/shard_map/ppermute | solution.py:396
  57.4 19.0 %collective-permute-start.12 = (bf16[1024,256]{1,0:T(8,128)(2,1)S(1)}, bf16[1024,256]{1,0:T(8,128)(2,1)}, u32[]{:S(2)}, u32[]{:S(2)}) collective-permute-start(bf16[1024,256]{1,0:T(8,128)(2,1)S(1)} %copy-done.6), channel_id=1, source_target_pairs={{0,65},{1,64},{64,1},{65,0},{2,67},{3,66},{66,3},{67,2},{4,69},{5,... | collective-permute-start | bytes 1572872 | tf_op jit(solution)/shard_map/ppermute | solution.py:407
  76.4 5.7 %copy-start.10 = (bf16[256,256]{1,0:T(8,128)(2,1)S(1)}, bf16[256,256]{1,0:T(8,128)(2,1)}, u32[]{:S(2)}) copy-start(bf16[256,256]{1,0:T(8,128)(2,1)} %copy-done.9) | copy-start | bytes 393220
  76.4 5.1 %copy-start.8 = (bf16[256,256]{1,0:T(8,128)(2,1)S(1)}, bf16[256,256]{1,0:T(8,128)(2,1)}, u32[]{:S(2)}) copy-start(bf16[256,256]{1,0:T(8,128)(2,1)} %copy-done.7) | copy-start | bytes 393220
  76.5 8.9 %collective-permute-start.22 = (bf16[1024,256]{1,0:T(8,128)(2,1)}, bf16[1024,256]{1,0:T(8,128)(2,1)S(1)}, u32[]{:S(2)}, u32[]{:S(2)}) collective-permute-start(bf16[1024,256]{1,0:T(8,128)(2,1)} %collective-permute-done.7.refs_8_), channel_id=1, source_target_pairs={{0,32},{32,0},{1,33},{33,1},{2,34},{34,2},{3,35},{35,3},{4,36},{36... | collective-permute-start | bytes 1572872 | tf_op jit(solution)/shard_map/ppermute | solution.py:377
  76.6 19.8 %all-to-all-start.1 = ((bf16[32,3,32,128]{3,2,1,0:T(8,128)(2,1)}), bf16[32,3,32,128]{3,2,1,0:T(8,128)(2,1)S(1)}, u32[]{:S(2)}, u32[]{:S(2)}) async-start(bf16[32,3,32,128]{3,2,1,0:T(8,128)(2,1)} %bitcast.5), calls=%async_computation.1 | async-start | bytes 1572864 | tf_op jit(solution)/shard_map/all_to_all | solution.py:442
  81.5 1.4 %collective-permute-start.14 = (bf16[256,256]{1,0:T(8,128)(2,1)S(1)}, bf16[256,256]{1,0:T(8,128)(2,1)S(1)}, u32[]{:S(2)}, u32[]{:S(2)}) collective-permute-start(bf16[256,256]{1,0:T(8,128)(2,1)S(1)} %copy-done.8), channel_id=1, source_target_pairs={{0,32},{32,0},{1,33},{33,1},{2,34},{34,2},{3,35},{35,3},{4,36},{36... | collective-permute-start | bytes 393224 | tf_op jit(solution)/shard_map/ppermute | solution.py:377
  81.9 14.5 %collective-permute-start.23 = (bf16[1024,256]{1,0:T(8,128)(2,1)}, bf16[1024,256]{1,0:T(8,128)(2,1)}, u32[]{:S(2)}, u32[]{:S(2)}) collective-permute-start(bf16[1024,256]{1,0:T(8,128)(2,1)} %collective-permute-done.12.refs_9_), channel_id=1, source_target_pairs={{0,32},{32,0},{1,33},{33,1},{2,34},{34,2},{3,35},{35,3},{4,36},{36... | collective-permute-start | bytes 1572872 | tf_op jit(solution)/shard_map/ppermute | solution.py:377
  82.1 2.1 %collective-permute-start.15 = (bf16[256,256]{1,0:T(8,128)(2,1)S(1)}, bf16[256,256]{1,0:T(8,128)(2,1)S(1)}, u32[]{:S(2)}, u32[]{:S(2)}) collective-permute-start(bf16[256,256]{1,0:T(8,128)(2,1)S(1)} %copy-done.10), channel_id=1, source_target_pairs={{0,32},{32,0},{1,33},{33,1},{2,34},{34,2},{3,35},{35,3},{4,36},{36... | collective-permute-start | bytes 393224 | tf_op jit(solution)/shard_map/ppermute | solution.py:377
  82.4 2.4 %collective-permute-start.16 = (bf16[256,256]{1,0:T(8,128)(2,1)}, bf16[256,256]{1,0:T(8,128)(2,1)}, u32[]{:S(2)}, u32[]{:S(2)}) collective-permute-start(bf16[256,256]{1,0:T(8,128)(2,1)} %collective-permute-done.4.refs_2_), channel_id=1, source_target_pairs={{0,32},{32,0},{1,33},{33,1},{2,34},{34,2},{3,35},{35,3},{4,36},{36... | collective-permute-start | bytes 393224 | tf_op jit(solution)/shard_map/ppermute | solution.py:377
  82.9 1.5 %copy-start.11 = (bf16[256,256]{1,0:T(8,128)(2,1)}, bf16[256,256]{1,0:T(8,128)(2,1)S(1)}, u32[]{:S(2)}) copy-start(bf16[256,256]{1,0:T(8,128)(2,1)S(1)} %collective-permute-done.14.refs_10_) | copy-start | bytes 393220
  82.9 2.1 %collective-permute-start.17 = (bf16[256,256]{1,0:T(8,128)(2,1)}, bf16[256,256]{1,0:T(8,128)(2,1)S(1)}, u32[]{:S(2)}, u32[]{:S(2)}) collective-permute-start(bf16[256,256]{1,0:T(8,128)(2,1)} %collective-permute-done.5.refs_3_), channel_id=1, source_target_pairs={{0,32},{32,0},{1,33},{33,1},{2,34},{34,2},{3,35},{35,3},{4,36},{36... | collective-permute-start | bytes 393224 | tf_op jit(solution)/shard_map/ppermute | solution.py:377
  84.2 0.7 copy-start.12
  84.2 14.4 %collective-permute-start.18 = (bf16[256,1280]{1,0:T(8,128)(2,1)}, bf16[256,1280]{1,0:T(8,128)(2,1)S(1)}, u32[]{:S(2)}, u32[]{:S(2)}) collective-permute-start(bf16[256,1280]{1,0:T(8,128)(2,1)} %collective-permute-done.6.refs_4_), channel_id=1, source_target_pairs={{0,32},{32,0},{1,33},{33,1},{2,34},{34,2},{3,35},{35,3},{4,36},{36... | collective-permute-start | bytes 1966088 | tf_op jit(solution)/shard_map/ppermute | solution.py:377
  84.8 13.7 %collective-permute-start.19 = (bf16[256,1280]{1,0:T(8,128)(2,1)}, bf16[256,1280]{1,0:T(8,128)(2,1)S(1)}, u32[]{:S(2)}, u32[]{:S(2)}) collective-permute-start(bf16[256,1280]{1,0:T(8,128)(2,1)} %collective-permute-done.9.refs_5_), channel_id=1, source_target_pairs={{0,32},{32,0},{1,33},{33,1},{2,34},{34,2},{3,35},{35,3},{4,36},{36... | collective-permute-start | bytes 1966088 | tf_op jit(solution)/shard_map/ppermute | solution.py:377
  85.0 11.3 %copy-start.13 = (bf16[256,256]{1,0:T(8,128)(2,1)}, bf16[256,256]{1,0:T(8,128)(2,1)S(1)}, u32[]{:S(2)}) copy-start(bf16[256,256]{1,0:T(8,128)(2,1)S(1)} %collective-permute-done.17.refs_13_) | copy-start | bytes 393220
  85.0 13.5 %collective-permute-start.20 = (bf16[256,1280]{1,0:T(8,128)(2,1)}, bf16[256,1280]{1,0:T(8,128)(2,1)}, u32[]{:S(2)}, u32[]{:S(2)}) collective-permute-start(bf16[256,1280]{1,0:T(8,128)(2,1)} %collective-permute-done.10.refs_6_), channel_id=1, source_target_pairs={{0,32},{32,0},{1,33},{33,1},{2,34},{34,2},{3,35},{35,3},{4,36},{36... | collective-permute-start | bytes 1966088 | tf_op jit(solution)/shard_map/ppermute | solution.py:377
  85.3 14.4 %copy-start.5 = (bf16[1024,256]{1,0:T(8,128)(2,1)}, bf16[1024,256]{1,0:T(8,128)(2,1)S(1)}, u32[]{:S(2)}) copy-start(bf16[1024,256]{1,0:T(8,128)(2,1)S(1)} %collective-permute-done.22.refs_18_) | copy-start | bytes 1572868
  85.3 13.2 %collective-permute-start.21 = (bf16[256,1280]{1,0:T(8,128)(2,1)}, bf16[256,1280]{1,0:T(8,128)(2,1)}, u32[]{:S(2)}, u32[]{:S(2)}) collective-permute-start(bf16[256,1280]{1,0:T(8,128)(2,1)} %collective-permute-done.11.refs_7_), channel_id=1, source_target_pairs={{0,32},{32,0},{1,33},{33,1},{2,34},{34,2},{3,35},{35,3},{4,36},{36... | collective-permute-start | bytes 1966088 | tf_op jit(solution)/shard_map/ppermute | solution.py:377
  96.4 3.3 %collective-permute-start.13 = (bf16[2,8,3,32,128]{4,3,2,1,0:T(8,128)(2,1)S(1)}, bf16[2,8,3,32,128]{4,3,2,1,0:T(8,128)(2,1)S(1)}, u32[]{:S(2)}, u32[]{:S(2)}) collective-permute-start(bf16[2,8,3,32,128]{4,3,2,1,0:T(8,128)(2,1)S(1)} %pick.1), channel_id=1, source_target_pairs={{0,32},{32,0},{1,33},{33,1},{2,34},{34,2},{3,35},{35,3},{4,36},{36... | collective-permute-start | bytes 1179656 | tf_op jit(solution)/shard_map/ppermute | solution.py:377
  98.5 1.2 %copy-start.3 = (bf16[256,1280]{1,0:T(8,128)(2,1)}, bf16[256,1280]{1,0:T(8,128)(2,1)S(1)}, u32[]{:S(2)}) copy-start(bf16[256,1280]{1,0:T(8,128)(2,1)S(1)} %collective-permute-done.18.refs_14_) | copy-start | bytes 1966084
  98.5 1.2 %copy-start.4 = (bf16[256,1280]{1,0:T(8,128)(2,1)}, bf16[256,1280]{1,0:T(8,128)(2,1)S(1)}, u32[]{:S(2)}) copy-start(bf16[256,1280]{1,0:T(8,128)(2,1)S(1)} %collective-permute-done.19.refs_15_) | copy-start | bytes 1966084

commit v6 on v5

--- a/solution.py
+++ b/solution.py
@@ -212,7 +212,7 @@
                 acc = acc + lax.dot_general(
                     value, p, (((0,), (0,)), ((), ())), preferred_element_type=F32
                 )
-            out = jnp.transpose(acc / l).astype(BF)
+            out = jnp.transpose(acc * (1.0 / l)).astype(BF)
             for b in range(TILE):
                 slot = meta_ref[NTILE + j * TILE + b]
                 chip = slot // CHIP_BLOCKS

time: 110 us -> 110 us (level)
  transfers between devices with their start and end apart: 26 -> 26, of which waited for: 6 -> 6; matrix products, arithmetic and copies ran while one was open for 5% -> 5% of each run, Pallas kernels for 19% -> 18%
where the time goes in v6:
time: 110 us
  starting transfers between devices  41.2 us (37%)
  Pallas kernels  31.4 us (29%)
  waiting for transfers between devices  27.7 us (25%)
  local copies, waits for them, and re-layouts  8.51 us (8%)
    pallas_call x1, Pallas kernels, attend(): pl.pallas_call(attend_kernel, out_shape=jax.ShapeDtypeStruct((2, NCTX, 3,...  14.5 us
    all_to_all x1, waiting for transfers between devices, shards(): y = lax.all_to_all(x, CTX, 0, 0, tiled=True).reshape(ROWS, 3 * HD)  12 us
    all_to_all x1, waiting for transfers between devices, shards(): lax.all_to_all(att.reshape(2 * NCTX, 3, QTR, HD), ('tensor',) + CTX, 0, 0...  10.8 us
    ppermute x4, starting transfers between devices, shards(): from_z = lambda x: lax.ppermute(x, ('z_lo', 'tensor'), across)  10.3 us
    pallas_call x1, Pallas kernels, project(): pl.pallas_call(project_kernel, in_specs=[pl.BlockSpec(memory_space=pltpu....  9.74 us
    ppermute x6, starting transfers between devices, along_line(): return lax.ppermute(x, ('core',) + CTX, pairs)  9.23 us
    ppermute x14, starting transfers between devices, swap(): return lax.ppermute(x, 'core', SWAP)  9.11 us
    all_to_all x1, starting transfers between devices, shards(): y = lax.all_to_all(x, CTX, 0, 0, tiled=True).reshape(ROWS, 3 * HD)  6.84 us
  transfers between devices with their start and end apart: 26, of which 6 were waited for; matrix products, arithmetic and copies ran while one was open for 5% of the time, Pallas kernels for 18%

profile of v6, /device:TPU:1, one launch (start us, length us, event | category | flops | bytes accessed | tf_op | source)
XLA Modules:
  0.0 109.6 jit_solution(13534282177214005409)
XLA Ops:
  0.0 1.7 %pack.1 = (bf16[8,192,384]{2,1,0:T(8,128)(2,1)S(1)}, bf16[8,192,384]{2,1,0:T(8,128)(2,1)S(1)}) custom-call(s32[1]{0:T(128)} %bitcast.core_ref, bf16[384,1024]{1,0:T(8,128)(2,1)} %q_hbm.1, bf16[384,1024]{1,0:T(8,128)(2,1)} %k_hbm.1, bf16[384,1024]{1,0:T(8,128)(2,1)} %v_hbm.1), custom_call_target="tpu_custom_call" | custom-call | tf_op jit(solution)/shard_map/pack/pallas_call | solution.py:58
  1.7 1.5 %collective-permute-start = (bf16[8,192,384]{2,1,0:T(8,128)(2,1)S(1)}, bf16[8,192,384]{2,1,0:T(8,128)(2,1)S(1)}, u32[]{:S(2)}, u32[]{:S(2)}) collective-permute-start(bf16[8,192,384]{2,1,0:T(8,128)(2,1)S(1)} %get-tuple-element.37), channel_id=1, source_target_pairs={{0,32},{32,0},{1,33},{33,1},{2,34},{34,2},{3,35},{35,3},{4,36},{36... | collective-permute-start | bytes 3538952 | tf_op jit(solution)/shard_map/ppermute | solution.py:377
  3.2 2.5 %collective-permute-done.recv_ref = bf16[8,192,384]{2,1,0:T(8,128)(2,1)S(1)} collective-permute-done((bf16[8,192,384]{2,1,0:T(8,128)(2,1)S(1)}, bf16[8,192,384]{2,1,0:T(8,128)(2,1)S(1)}, u32[]{:S(2)}, u32[]{:S(2)}) %collective-permute-start) | collective-permute-done | bytes 1179680 | tf_op jit(solution)/shard_map/ppermute | solution.py:377
  5.7 0.2 merge.1
  5.9 1.4 %copy-done = bf16[16,192,384]{2,1,0:T(8,128)(2,1)} copy-done((bf16[16,192,384]{2,1,0:T(8,128)(2,1)}, bf16[16,192,384]{2,1,0:T(8,128)(2,1)S(1)}, u32[]{:S(2)}) %copy-start) | copy-done | bytes 2359320
  7.3 6.8 %all-to-all-start = ((bf16[16,192,384]{2,1,0:T(8,128)(2,1)}), bf16[16,192,384]{2,1,0:T(8,128)(2,1)S(1)}, u32[]{:S(2)}, u32[]{:S(2)}) async-start(bf16[16,192,384]{2,1,0:T(8,128)(2,1)} %copy-done), calls=%async_computation | async-start | bytes 4718592 | tf_op jit(solution)/shard_map/all_to_all | solution.py:431
  14.2 0.9 dynamic_slice.12
  15.1 3.8 %collective-permute-start.2 = (bf16[256,256]{1,0:T(8,128)(2,1)S(1)}, bf16[256,256]{1,0:T(8,128)(2,1)S(1)}, u32[]{:S(2)}, u32[]{:S(2)}) collective-permute-start(bf16[256,256]{1,0:T(8,128)(2,1)S(1)} %dynamic_slice.12), channel_id=1, source_target_pairs={{0,65},{1,64},{64,1},{65,0},{2,67},{3,66},{66,3},{67,2},{4,69},{5,... | collective-permute-start | bytes 393224 | tf_op jit(solution)/shard_map/ppermute | solution.py:407
  18.9 2.0 %dynamic_slice.13 = bf16[256,1280]{1,0:T(8,128)(2,1)} dynamic-slice(bf16[1024,4096]{1,0:T(8,128)(2,1)} %w_ref.1, s32[]{:T(128)S(6)} %select_n.46, s32[]{:T(128)S(6)} %select_n.48), dynamic_slice_sizes={256,1280} | dynamic-slice | bytes 1310724 | tf_op jit(solution)/shard_map/dynamic_slice | solution.py:413
  21.0 2.2 %constant_dynamic-slice_fusion = (bf16[1024,256]{1,0:T(8,128)(2,1)}, bf16[1024,256]{1,0:T(8,128)(2,1)}) fusion(bf16[1024,4096]{1,0:T(8,128)(2,1)} %w_ref.1, s32[]{:T(128)S(6)} %select_n.50, s32[]{:T(128)S(6)} %select_n.49), kind=kLoop, calls=%fused_computation.5 | loop fusion | bytes 2097160 | tf_op jit(solution)/shard_map/dynamic_slice | solution.py:417
  23.2 2.7 %collective-permute-start.7 = (bf16[1024,256]{1,0:T(8,128)(2,1)}, bf16[1024,256]{1,0:T(8,128)(2,1)}, u32[]{:S(2)}, u32[]{:S(2)}) collective-permute-start(bf16[1024,256]{1,0:T(8,128)(2,1)} %get-tuple-element.44), channel_id=1, source_target_pairs={{0,65},{1,64},{64,1},{65,0},{2,67},{3,66},{66,3},{67,2},{4,69},{5,... | collective-permute-start | bytes 1572872 | tf_op jit(solution)/shard_map/ppermute | solution.py:407
  25.9 0.1 copy.9
  26.0 0.1 reshape.13
  26.1 0.1 pad_add_fusion.1
  26.2 1.5 %collective-permute-start.1 = (s32[116]{0:T(128)S(1)}, s32[116]{0:T(128)S(1)}, u32[]{:S(2)}, u32[]{:S(2)}) collective-permute-start(s32[116]{0:T(128)S(1)} %pad_add_fusion.1), channel_id=1, source_target_pairs={{0,32},{32,0},{1,33},{33,1},{2,34},{34,2},{3,35},{35,3},{4,36},{36... | collective-permute-start | bytes 1400 | tf_op jit(solution)/shard_map/ppermute | solution.py:377
  27.7 2.8 %collective-permute-start.3 = (bf16[256,256]{1,0:T(8,128)(2,1)S(1)}, bf16[256,256]{1,0:T(8,128)(2,1)S(1)}, u32[]{:S(2)}, u32[]{:S(2)}) collective-permute-start(bf16[256,256]{1,0:T(8,128)(2,1)S(1)} %collective-permute-done.2.refs_0_), channel_id=1, source_target_pairs={{0,6},{32,56},{2,0},{34,58},{4,2},{36,60},{6,4},{38,62},{8,14},{40... | collective-permute-start | bytes 393224 | tf_op jit(solution)/shard_map/ppermute | solution.py:396
  30.5 0.6 collective-permute-start.4
  31.1 0.6 collective-permute-start.5
  31.7 0.1 broadcast_select_fusion
  31.8 0.1 pad_add_fusion.2.ints_ref
  31.8 5.3 %prepare.1 = (bf16[2,3072,128]{2,1,0:T(8,128)(2,1)S(1)}, bf16[3072,128]{1,0:T(8,128)(2,1)S(1)}, s32[12,8,256]{2,1,0:T(8,128)S(1)}, s32[60]{0:T(128)S(1)}) custom-call(s32[117]{0:T(128)S(1)} %pad_add_fusion.2.ints_ref), custom_call_target="tpu_custom_call" | custom-call | tf_op jit(solution)/shard_map/prepare/pallas_call | solution.py:153
  37.2 1.1 %copy-done.1 = bf16[2,3072,128]{2,1,0:T(8,128)(2,1)} copy-done((bf16[2,3072,128]{2,1,0:T(8,128)(2,1)}, bf16[2,3072,128]{2,1,0:T(8,128)(2,1)S(1)}, u32[]{:S(2)}) %copy-start.1) | copy-done | bytes 1572888
  38.3 12.0 %all-to-all-done = bf16[16,192,384]{2,1,0:T(8,128)(2,1)S(1)} async-done(((bf16[16,192,384]{2,1,0:T(8,128)(2,1)}), bf16[16,192,384]{2,1,0:T(8,128)(2,1)S(1)}, u32[]{:S(2)}, u32[]{:S(2)}) %all-to-all-start) | async-done | bytes 2359328 | tf_op jit(solution)/shard_map/all_to_all | solution.py:431
  50.3 0.1 slice.3
  50.5 1.7 %collective-permute-start.8 = (bf16[3072,256]{1,0:T(8,128)(2,1)S(1)}, bf16[3072,256]{1,0:T(8,128)(2,1)S(1)}, u32[]{:S(2)}, u32[]{:S(2)}) collective-permute-start(bf16[3072,256]{1,0:T(8,128)(2,1)S(1)} %slice.3), channel_id=1, source_target_pairs={{0,32},{32,0},{1,33},{33,1},{2,34},{34,2},{3,35},{35,3},{4,36},{36... | collective-permute-start | bytes 4718600 | tf_op jit(solution)/shard_map/ppermute | solution.py:377
  52.2 2.6 %collective-permute-start.10 = (bf16[256,1280]{1,0:T(8,128)(2,1)}, bf16[256,1280]{1,0:T(8,128)(2,1)}, u32[]{:S(2)}, u32[]{:S(2)}) collective-permute-start(bf16[256,1280]{1,0:T(8,128)(2,1)} %collective-permute-done.6.refs_4_), channel_id=1, source_target_pairs={{0,4},{32,48},{2,6},{34,50},{4,0},{36,52},{6,2},{38,54},{8,12},{40... | collective-permute-start | bytes 1966088 | tf_op jit(solution)/shard_map/ppermute | solution.py:396
  54.7 2.7 %collective-permute-start.9 = (bf16[256,1280]{1,0:T(8,128)(2,1)}, bf16[256,1280]{1,0:T(8,128)(2,1)}, u32[]{:S(2)}, u32[]{:S(2)}) collective-permute-start(bf16[256,1280]{1,0:T(8,128)(2,1)} %collective-permute-done.6.refs_4_), channel_id=1, source_target_pairs={{0,6},{32,56},{2,0},{34,58},{4,2},{36,60},{6,4},{38,62},{8,14},{40... | collective-permute-start | bytes 1966088 | tf_op jit(solution)/shard_map/ppermute | solution.py:396
  57.4 3.8 %collective-permute-start.12 = (bf16[1024,256]{1,0:T(8,128)(2,1)S(1)}, bf16[1024,256]{1,0:T(8,128)(2,1)}, u32[]{:S(2)}, u32[]{:S(2)}) collective-permute-start(bf16[1024,256]{1,0:T(8,128)(2,1)S(1)} %copy-done.6), channel_id=1, source_target_pairs={{0,65},{1,64},{64,1},{65,0},{2,67},{3,66},{66,3},{67,2},{4,69},{5,... | collective-permute-start | bytes 1572872 | tf_op jit(solution)/shard_map/ppermute | solution.py:407
  61.2 14.5 %attend.1 = bf16[2,16,3,32,128]{4,3,2,1,0:T(8,128)(2,1)} custom-call(s32[1]{0:T(128)} %bitcast.core_ref, s32[60]{0:T(128)S(1)} %get-tuple-element.42.meta_ref, bf16[3072,384]{1,0:T(8,128)(2,1)S(1)} %bitcast.8, bf16[3072,256]{1,0:T(8,128)(2,1)S(1)} %collective-permute-done.8.kvo_ref, bf16[2,3072,128]{2,1,0:T(8,128)(2,1)S(1)} %copy-done.2, ...), custom_call_target="tpu_custom_call" | custom-call | tf_op jit(solution)/shard_map/attend/pallas_call | solution.py:237
  75.7 0.1 collective-permute-start.22
  75.8 5.7 %all-to-all-start.1 = ((bf16[32,3,32,128]{3,2,1,0:T(8,128)(2,1)}), bf16[32,3,32,128]{3,2,1,0:T(8,128)(2,1)S(1)}, u32[]{:S(2)}, u32[]{:S(2)}) async-start(bf16[32,3,32,128]{3,2,1,0:T(8,128)(2,1)} %bitcast.5), calls=%async_computation.1 | async-start | bytes 1572864 | tf_op jit(solution)/shard_map/all_to_all | solution.py:442
  81.5 0.4 collective-permute-start.14
  81.9 0.2 collective-permute-start.23
  82.1 0.3 collective-permute-start.15
  82.4 0.2 collective-permute-start.16
  82.6 0.3 collective-permute-done.14.refs_10_
  82.9 0.3 collective-permute-start.17
  83.2 0.9 collective-permute-done.15.refs_11_
  84.2 0.2 collective-permute-start.18
  84.4 0.4 copy-done.12
  84.8 0.2 collective-permute-start.19
  85.0 0.3 collective-permute-start.20
  85.3 0.2 collective-permute-start.21
  85.6 10.8 %all-to-all-done.1 = bf16[32,3,32,128]{3,2,1,0:T(8,128)(2,1)S(1)} async-done(((bf16[32,3,32,128]{3,2,1,0:T(8,128)(2,1)}), bf16[32,3,32,128]{3,2,1,0:T(8,128)(2,1)S(1)}, u32[]{:S(2)}, u32[]{:S(2)}) %all-to-all-start.1) | async-done | bytes 786464 | tf_op jit(solution)/shard_map/all_to_all | solution.py:442
  96.4 1.9 %collective-permute-start.13 = (bf16[2,8,3,32,128]{4,3,2,1,0:T(8,128)(2,1)S(1)}, bf16[2,8,3,32,128]{4,3,2,1,0:T(8,128)(2,1)S(1)}, u32[]{:S(2)}, u32[]{:S(2)}) collective-permute-start(bf16[2,8,3,32,128]{4,3,2,1,0:T(8,128)(2,1)S(1)} %pick.1), channel_id=1, source_target_pairs={{0,32},{32,0},{1,33},{33,1},{2,34},{34,2},{3,35},{35,3},{4,36},{36... | collective-permute-start | bytes 1179656 | tf_op jit(solution)/shard_map/ppermute | solution.py:377
  98.4 0.1 pad_add_fusion.ids_ref
  98.6 1.1 %collective-permute-done.13.zo_ref = bf16[2,8,3,32,128]{4,3,2,1,0:T(8,128)(2,1)S(1)} collective-permute-done((bf16[2,8,3,32,128]{4,3,2,1,0:T(8,128)(2,1)S(1)}, bf16[2,8,3,32,128]{4,3,2,1,0:T(8,128)(2,1)S(1)}, u32[]{:S(2)}, u32[]{:S(2)}) %collective-permute-start.13) | collective-permute-done | bytes 393248 | tf_op jit(solution)/shard_map/ppermute | solution.py:377
  99.7 9.7 %project.1 = bf16[192,4096]{1,0:T(8,128)(2,1)} custom-call(s32[4]{0:T(128)S(1)} %pad_add_fusion.ids_ref, bf16[2,16,3,32,128]{4,3,2,1,0:T(8,128)(2,1)S(1)} %bitcast.10, bf16[2,8,3,32,128]{4,3,2,1,0:T(8,128)(2,1)S(1)} %collective-permute-done.13.zo_ref, bf16[1024,4096]{1,0:T(8,128)(2,1)} %w_ref.1, bf16[256,256]{1,0:T(8,128)(2,1)} %copy-done.7, ...), custom_call_target="tpu_custom_call" | custom-call | tf_op jit(solution)/shard_map/project/pallas_call | solution.py:339
  (55 shorter events, 0.2 us)
Async XLA Ops:
  1.7 4.0 %collective-permute-start = (bf16[8,192,384]{2,1,0:T(8,128)(2,1)S(1)}, bf16[8,192,384]{2,1,0:T(8,128)(2,1)S(1)}, u32[]{:S(2)}, u32[]{:S(2)}) collective-permute-start(bf16[8,192,384]{2,1,0:T(8,128)(2,1)S(1)} %get-tuple-element.37), channel_id=1, source_target_pairs={{0,32},{32,0},{1,33},{33,1},{2,34},{34,2},{3,35},{35,3},{4,36},{36... | collective-permute-start | bytes 3538952 | tf_op jit(solution)/shard_map/ppermute | solution.py:377
  5.9 1.4 %copy-start = (bf16[16,192,384]{2,1,0:T(8,128)(2,1)}, bf16[16,192,384]{2,1,0:T(8,128)(2,1)S(1)}, u32[]{:S(2)}) copy-start(bf16[16,192,384]{2,1,0:T(8,128)(2,1)S(1)} %merge.1) | copy-start | bytes 7077892
  7.3 43.0 %all-to-all-start = ((bf16[16,192,384]{2,1,0:T(8,128)(2,1)}), bf16[16,192,384]{2,1,0:T(8,128)(2,1)S(1)}, u32[]{:S(2)}, u32[]{:S(2)}) async-start(bf16[16,192,384]{2,1,0:T(8,128)(2,1)} %copy-done), calls=%async_computation | async-start | bytes 4718592 | tf_op jit(solution)/shard_map/all_to_all | solution.py:431
  15.1 8.1 %collective-permute-start.2 = (bf16[256,256]{1,0:T(8,128)(2,1)S(1)}, bf16[256,256]{1,0:T(8,128)(2,1)S(1)}, u32[]{:S(2)}, u32[]{:S(2)}) collective-permute-start(bf16[256,256]{1,0:T(8,128)(2,1)S(1)} %dynamic_slice.12), channel_id=1, source_target_pairs={{0,65},{1,64},{64,1},{65,0},{2,67},{3,66},{66,3},{67,2},{4,69},{5,... | collective-permute-start | bytes 393224 | tf_op jit(solution)/shard_map/ppermute | solution.py:407
  18.9 6.9 %copy-start.16 = (s32[31,2]{0,1:T(2,128)S(1)}, s32[31,2]{0,1:T(2,128)}, u32[]{:S(2)}) copy-start(s32[31,2]{0,1:T(2,128)} %param.12) | copy-start | bytes 748
  18.9 7.1 %copy-start.14 = (s32[48]{0:T(128)S(1)}, s32[48]{0:T(128)}, u32[]{:S(2)}) copy-start(s32[48]{0:T(128)} %param.13) | copy-start | bytes 580
  18.9 7.2 %copy-start.15 = (s32[6]{0:T(128)S(1)}, s32[6]{0:T(128)}, u32[]{:S(2)}) copy-start(s32[6]{0:T(128)} %param.11) | copy-start | bytes 76
  20.9 29.4 %collective-permute-start.6 = (bf16[256,1280]{1,0:T(8,128)(2,1)}, bf16[256,1280]{1,0:T(8,128)(2,1)}, u32[]{:S(2)}, u32[]{:S(2)}) collective-permute-start(bf16[256,1280]{1,0:T(8,128)(2,1)} %dynamic_slice.13), channel_id=1, source_target_pairs={{0,65},{1,64},{64,1},{65,0},{2,67},{3,66},{66,3},{67,2},{4,69},{5,... | collective-permute-start | bytes 1966088 | tf_op jit(solution)/shard_map/ppermute | solution.py:407
  23.2 52.4 %copy-start.7 = (bf16[256,256]{1,0:T(8,128)(2,1)}, bf16[256,256]{1,0:T(8,128)(2,1)S(1)}, u32[]{:S(2)}) copy-start(bf16[256,256]{1,0:T(8,128)(2,1)S(1)} %collective-permute-done.2.refs_0_) | copy-start | bytes 393220
  23.2 27.1 %collective-permute-start.7 = (bf16[1024,256]{1,0:T(8,128)(2,1)}, bf16[1024,256]{1,0:T(8,128)(2,1)}, u32[]{:S(2)}, u32[]{:S(2)}) collective-permute-start(bf16[1024,256]{1,0:T(8,128)(2,1)} %get-tuple-element.44), channel_id=1, source_target_pairs={{0,65},{1,64},{64,1},{65,0},{2,67},{3,66},{66,3},{67,2},{4,69},{5,... | collective-permute-start | bytes 1572872 | tf_op jit(solution)/shard_map/ppermute | solution.py:407
  26.2 4.9 %collective-permute-start.1 = (s32[116]{0:T(128)S(1)}, s32[116]{0:T(128)S(1)}, u32[]{:S(2)}, u32[]{:S(2)}) collective-permute-start(s32[116]{0:T(128)S(1)} %pad_add_fusion.1), channel_id=1, source_target_pairs={{0,32},{32,0},{1,33},{33,1},{2,34},{34,2},{3,35},{35,3},{4,36},{36... | collective-permute-start | bytes 1400 | tf_op jit(solution)/shard_map/ppermute | solution.py:377
  27.7 22.6 %collective-permute-start.3 = (bf16[256,256]{1,0:T(8,128)(2,1)S(1)}, bf16[256,256]{1,0:T(8,128)(2,1)S(1)}, u32[]{:S(2)}, u32[]{:S(2)}) collective-permute-start(bf16[256,256]{1,0:T(8,128)(2,1)S(1)} %collective-permute-done.2.refs_0_), channel_id=1, source_target_pairs={{0,6},{32,56},{2,0},{34,58},{4,2},{36,60},{6,4},{38,62},{8,14},{40... | collective-permute-start | bytes 393224 | tf_op jit(solution)/shard_map/ppermute | solution.py:396
  30.5 19.8 %collective-permute-start.4 = (bf16[256,256]{1,0:T(8,128)(2,1)S(1)}, bf16[256,256]{1,0:T(8,128)(2,1)}, u32[]{:S(2)}, u32[]{:S(2)}) collective-permute-start(bf16[256,256]{1,0:T(8,128)(2,1)S(1)} %collective-permute-done.2.refs_0_), channel_id=1, source_target_pairs={{0,4},{32,48},{2,6},{34,50},{4,0},{36,52},{6,2},{38,54},{8,12},{40... | collective-permute-start | bytes 393224 | tf_op jit(solution)/shard_map/ppermute | solution.py:396
  31.1 19.2 %collective-permute-start.5 = (bf16[256,256]{1,0:T(8,128)(2,1)S(1)}, bf16[256,256]{1,0:T(8,128)(2,1)}, u32[]{:S(2)}, u32[]{:S(2)}) collective-permute-start(bf16[256,256]{1,0:T(8,128)(2,1)S(1)} %collective-permute-done.2.refs_0_), channel_id=1, source_target_pairs={{0,2},{32,40},{2,4},{34,42},{4,6},{36,44},{6,0},{38,46},{8,10},{40... | collective-permute-start | bytes 393224 | tf_op jit(solution)/shard_map/ppermute | solution.py:396
  37.1 1.1 %copy-start.1 = (bf16[2,3072,128]{2,1,0:T(8,128)(2,1)}, bf16[2,3072,128]{2,1,0:T(8,128)(2,1)S(1)}, u32[]{:S(2)}) copy-start(bf16[2,3072,128]{2,1,0:T(8,128)(2,1)S(1)} %get-tuple-element.46.kdoc_ref) | copy-start | bytes 4718596
  50.3 7.1 %copy-start.6 = (bf16[1024,256]{1,0:T(8,128)(2,1)S(1)}, bf16[1024,256]{1,0:T(8,128)(2,1)}, u32[]{:S(2)}) copy-start(bf16[1024,256]{1,0:T(8,128)(2,1)} %get-tuple-element.55) | copy-start | bytes 1572868
  50.3 10.9 %copy-start.2 = (bf16[2,3072,128]{2,1,0:T(8,128)(2,1)S(1)}, bf16[2,3072,128]{2,1,0:T(8,128)(2,1)}, u32[]{:S(2)}) copy-start(bf16[2,3072,128]{2,1,0:T(8,128)(2,1)} %copy-done.1) | copy-start | bytes 4718596
  50.3 7.1 %copy-start.9 = (bf16[256,256]{1,0:T(8,128)(2,1)}, bf16[256,256]{1,0:T(8,128)(2,1)S(1)}, u32[]{:S(2)}) copy-start(bf16[256,256]{1,0:T(8,128)(2,1)S(1)} %collective-permute-done.3.refs_1_) | copy-start | bytes 393220
  50.5 10.7 %collective-permute-start.8 = (bf16[3072,256]{1,0:T(8,128)(2,1)S(1)}, bf16[3072,256]{1,0:T(8,128)(2,1)S(1)}, u32[]{:S(2)}, u32[]{:S(2)}) collective-permute-start(bf16[3072,256]{1,0:T(8,128)(2,1)S(1)} %slice.3), channel_id=1, source_target_pairs={{0,32},{32,0},{1,33},{33,1},{2,34},{34,2},{3,35},{35,3},{4,36},{36... | collective-permute-start | bytes 4718600 | tf_op jit(solution)/shard_map/ppermute | solution.py:377
  52.2 23.5 %collective-permute-start.10 = (bf16[256,1280]{1,0:T(8,128)(2,1)}, bf16[256,1280]{1,0:T(8,128)(2,1)}, u32[]{:S(2)}, u32[]{:S(2)}) collective-permute-start(bf16[256,1280]{1,0:T(8,128)(2,1)} %collective-permute-done.6.refs_4_), channel_id=1, source_target_pairs={{0,4},{32,48},{2,6},{34,50},{4,0},{36,52},{6,2},{38,54},{8,12},{40... | collective-permute-start | bytes 1966088 | tf_op jit(solution)/shard_map/ppermute | solution.py:396
  54.7 20.9 %collective-permute-start.11 = (bf16[256,1280]{1,0:T(8,128)(2,1)}, bf16[256,1280]{1,0:T(8,128)(2,1)}, u32[]{:S(2)}, u32[]{:S(2)}) collective-permute-start(bf16[256,1280]{1,0:T(8,128)(2,1)} %collective-permute-done.6.refs_4_), channel_id=1, source_target_pairs={{0,2},{32,40},{2,4},{34,42},{4,6},{36,44},{6,0},{38,46},{8,10},{40... | collective-permute-start | bytes 1966088 | tf_op jit(solution)/shard_map/ppermute | solution.py:396
  54.7 20.9 %collective-permute-start.9 = (bf16[256,1280]{1,0:T(8,128)(2,1)}, bf16[256,1280]{1,0:T(8,128)(2,1)}, u32[]{:S(2)}, u32[]{:S(2)}) collective-permute-start(bf16[256,1280]{1,0:T(8,128)(2,1)} %collective-permute-done.6.refs_4_), channel_id=1, source_target_pairs={{0,6},{32,56},{2,0},{34,58},{4,2},{36,60},{6,4},{38,62},{8,14},{40... | collective-permute-start | bytes 1966088 | tf_op jit(solution)/shard_map/ppermute | solution.py:396
  57.4 18.2 %collective-permute-start.12 = (bf16[1024,256]{1,0:T(8,128)(2,1)S(1)}, bf16[1024,256]{1,0:T(8,128)(2,1)}, u32[]{:S(2)}, u32[]{:S(2)}) collective-permute-start(bf16[1024,256]{1,0:T(8,128)(2,1)S(1)} %copy-done.6), channel_id=1, source_target_pairs={{0,65},{1,64},{64,1},{65,0},{2,67},{3,66},{66,3},{67,2},{4,69},{5,... | collective-permute-start | bytes 1572872 | tf_op jit(solution)/shard_map/ppermute | solution.py:407
  75.7 6.4 %copy-start.10 = (bf16[256,256]{1,0:T(8,128)(2,1)S(1)}, bf16[256,256]{1,0:T(8,128)(2,1)}, u32[]{:S(2)}) copy-start(bf16[256,256]{1,0:T(8,128)(2,1)} %copy-done.9) | copy-start | bytes 393220
  75.7 5.8 %copy-start.8 = (bf16[256,256]{1,0:T(8,128)(2,1)S(1)}, bf16[256,256]{1,0:T(8,128)(2,1)}, u32[]{:S(2)}) copy-start(bf16[256,256]{1,0:T(8,128)(2,1)} %copy-done.7) | copy-start | bytes 393220
  75.7 9.6 %collective-permute-start.22 = (bf16[1024,256]{1,0:T(8,128)(2,1)}, bf16[1024,256]{1,0:T(8,128)(2,1)S(1)}, u32[]{:S(2)}, u32[]{:S(2)}) collective-permute-start(bf16[1024,256]{1,0:T(8,128)(2,1)} %collective-permute-done.7.refs_8_), channel_id=1, source_target_pairs={{0,32},{32,0},{1,33},{33,1},{2,34},{34,2},{3,35},{35,3},{4,36},{36... | collective-permute-start | bytes 1572872 | tf_op jit(solution)/shard_map/ppermute | solution.py:377
  75.8 20.6 %all-to-all-start.1 = ((bf16[32,3,32,128]{3,2,1,0:T(8,128)(2,1)}), bf16[32,3,32,128]{3,2,1,0:T(8,128)(2,1)S(1)}, u32[]{:S(2)}, u32[]{:S(2)}) async-start(bf16[32,3,32,128]{3,2,1,0:T(8,128)(2,1)} %bitcast.5), calls=%async_computation.1 | async-start | bytes 1572864 | tf_op jit(solution)/shard_map/all_to_all | solution.py:442
  81.5 1.4 %collective-permute-start.14 = (bf16[256,256]{1,0:T(8,128)(2,1)S(1)}, bf16[256,256]{1,0:T(8,128)(2,1)S(1)}, u32[]{:S(2)}, u32[]{:S(2)}) collective-permute-start(bf16[256,256]{1,0:T(8,128)(2,1)S(1)} %copy-done.8), channel_id=1, source_target_pairs={{0,32},{32,0},{1,33},{33,1},{2,34},{34,2},{3,35},{35,3},{4,36},{36... | collective-permute-start | bytes 393224 | tf_op jit(solution)/shard_map/ppermute | solution.py:377
  81.9 14.5 %collective-permute-start.23 = (bf16[1024,256]{1,0:T(8,128)(2,1)}, bf16[1024,256]{1,0:T(8,128)(2,1)}, u32[]{:S(2)}, u32[]{:S(2)}) collective-permute-start(bf16[1024,256]{1,0:T(8,128)(2,1)} %collective-permute-done.12.refs_9_), channel_id=1, source_target_pairs={{0,32},{32,0},{1,33},{33,1},{2,34},{34,2},{3,35},{35,3},{4,36},{36... | collective-permute-start | bytes 1572872 | tf_op jit(solution)/shard_map/ppermute | solution.py:377
  82.1 2.1 %collective-permute-start.15 = (bf16[256,256]{1,0:T(8,128)(2,1)S(1)}, bf16[256,256]{1,0:T(8,128)(2,1)S(1)}, u32[]{:S(2)}, u32[]{:S(2)}) collective-permute-start(bf16[256,256]{1,0:T(8,128)(2,1)S(1)} %copy-done.10), channel_id=1, source_target_pairs={{0,32},{32,0},{1,33},{33,1},{2,34},{34,2},{3,35},{35,3},{4,36},{36... | collective-permute-start | bytes 393224 | tf_op jit(solution)/shard_map/ppermute | solution.py:377
  82.4 2.4 %collective-permute-start.16 = (bf16[256,256]{1,0:T(8,128)(2,1)}, bf16[256,256]{1,0:T(8,128)(2,1)}, u32[]{:S(2)}, u32[]{:S(2)}) collective-permute-start(bf16[256,256]{1,0:T(8,128)(2,1)} %collective-permute-done.4.refs_2_), channel_id=1, source_target_pairs={{0,32},{32,0},{1,33},{33,1},{2,34},{34,2},{3,35},{35,3},{4,36},{36... | collective-permute-start | bytes 393224 | tf_op jit(solution)/shard_map/ppermute | solution.py:377
  82.9 1.5 %copy-start.11 = (bf16[256,256]{1,0:T(8,128)(2,1)}, bf16[256,256]{1,0:T(8,128)(2,1)S(1)}, u32[]{:S(2)}) copy-start(bf16[256,256]{1,0:T(8,128)(2,1)S(1)} %collective-permute-done.14.refs_10_) | copy-start | bytes 393220
  82.9 2.1 %collective-permute-start.17 = (bf16[256,256]{1,0:T(8,128)(2,1)}, bf16[256,256]{1,0:T(8,128)(2,1)S(1)}, u32[]{:S(2)}, u32[]{:S(2)}) collective-permute-start(bf16[256,256]{1,0:T(8,128)(2,1)} %collective-permute-done.5.refs_3_), channel_id=1, source_target_pairs={{0,32},{32,0},{1,33},{33,1},{2,34},{34,2},{3,35},{35,3},{4,36},{36... | collective-permute-start | bytes 393224 | tf_op jit(solution)/shard_map/ppermute | solution.py:377
  84.2 0.7 copy-start.12
  84.2 14.4 %collective-permute-start.18 = (bf16[256,1280]{1,0:T(8,128)(2,1)}, bf16[256,1280]{1,0:T(8,128)(2,1)S(1)}, u32[]{:S(2)}, u32[]{:S(2)}) collective-permute-start(bf16[256,1280]{1,0:T(8,128)(2,1)} %collective-permute-done.6.refs_4_), channel_id=1, source_target_pairs={{0,32},{32,0},{1,33},{33,1},{2,34},{34,2},{3,35},{35,3},{4,36},{36... | collective-permute-start | bytes 1966088 | tf_op jit(solution)/shard_map/ppermute | solution.py:377
  84.8 13.7 %collective-permute-start.19 = (bf16[256,1280]{1,0:T(8,128)(2,1)}, bf16[256,1280]{1,0:T(8,128)(2,1)S(1)}, u32[]{:S(2)}, u32[]{:S(2)}) collective-permute-start(bf16[256,1280]{1,0:T(8,128)(2,1)} %collective-permute-done.9.refs_5_), channel_id=1, source_target_pairs={{0,32},{32,0},{1,33},{33,1},{2,34},{34,2},{3,35},{35,3},{4,36},{36... | collective-permute-start | bytes 1966088 | tf_op jit(solution)/shard_map/ppermute | solution.py:377
  85.0 11.3 %copy-start.13 = (bf16[256,256]{1,0:T(8,128)(2,1)}, bf16[256,256]{1,0:T(8,128)(2,1)S(1)}, u32[]{:S(2)}) copy-start(bf16[256,256]{1,0:T(8,128)(2,1)S(1)} %collective-permute-done.17.refs_13_) | copy-start | bytes 393220
  85.0 13.5 %collective-permute-start.20 = (bf16[256,1280]{1,0:T(8,128)(2,1)}, bf16[256,1280]{1,0:T(8,128)(2,1)}, u32[]{:S(2)}, u32[]{:S(2)}) collective-permute-start(bf16[256,1280]{1,0:T(8,128)(2,1)} %collective-permute-done.10.refs_6_), channel_id=1, source_target_pairs={{0,32},{32,0},{1,33},{33,1},{2,34},{34,2},{3,35},{35,3},{4,36},{36... | collective-permute-start | bytes 1966088 | tf_op jit(solution)/shard_map/ppermute | solution.py:377
  85.3 14.4 %copy-start.5 = (bf16[1024,256]{1,0:T(8,128)(2,1)}, bf16[1024,256]{1,0:T(8,128)(2,1)S(1)}, u32[]{:S(2)}) copy-start(bf16[1024,256]{1,0:T(8,128)(2,1)S(1)} %collective-permute-done.22.refs_18_) | copy-start | bytes 1572868
  85.3 13.2 %collective-permute-start.21 = (bf16[256,1280]{1,0:T(8,128)(2,1)}, bf16[256,1280]{1,0:T(8,128)(2,1)}, u32[]{:S(2)}, u32[]{:S(2)}) collective-permute-start(bf16[256,1280]{1,0:T(8,128)(2,1)} %collective-permute-done.11.refs_7_), channel_id=1, source_target_pairs={{0,32},{32,0},{1,33},{33,1},{2,34},{34,2},{3,35},{35,3},{4,36},{36... | collective-permute-start | bytes 1966088 | tf_op jit(solution)/shard_map/ppermute | solution.py:377
  96.4 3.3 %collective-permute-start.13 = (bf16[2,8,3,32,128]{4,3,2,1,0:T(8,128)(2,1)S(1)}, bf16[2,8,3,32,128]{4,3,2,1,0:T(8,128)(2,1)S(1)}, u32[]{:S(2)}, u32[]{:S(2)}) collective-permute-start(bf16[2,8,3,32,128]{4,3,2,1,0:T(8,128)(2,1)S(1)} %pick.1), channel_id=1, source_target_pairs={{0,32},{32,0},{1,33},{33,1},{2,34},{34,2},{3,35},{35,3},{4,36},{36... | collective-permute-start | bytes 1179656 | tf_op jit(solution)/shard_map/ppermute | solution.py:377
  98.5 1.2 %copy-start.3 = (bf16[256,1280]{1,0:T(8,128)(2,1)}, bf16[256,1280]{1,0:T(8,128)(2,1)S(1)}, u32[]{:S(2)}) copy-start(bf16[256,1280]{1,0:T(8,128)(2,1)S(1)} %collective-permute-done.18.refs_14_) | copy-start | bytes 1966084
  98.5 1.2 %copy-start.4 = (bf16[256,1280]{1,0:T(8,128)(2,1)}, bf16[256,1280]{1,0:T(8,128)(2,1)S(1)}, u32[]{:S(2)}) copy-start(bf16[256,1280]{1,0:T(8,128)(2,1)S(1)} %collective-permute-done.19.refs_15_) | copy-start | bytes 1966084
